TPU v7x, 512 devices: a whole 4x4x16 slice. The times are simulated.
512 devices in a mesh: dp: 32 (over y, x, core), tensor: 16 (over z).
Axes of the slice: x: 4, y: 4, z: 16, core: 2. Of those that a mesh axis runs over, the one named last changes fastest.
Arguments:
- gradient: bfloat16 [32, 512, 8192], P('dp', 'tensor'), may hold values from -50 to 50
- feedback: float32 [32, 512, 8192], P('dp', 'tensor'), may hold values from -4 to 4
- momentum: float32 [512, 8192], P('tensor'), may hold values from -6 to 6
- q_previous: float32 [64, 8192], P(None, 'tensor'), may hold values from -6 to 6
Outputs:
- new_feedback: float32 [32, 512, 8192], P('dp', 'tensor')
- new_momentum: float32 [512, 8192], P('tensor')
- q_factor: float32 [64, 8192], P(None, 'tensor')
All inputs are finite; a program needn't handle non-finite values.
Results may differ from a plain program's by a relative error of at most 0.0003.
Values sent between devices are 32-bit elements; how exact they have to be, the bound alone decides.
No kernel may reach another device: no remote copies, remote signals or barrier semaphores. Data moves between devices by JAX's collectives and lax.ppermute only.
A program may use at most 64 MiB of HBM per device.

v0:
```python
import jax
import jax.numpy as jnp
from jax import lax
from jax.sharding import PartitionSpec as P

BLOCK = 16


BETA = 0.9
HIGH = lax.Precision.HIGHEST


def inner_rows(left, right):
    return lax.dot_general(
        left, right, (((0,), (0,)), ((), ())), precision=HIGH, preferred_element_type=jnp.float32
    )


def orthonormal(matrix, gram_matrix):
    triangle = jnp.linalg.cholesky(gram_matrix)
    return jax.scipy.linalg.solve_triangular(triangle, matrix.T, lower=True).T


def on_device(gradient, feedback, momentum, q_previous):
    merged = gradient[0].astype(jnp.float32) + feedback[0]
    rank_count = q_previous.shape[0]
    local_factor = lax.dot_general(
        merged,
        lax.all_gather(q_previous, "tensor", axis=1, tiled=True),
        (((1,), (1,)), ((), ())),
        precision=HIGH,
        preferred_element_type=jnp.float32,
    )
    factor = lax.psum(local_factor, "dp")
    finished = []
    for position in range(rank_count // BLOCK):
        column_block = factor[:, position * BLOCK : (position + 1) * BLOCK]
        if position > 0:
            previous = jnp.concatenate(finished, axis=1)
            projection = lax.psum(inner_rows(previous, column_block), "tensor")
            column_block = column_block - jnp.dot(previous, projection, precision=HIGH)
        block_matrix = lax.psum(inner_rows(column_block, column_block), "tensor")
        finished.append(orthonormal(column_block, block_matrix))
    ortho_basis = jnp.concatenate(finished, axis=1)
    q_term = inner_rows(ortho_basis, merged)
    replica_count = lax.axis_size("dp")
    q_shard = lax.psum_scatter(q_term, "tensor", scatter_dimension=1, tiled=True)
    q_shard = lax.psum(q_shard, "dp") / replica_count
    approx = jnp.dot(
        ortho_basis, lax.all_gather(q_shard, "tensor", axis=1, tiled=True), precision=HIGH
    )
    new_feedback = (merged - approx)[None]
    new_momentum = BETA * momentum + approx
    return (new_feedback, new_momentum, q_shard)


def solution(mesh):
    placed = (
        P("dp", "tensor", None),
        P("dp", "tensor", None),
        P("tensor", None),
        P(None, "tensor"),
    )
    return jax.shard_map(
        on_device,
        mesh=mesh,
        in_specs=placed,
        out_specs=(P("dp", "tensor", None), P("tensor", None), P(None, "tensor")),
        check_vma=False,
    )
```

profile of v0, /device:TPU:1, one launch (start us, length us, event | category | flops | bytes accessed | tf_op | source)
XLA Modules:
  0.0 762.7 jit_solution(13664649303600476803)
XLA Ops:
  7.2 0.7 all-gather.3.cloned.1.call-update
  8.0 71.5 %all-gather.3.cloned.1.call-done = f32[64,8192]{1,0:T(8,128)} async-done(((f32[64,512]{1,0:T(8,128)}), f32[64,8192]{1,0:T(8,128)}) %all-gather.3.cloned.1.call-update) | async-done | bytes 2097168 | tf_op jit(solution)/shard_map/all_gather | solution.py:29
  79.5 3.8 fusion.2
  83.3 127.8 %psum.63 = f32[32,64]{1,0:T(8,128)S(1)} all-reduce(f32[32,64]{1,0:T(8,128)S(1)} %fusion.2), channel_id=1, replica_groups=mesh['dp'=32,'tensor'=16] {'dp'}, use_global_device_ids=true, to_apply=%region_0.0 | all-reduce | flops 2048 | bytes 16384 | tf_op jit(solution)/shard_map/psum | solution.py:34
  211.3 23.0 %psum.64 = f32[16,16]{0,1:T(8,128)S(1)} all-reduce(f32[16,16]{0,1:T(8,128)S(1)} %fusion.18), channel_id=1, replica_groups=mesh['dp'=32,'tensor'=16] {'tensor'}, use_global_device_ids=true, to_apply=%region_1.0 | all-reduce | flops 256 | bytes 2048 | tf_op jit(solution)/shard_map/psum | solution.py:42
  234.5 1.5 cholesky.74
  236.6 0.6 fusion.20
  237.3 1.2 custom-call.8
  238.9 20.6 %psum.65 = f32[16,16]{1,0:T(8,128)S(1)} all-reduce(f32[16,16]{1,0:T(8,128)S(1)} %fusion.15), channel_id=1, replica_groups=mesh['dp'=32,'tensor'=16] {'tensor'}, use_global_device_ids=true, to_apply=%region_4.0 | all-reduce | flops 256 | bytes 2048 | tf_op jit(solution)/shard_map/psum | solution.py:40
  259.9 22.4 %psum.66 = f32[16,16]{0,1:T(8,128)S(1)} all-reduce(f32[16,16]{0,1:T(8,128)S(1)} %fusion.38), channel_id=1, replica_groups=mesh['dp'=32,'tensor'=16] {'tensor'}, use_global_device_ids=true, to_apply=%region_5.0 | all-reduce | flops 256 | bytes 2048 | tf_op jit(solution)/shard_map/psum | solution.py:42
  282.3 1.5 cholesky.85
  283.8 0.6 compare_reduce_fusion.2
  284.5 0.6 fusion.21
  285.1 1.2 custom-call.9
  286.8 39.1 %psum.67 = f32[32,16]{1,0:T(8,128)S(1)} all-reduce(f32[32,16]{1,0:T(8,128)S(1)} %fusion.13), channel_id=1, replica_groups=mesh['dp'=32,'tensor'=16] {'tensor'}, use_global_device_ids=true, to_apply=%region_6.0 | all-reduce | flops 512 | bytes 4096 | tf_op jit(solution)/shard_map/psum | solution.py:40
  326.3 20.8 %psum.68 = f32[16,16]{0,1:T(8,128)S(1)} all-reduce(f32[16,16]{0,1:T(8,128)S(1)} %fusion.39), channel_id=1, replica_groups=mesh['dp'=32,'tensor'=16] {'tensor'}, use_global_device_ids=true, to_apply=%region_7.0 | all-reduce | flops 256 | bytes 2048 | tf_op jit(solution)/shard_map/psum | solution.py:42
  347.2 1.5 cholesky.96
  348.7 0.6 compare_reduce_fusion.1
  349.4 0.6 fusion.22
  350.0 1.2 custom-call.10
  351.7 40.4 %psum.69 = f32[48,16]{1,0:T(8,128)S(1)} all-reduce(f32[48,16]{1,0:T(8,128)S(1)} %fusion.6), channel_id=1, replica_groups=mesh['dp'=32,'tensor'=16] {'tensor'}, use_global_device_ids=true, to_apply=%region_8.0 | all-reduce | flops 768 | bytes 6144 | tf_op jit(solution)/shard_map/psum | solution.py:40
  392.5 20.8 %psum.70 = f32[16,16]{0,1:T(8,128)S(1)} all-reduce(f32[16,16]{0,1:T(8,128)S(1)} %fusion.40), channel_id=1, replica_groups=mesh['dp'=32,'tensor'=16] {'tensor'}, use_global_device_ids=true, to_apply=%region_9.0 | all-reduce | flops 256 | bytes 2048 | tf_op jit(solution)/shard_map/psum | solution.py:42
  413.4 1.5 cholesky.107
  414.9 0.6 compare_reduce_fusion
  415.5 0.6 fusion.23
  416.2 1.2 custom-call.11
  417.6 3.1 fusion
  420.9 122.3 %reduce-scatter.2.cloned.1.call-done = f32[64,512]{1,0:T(8,128)} async-done(((f32[64,8192]{1,0:T(8,128)}), f32[64,512]{1,0:T(8,128)}) %reduce-scatter.2.cloned.1.call-update) | async-done | bytes 131088 | tf_op jit(solution)/shard_map/reduce_scatter | solution.py:47
  543.3 142.0 %all-reduce.2.cloned.1.call-done = f32[64,512]{1,0:T(8,128)} async-done(((f32[64,512]{1,0:T(8,128)}), f32[64,512]{1,0:T(8,128)}) %all-reduce.2.cloned.1.call-update) | async-done | bytes 131088 | tf_op jit(solution)/shard_map/psum | solution.py:48
  685.2 1.6 broadcast_multiply_fusion
  686.8 65.1 %all-gather.5.cloned.1.call-done = f32[64,8192]{1,0:T(8,128)} async-done(((f32[64,512]{1,0:T(8,128)}), f32[64,8192]{1,0:T(8,128)}) %all-gather.5.cloned.1.call-update) | async-done | bytes 2097168 | tf_op jit(solution)/shard_map/all_gather | solution.py:50
  751.9 4.2 multiply_add_fusion
  (40 shorter events, 4.2 us)
Async XLA Ops:
  7.2 72.3 %all-gather.3.cloned.1.call-start = ((), (), s32[]{:S(2)}) async-start(), calls=%async_computation.1 | async-start | bytes 2228224 | tf_op jit(solution)/shard_map/all_gather | solution.py:29
  7.9 409.7 %copy-start = (f32[1,32,8192]{2,1,0:T(8,128)S(1)}, f32[1,32,8192]{2,1,0:T(8,128)}, u32[]{:S(2)}) copy-start(f32[1,32,8192]{2,1,0:T(8,128)} %param.8) | copy-start | bytes 3145732
  7.9 409.7 %copy-start.1 = (bf16[1,32,8192]{2,1,0:T(8,128)(2,1)S(1)}, bf16[1,32,8192]{2,1,0:T(8,128)(2,1)}, u32[]{:S(2)}) copy-start(bf16[1,32,8192]{2,1,0:T(8,128)(2,1)} %param.7) | copy-start | bytes 1572868
  7.9 535.3 %reduce-scatter.2.cloned.1.call-start = ((), (), s32[]{:S(2)}) async-start(), calls=%async_computation.2 | async-start | bytes 2228224 | tf_op jit(solution)/shard_map/reduce_scatter | solution.py:47
  420.8 331.1 %copy-start.2 = (f32[32,8192]{1,0:T(8,128)S(1)}, f32[32,8192]{1,0:T(8,128)}, u32[]{:S(2)}) copy-start(f32[32,8192]{1,0:T(8,128)} %param.9) | copy-start | bytes 3145732
  420.8 264.4 %all-reduce.2.cloned.1.call-start = ((), (), s32[]{:S(2)}) async-start(), calls=%async_computation.3 | async-start | bytes 262144 | tf_op jit(solution)/shard_map/psum | solution.py:48
  543.2 208.7 %all-gather.5.cloned.1.call-start = ((), (), s32[]{:S(2)}) async-start(), calls=%async_computation.4 | async-start | bytes 2228224 | tf_op jit(solution)/shard_map/all_gather | solution.py:50
Sparse Core Ops, SparseCore 0:
  10.1 69.3 all-gather.2
  420.9 122.2 reduce-scatter.1
  546.4 138.7 all-reduce.1
  687.9 63.8 all-gather.4
where the time goes:
time: 771 us; the launch traced here: 763 us
  waiting for transfers between devices  402 us (52%)
  blocking collectives  315 us (41%)
  other arithmetic  17.6 us (2%)
  matrix products  14.1 us (2%)
  between operations  13.9 us (2%)
    psum x1, waiting for transfers between devices, on_device(): q_shard = lax.psum(q_shard, 'dp') / replica_count  142 us
    psum x1, blocking collectives, on_device(): factor = lax.psum(local_factor, 'dp')  128 us
    reduce_scatter x1, waiting for transfers between devices, on_device(): lax.psum_scatter(q_term, 'tensor', scatter_dimension=1, tiled=True)  122 us
    psum x3, blocking collectives, on_device(): projection = lax.psum(inner_rows(previous, column_block), 'tensor')  100 us
    psum x4, blocking collectives, on_device(): block_matrix = lax.psum(inner_rows(column_block, column_block), 'tensor')  87 us
    all_gather x1, waiting for transfers between devices, on_device(): lax.all_gather(q_previous, 'tensor', axis=1, tiled=True)  71.5 us
    all_gather x1, waiting for transfers between devices, on_device(): lax.all_gather(q_shard, 'tensor', axis=1, tiled=True)  65.1 us
  transfers between devices with their start and end apart: 4, of which 4 were waited for; matrix products, arithmetic and copies ran while one was open for 0% of the time, Pallas kernels for 0%

commit v1 on v0

v1 whole, which is shorter than its diff:
```python
import jax
import jax.numpy as jnp
from jax import lax
from jax.experimental import pallas as pl
from jax.experimental.pallas import tpu as pltpu
from jax.sharding import PartitionSpec as P

BETA = 0.9
HIGH = lax.Precision.HIGHEST

DP = 32
TP = 16
ROWS = 32
RANK = 64
LANES = 128
BLOCK = 16
GROUP = LANES // BLOCK
SHARD = DP * BLOCK


def dot(left, right, left_dim, right_dim):
    return lax.dot_general(
        left,
        right,
        (((left_dim,), (right_dim,)), ((), ())),
        precision=HIGH,
        preferred_element_type=jnp.float32,
    )


def swap_blocks(parts):
    parts = list(parts)
    block = lax.broadcasted_iota(jnp.int32, parts[0].shape, 1) // BLOCK
    for step in (1, 2, 4):
        upper = (block & step) != 0
        for i in range(GROUP):
            if i & step:
                continue
            a, b = parts[i], parts[i | step]
            parts[i] = jnp.where(upper, pltpu.roll(b, step * BLOCK, 1), a)
            parts[i | step] = jnp.where(upper, b, pltpu.roll(a, LANES - step * BLOCK, 1))
    return parts


def gather_blocks(matrix, lane_block):
    block = lax.broadcasted_iota(jnp.int32, (8, LANES), 1) // BLOCK
    moved = pltpu.roll(matrix, (GROUP - lane_block) % GROUP * BLOCK, 1)
    out = jnp.zeros((8, LANES), jnp.float32)
    for kh in range(GROUP):
        piece = moved[kh * 8 : (kh + 1) * 8, :]
        if kh:
            piece = pltpu.roll(piece, kh * BLOCK, 1)
        out = jnp.where(block == kh, piece, out)
    return out


def merge_kernel(gradient, feedback, out):
    for c in range(SHARD // LANES):
        for th in range(TP // GROUP):
            parts = []
            for tl in range(GROUP):
                lanes = pl.ds((th * GROUP + tl) * SHARD + c * LANES, LANES)
                parts.append(gradient[0, :, lanes].astype(jnp.float32) + feedback[0, :, lanes])
            for e, part in enumerate(swap_blocks(parts)):
                out[c * GROUP + e, th * ROWS : (th + 1) * ROWS, :] = part


def pack_q_kernel(d_ref, q_ref, out):
    d = d_ref[0]
    tile = q_ref[:, pl.ds(pl.multiple_of(d // GROUP * LANES, LANES), LANES)]
    packed = gather_blocks(tile, d % GROUP)
    for t in range(TP):
        out[t] = packed


def factor_kernel(merged, q_parts, factor_out, sum_out):
    total = merged[0]
    for r in range(1, DP):
        total = total + merged[r]
    factor = jnp.zeros((ROWS, LANES), jnp.float32)
    for th in range(TP // GROUP):
        q_rows = swap_blocks([q_parts[th * GROUP + tl] for tl in range(GROUP)])
        q_twice = jnp.concatenate(q_rows + q_rows, axis=0)
        factor = factor + dot(total[th * ROWS : (th + 1) * ROWS], q_twice, 1, 1)
    lane = lax.broadcasted_iota(jnp.int32, (ROWS // 2, LANES), 1)
    packed = jnp.where(lane < RANK, factor[: ROWS // 2], factor[ROWS // 2 :])
    for d in range(DP):
        factor_out[d] = packed
    for t in range(TP):
        sum_out[t] = total


def sum_kernel(factors, out):
    total = factors[0]
    for d in range(1, DP):
        total = total + factors[d]
    for t in range(TP):
        out[t] = total


def inverse_triangle(gram, rows_ref):
    row = lax.broadcasted_iota(jnp.int32, (RANK, LANES), 0)
    lane = lax.broadcasted_iota(jnp.int32, (RANK, LANES), 1)
    identity = jnp.where(lane == row + RANK, 1.0, 0.0)
    work = jnp.concatenate([gram, jnp.zeros_like(gram)], axis=1) + identity
    for k in range(RANK):
        pivot_row = work[k : k + 1, :]
        pivot = work[k : k + 1, k : k + 1]
        rows_ref[k : k + 1, :] = pivot_row * lax.rsqrt(pivot)
        if k + 1 < RANK:
            scaled = pivot_row * (1.0 / pivot)
            column = work[:, k : k + 1]
            work = work - jnp.where(row > k, column, 0.0) * scaled
    return rows_ref[:, RANK:]


def solve_kernel(t_ref, factors, sums, out, rows_ref):
    half = ROWS // 2
    flat = factors[...].reshape(TP * half, LANES)
    whole = jnp.concatenate([flat[:, :RANK], flat[:, RANK:]], axis=0)
    gram = dot(whole, whole, 0, 0)
    inverse = inverse_triangle(gram, rows_ref)
    own = factors[t_ref[0]]
    own = jnp.concatenate([own[:, :RANK], own[:, RANK:]], axis=0)
    basis = dot(own, inverse, 1, 1)
    t = t_ref[0]
    approx, q_tiles = [], []
    for th in range(TP // GROUP):
        columns = jnp.concatenate(
            [
                sums[:, th * ROWS + h * half : th * ROWS + (h + 1) * half, :].reshape(TP * half, LANES)
                for h in range(2)
            ],
            axis=0,
        )
        q_tile = dot(inverse, dot(whole, columns, 0, 0), 1, 0) * (1.0 / DP)
        q_tiles.append(q_tile)
        approx.append(dot(basis, q_tile, 1, 0))
    mine = jnp.where(t // GROUP == 0, q_tiles[0], q_tiles[1])
    message = jnp.concatenate(approx + [gather_blocks(mine, t % GROUP)], axis=0)
    for d in range(DP):
        out[d] = message


def finish_kernel(gradient, feedback, momentum, parts_ref, new_feedback, new_momentum, q_out):
    for c in range(SHARD // LANES):
        for th in range(TP // GROUP):
            rows = slice(th * ROWS, (th + 1) * ROWS)
            parts = swap_blocks([parts_ref[c * GROUP + e, rows, :] for e in range(GROUP)])
            for tl, part in enumerate(parts):
                lanes = pl.ds((th * GROUP + tl) * SHARD + c * LANES, LANES)
                merged = gradient[0, :, lanes].astype(jnp.float32) + feedback[0, :, lanes]
                new_feedback[0, :, lanes] = merged - part
                new_momentum[:, lanes] = BETA * momentum[:, lanes] + part
        tail = swap_blocks([parts_ref[c * GROUP + e, 2 * ROWS :, :] for e in range(GROUP)])
        q_out[:, c * LANES : (c + 1) * LANES] = jnp.concatenate(tail, axis=0)


def local(kernel, *shapes, scalars=0, inputs=1, scratch=()):
    return pl.pallas_call(
        kernel,
        out_shape=[jax.ShapeDtypeStruct(shape, jnp.float32) for shape in shapes],
        in_specs=[pl.BlockSpec(memory_space=pltpu.SMEM)] * scalars
        + [pl.BlockSpec(memory_space=pltpu.VMEM)] * inputs,
        out_specs=[pl.BlockSpec(memory_space=pltpu.VMEM)] * len(shapes),
        scratch_shapes=list(scratch),
        compiler_params=pltpu.CompilerParams(vmem_limit_bytes=32 * 1024 * 1024),
    )


def exchange(parts, axis):
    return lax.all_to_all(parts, axis, 0, 0, tiled=True)


def on_device(gradient, feedback, momentum, q_previous):
    d = lax.axis_index("dp").reshape(1)
    t = lax.axis_index("tensor").reshape(1)
    half = ROWS // 2
    (merged,) = local(merge_kernel, (DP, 2 * ROWS, LANES), inputs=2)(gradient, feedback)
    (q_parts,) = local(pack_q_kernel, (TP, 8, LANES), scalars=1)(d, q_previous)
    merged = exchange(merged, "dp")
    q_parts = exchange(q_parts, "tensor")
    factor, summed = local(
        factor_kernel, (DP, half, LANES), (TP, 2 * ROWS, LANES), inputs=2
    )(merged, q_parts)
    factor = exchange(factor, "dp")
    summed = exchange(summed, "tensor")
    (factor,) = local(sum_kernel, (TP, half, LANES))(factor)
    factor = exchange(factor, "tensor")
    (parts,) = local(
        solve_kernel,
        (DP, 2 * ROWS + 8, LANES),
        scalars=1,
        inputs=2,
        scratch=[pltpu.VMEM((RANK, LANES), jnp.float32)],
    )(t, factor, summed)
    parts = exchange(parts, "dp")
    return tuple(
        local(finish_kernel, feedback.shape, momentum.shape, q_previous.shape, inputs=4)(
            gradient, feedback, momentum, parts
        )
    )


def solution(mesh):
    placed = (
        P("dp", "tensor", None),
        P("dp", "tensor", None),
        P("tensor", None),
        P(None, "tensor"),
    )
    return jax.shard_map(
        on_device,
        mesh=mesh,
        in_specs=placed,
        out_specs=(P("dp", "tensor", None), P("tensor", None), P(None, "tensor")),
        check_vma=False,
    )
```

time: 771 us -> 154 us (0.20)
  waiting for transfers between devices: 402 us -> 30.5 us
  blocking collectives: 315 us -> 82.9 us
  starting transfers between devices: 0.16 us -> 22.2 us
  other arithmetic: 17.6 us -> 0 us
  matrix products: 14.1 us -> 0 us
  Pallas kernels: 0 us -> 13.7 us
  between operations: 13.9 us -> 0.72 us
    psum x8 -> x0, blocking collectives: 315 us -> none  [the longest x1 128 us: on_device(): factor = lax.psum(local_factor, 'dp')]
    psum x1 -> x0, waiting for transfers between devices: 142 us -> none  [on_device(): q_shard = lax.psum(q_shard, 'dp') / replica_count]
    all_gather x2 -> x0, waiting for transfers between devices: 137 us -> none  [the longest x1 71.5 us: on_device(): lax.all_gather(q_previous, 'tensor', axis=1, tiled=True)]
    reduce_scatter x1 -> x0, waiting for transfers between devices: 122 us -> none  [on_device(): lax.psum_scatter(q_term, 'tensor', scatter_dimension=1, tiled=True)]
    all_to_all x0 -> x4, blocking collectives: none -> 82.9 us  [exchange(): return lax.all_to_all(parts, axis, 0, 0, tiled=True)]
    all_to_all x0 -> x2, waiting for transfers between devices: none -> 30.5 us  [exchange(): return lax.all_to_all(parts, axis, 0, 0, tiled=True)]
    all_to_all x0 -> x2, starting transfers between devices: none -> 22.2 us  [exchange(): return lax.all_to_all(parts, axis, 0, 0, tiled=True)]
    another operation x20 -> x0, other arithmetic: 16 us -> none  [the longest x12 8.52 us: orthonormal(): triangle = jnp.linalg.cholesky(gram_matrix)]
  transfers between devices with their start and end apart: 4 -> 2, of which waited for: 4 -> 2; matrix products, arithmetic and copies ran while one was open for 0% -> 0% of each run, Pallas kernels for 0% -> 1%
where the time goes in v1:
time: 154 us; the launch traced here: 153 us
  blocking collectives  82.9 us (54%)
  waiting for transfers between devices  30.5 us (20%)
  starting transfers between devices  22.2 us (14%)
  Pallas kernels  13.7 us (9%)
  local copies, waits for them, and re-layouts  3.17 us (2%)
    all_to_all x4, blocking collectives, exchange(): return lax.all_to_all(parts, axis, 0, 0, tiled=True)  82.9 us
    all_to_all x2, waiting for transfers between devices, exchange(): return lax.all_to_all(parts, axis, 0, 0, tiled=True)  30.5 us
    all_to_all x2, starting transfers between devices, exchange(): return lax.all_to_all(parts, axis, 0, 0, tiled=True)  22.2 us
    pallas_call x1, Pallas kernels, on_device(): local(solve_kernel, (DP, 2 * ROWS + 8, LANES), scalars=1, inputs=2, scrat...  6.85 us
    pallas_call x1, Pallas kernels, on_device(): local(finish_kernel, feedback.shape, momentum.shape, q_previous.shape, in...  3.44 us
    unnamed x12, local copies, waits for them, and re-layouts  3.17 us
  transfers between devices with their start and end apart: 2, of which 2 were waited for; matrix products, arithmetic and copies ran while one was open for 0% of the time, Pallas kernels for 1%

profile of v1, /device:TPU:1, one launch (start us, length us, event | category | flops | bytes accessed | tf_op | source)
XLA Modules:
  0.0 153.2 jit_solution(6694525827991280694)
XLA Ops:
  0.6 0.0 copy-start.5
  0.6 0.9 copy-done.5
  1.5 0.8 shard_map.68
  2.3 15.7 %all-to-all-start.1 = ((f32[16,8,128]{2,1,0:T(8,128)}), f32[16,8,128]{2,1,0:T(8,128)S(1)}, u32[]{:S(2)}, u32[]{:S(2)}) async-start(f32[16,8,128]{2,1,0:T(8,128)} %shard_map.68), calls=%async_computation.1 | async-start | bytes 131072 | tf_op jit(solution)/shard_map/all_to_all | solution.py:172
  18.1 0.0 copy-start
  18.1 1.2 copy-done
  19.3 0.0 copy-start.2
  19.3 1.0 copy-done.2
  20.3 1.6 %shard_map.67 = f32[32,64,128]{2,1,0:T(8,128)S(1)} custom-call(bf16[1,32,8192]{2,1,0:T(8,128)(2,1)S(1)} %copy-done.2, f32[1,32,8192]{2,1,0:T(8,128)S(1)} %copy-done), custom_call_target="tpu_custom_call" | custom-call | tf_op jit(solution)/shard_map/pallas_call | solution.py:179
  21.9 7.7 %all-to-all-done.1.q_parts = f32[16,8,128]{2,1,0:T(8,128)S(1)} async-done(((f32[16,8,128]{2,1,0:T(8,128)}), f32[16,8,128]{2,1,0:T(8,128)S(1)}, u32[]{:S(2)}, u32[]{:S(2)}) %all-to-all-start.1) | async-done | bytes 65568 | tf_op jit(solution)/shard_map/all_to_all | solution.py:172
  29.6 26.2 %all_to_all.30.merged = f32[32,64,128]{2,1,0:T(8,128)S(1)} all-to-all(f32[32,64,128]{2,1,0:T(8,128)S(1)} %shard_map.67), channel_id=1, replica_groups=mesh['dp'=32,'tensor'=16] {'dp'}, dimensions={0} | all-to-all | bytes 2097152 | tf_op jit(solution)/shard_map/all_to_all | solution.py:172
  55.8 1.0 shard_map.69
  56.8 12.4 %all_to_all.31.factors = f32[32,16,128]{2,1,0:T(8,128)S(1)} all-to-all(f32[32,16,128]{2,1,0:T(8,128)S(1)} %get-tuple-element.5), channel_id=1, replica_groups=mesh['dp'=32,'tensor'=16] {'dp'}, dimensions={0} | all-to-all | bytes 524288 | tf_op jit(solution)/shard_map/all_to_all | solution.py:172
  69.3 14.9 %all_to_all.32.factors = f32[16,16,128]{2,1,0:T(8,128)S(1)} all-to-all(f32[16,16,128]{2,1,0:T(8,128)S(1)} %shard_map.70), channel_id=1, replica_groups=mesh['dp'=32,'tensor'=16] {'tensor'}, dimensions={0} | all-to-all | bytes 262144 | tf_op jit(solution)/shard_map/all_to_all | solution.py:172
  84.1 6.4 %all-to-all-start.4 = ((f32[16,64,128]{2,1,0:T(8,128)}), f32[16,64,128]{2,1,0:T(8,128)S(1)}, u32[]{:S(2)}, u32[]{:S(2)}) async-start(f32[16,64,128]{2,1,0:T(8,128)} %get-tuple-element.6), calls=%async_computation.4 | async-start | bytes 1048576 | tf_op jit(solution)/shard_map/all_to_all | solution.py:172
  90.6 22.8 %all-to-all-done.4.sums = f32[16,64,128]{2,1,0:T(8,128)S(1)} async-done(((f32[16,64,128]{2,1,0:T(8,128)}), f32[16,64,128]{2,1,0:T(8,128)S(1)}, u32[]{:S(2)}, u32[]{:S(2)}) %all-to-all-start.4) | async-done | bytes 524320 | tf_op jit(solution)/shard_map/all_to_all | solution.py:172
  113.4 0.0 copy-start.4
  113.4 6.8 %shard_map.71 = f32[32,72,128]{2,1,0:T(8,128)S(1)} custom-call(s32[1]{0:T(128)} %bitcast.t_ref, f32[16,16,128]{2,1,0:T(8,128)S(1)} %all_to_all.32.factors, f32[16,64,128]{2,1,0:T(8,128)S(1)} %all-to-all-done.4.sums), custom_call_target="tpu_custom_call" | custom-call | tf_op jit(solution)/shard_map/pallas_call | solution.py:190
  120.2 0.0 copy-start.1
  120.3 0.0 copy-start.3
  120.3 29.5 %all_to_all.33.parts_ref = f32[32,72,128]{2,1,0:T(8,128)S(1)} all-to-all(f32[32,72,128]{2,1,0:T(8,128)S(1)} %shard_map.71), channel_id=1, replica_groups=mesh['dp'=32,'tensor'=16] {'dp'}, dimensions={0} | all-to-all | bytes 2359296 | tf_op jit(solution)/shard_map/all_to_all | solution.py:172
  149.8 0.0 copy-done.4
  149.8 0.0 copy-done.1
  149.8 0.0 copy-done.3
  149.8 3.4 %shard_map.72 = (f32[1,32,8192]{2,1,0:T(8,128)}, f32[32,8192]{1,0:T(8,128)}, f32[64,512]{1,0:T(8,128)}) custom-call(bf16[1,32,8192]{2,1,0:T(8,128)(2,1)S(1)} %copy-done.3, f32[1,32,8192]{2,1,0:T(8,128)S(1)} %copy-done.1, f32[32,8192]{1,0:T(8,128)S(1)} %copy-done.4, f32[32,72,128]{2,1,0:T(8,128)S(1)} %all_to_all.33.parts_ref), custom_call_target="tpu_custom_call" | custom-call | tf_op jit(solution)/shard_map/pallas_call | solution.py:199
  (1 shorter events, 0.0 us)
Async XLA Ops:
  0.6 0.9 copy-start.5
  2.3 27.3 %all-to-all-start.1 = ((f32[16,8,128]{2,1,0:T(8,128)}), f32[16,8,128]{2,1,0:T(8,128)S(1)}, u32[]{:S(2)}, u32[]{:S(2)}) async-start(f32[16,8,128]{2,1,0:T(8,128)} %shard_map.68), calls=%async_computation.1 | async-start | bytes 131072 | tf_op jit(solution)/shard_map/all_to_all | solution.py:172
  18.1 1.2 copy-start
  19.3 1.0 copy-start.2
  84.1 29.2 %all-to-all-start.4 = ((f32[16,64,128]{2,1,0:T(8,128)}), f32[16,64,128]{2,1,0:T(8,128)S(1)}, u32[]{:S(2)}, u32[]{:S(2)}) async-start(f32[16,64,128]{2,1,0:T(8,128)} %get-tuple-element.6), calls=%async_computation.4 | async-start | bytes 1048576 | tf_op jit(solution)/shard_map/all_to_all | solution.py:172
  113.4 36.4 %copy-start.4 = (f32[32,8192]{1,0:T(8,128)S(1)}, f32[32,8192]{1,0:T(8,128)}, u32[]{:S(2)}) copy-start(f32[32,8192]{1,0:T(8,128)} %momentum.1) | copy-start | bytes 3145732
  120.2 29.5 %copy-start.1 = (f32[1,32,8192]{2,1,0:T(8,128)S(1)}, f32[1,32,8192]{2,1,0:T(8,128)}, u32[]{:S(2)}) copy-start(f32[1,32,8192]{2,1,0:T(8,128)} %feedback.3) | copy-start | bytes 3145732
  120.3 29.5 %copy-start.3 = (bf16[1,32,8192]{2,1,0:T(8,128)(2,1)S(1)}, bf16[1,32,8192]{2,1,0:T(8,128)(2,1)}, u32[]{:S(2)}) copy-start(bf16[1,32,8192]{2,1,0:T(8,128)(2,1)} %gradient.3) | copy-start | bytes 1572868

commit v2 on v1

v2 whole, which is shorter than its diff:
```python
import jax
import jax.numpy as jnp
from jax import lax
from jax.experimental import pallas as pl
from jax.experimental.pallas import tpu as pltpu
from jax.sharding import PartitionSpec as P

BETA = 0.9
HIGH = lax.Precision.HIGHEST

DP = 32
TP = 16
ROWS = 32
RANK = 64
LANES = 128
BLOCK = 16
GROUP = LANES // BLOCK
SHARD = DP * BLOCK
CHIPS = DP // 2
HALF = ROWS // 2


def dot(left, right, left_dim, right_dim):
    return lax.dot_general(
        left,
        right,
        (((left_dim,), (right_dim,)), ((), ())),
        precision=HIGH,
        preferred_element_type=jnp.float32,
    )


def swap_blocks(parts):
    parts = list(parts)
    block = lax.broadcasted_iota(jnp.int32, parts[0].shape, 1) // BLOCK
    for step in (1, 2, 4):
        upper = (block & step) != 0
        for i in range(GROUP):
            if i & step:
                continue
            a, b = parts[i], parts[i | step]
            parts[i] = jnp.where(upper, pltpu.roll(b, step * BLOCK, 1), a)
            parts[i | step] = jnp.where(upper, b, pltpu.roll(a, LANES - step * BLOCK, 1))
    return parts


def gather_blocks(matrix, lane_block):
    block = lax.broadcasted_iota(jnp.int32, (8, LANES), 1) // BLOCK
    moved = pltpu.roll(matrix, (GROUP - lane_block) % GROUP * BLOCK, 1)
    out = jnp.zeros((8, LANES), jnp.float32)
    for kh in range(GROUP):
        piece = moved[kh * 8 : (kh + 1) * 8, :]
        if kh:
            piece = pltpu.roll(piece, kh * BLOCK, 1)
        out = jnp.where(block == kh, piece, out)
    return out


def merge_kernel(core_ref, gradient, feedback, keep, send):
    first = core_ref[0] == 0
    for c in range(SHARD // LANES):
        for th in range(TP // GROUP):
            parts = []
            for tl in range(GROUP):
                lanes = pl.ds((th * GROUP + tl) * SHARD + c * LANES, LANES)
                parts.append(gradient[0, :, lanes].astype(jnp.float32) + feedback[0, :, lanes])
            parts = swap_blocks(parts)
            rows = slice(th * ROWS, (th + 1) * ROWS)
            for pair in range(GROUP // 2):
                chip = c * (GROUP // 2) + pair
                even, odd = parts[2 * pair], parts[2 * pair + 1]
                keep[chip, rows, :] = jnp.where(first, even, odd)
                send[chip, rows, :] = jnp.where(first, odd, even)


def add_kernel(left, right, out):
    out[...] = left[...] + right[...]


def pack_q_kernel(d_ref, q_ref, out):
    d = d_ref[0]
    tile = q_ref[:, pl.ds(pl.multiple_of(d // GROUP * LANES, LANES), LANES)]
    packed = gather_blocks(tile, d % GROUP)
    for t in range(TP):
        out[t] = packed


def unpack_blocks(parts, th):
    return jnp.concatenate(swap_blocks([parts[th * GROUP + tl] for tl in range(GROUP)]), axis=0)


def factor_kernel(merged, q_parts, factor_out, sum_out):
    total = merged[0]
    for chip in range(1, CHIPS):
        total = total + merged[chip]
    sum_out[...] = total
    factor = jnp.zeros((ROWS, LANES), jnp.float32)
    for th in range(TP // GROUP):
        q_tile = unpack_blocks(q_parts, th)
        q_twice = jnp.concatenate([q_tile, q_tile], axis=0)
        factor = factor + dot(total[th * ROWS : (th + 1) * ROWS], q_twice, 1, 1)
    lane = lax.broadcasted_iota(jnp.int32, (HALF, LANES), 1)
    packed = jnp.where(lane < RANK, factor[:HALF], factor[HALF:])
    for d in range(DP):
        factor_out[d] = packed


def unpack_rows(packed):
    return jnp.concatenate([packed[:, :RANK], packed[:, RANK:]], axis=0)


def project_kernel(factors, total, out):
    packed = factors[0]
    for d in range(1, DP):
        packed = packed + factors[d]
    rows = unpack_rows(packed)
    for th in range(TP // GROUP):
        term = dot(rows, total[th * ROWS : (th + 1) * ROWS, :], 0, 0)
        chunks = swap_blocks([term[kh * 8 : (kh + 1) * 8] for kh in range(GROUP)])
        for tl, chunk in enumerate(chunks):
            out[th * GROUP + tl, :HALF, :] = packed
            out[th * GROUP + tl, HALF:, :] = chunk


def chunk_kernel(parts, out):
    total = parts[0, HALF:, :]
    for t in range(1, TP):
        total = total + parts[t, HALF:, :]
    for t in range(TP):
        out[t] = total


def inverse_triangle(gram, rows_ref):
    row = lax.broadcasted_iota(jnp.int32, (RANK, LANES), 0)
    lane = lax.broadcasted_iota(jnp.int32, (RANK, LANES), 1)
    identity = jnp.where(lane == row + RANK, 1.0, 0.0)
    work = jnp.concatenate([gram, jnp.zeros_like(gram)], axis=1) + identity
    for k in range(RANK):
        pivot_row = work[k : k + 1, :]
        pivot = work[k : k + 1, k : k + 1]
        rows_ref[k : k + 1, :] = pivot_row * lax.rsqrt(pivot)
        if k + 1 < RANK:
            scaled = pivot_row * (1.0 / pivot)
            column = work[:, k : k + 1]
            work = work - jnp.where(row > k, column, 0.0) * scaled
    return rows_ref[:, RANK:]


def basis_kernel(t_ref, parts, inverse_out, basis_out, rows_ref):
    flat = parts[:, :HALF, :].reshape(TP * HALF, LANES)
    whole = unpack_rows(flat)
    inverse = inverse_triangle(dot(whole, whole, 0, 0), rows_ref)
    inverse_out[...] = inverse
    own = unpack_rows(parts[t_ref[0], :HALF, :])
    basis_out[...] = dot(own, inverse, 1, 1)


def approx_kernel(t_ref, inverse, basis, w_parts, out):
    t = t_ref[0]
    approx, q_tiles = [], []
    for th in range(TP // GROUP):
        q_tile = dot(inverse[...], unpack_blocks(w_parts, th), 1, 0) * (1.0 / DP)
        q_tiles.append(q_tile)
        approx.append(dot(basis[...], q_tile, 1, 0))
    mine = jnp.where(t // GROUP == 0, q_tiles[0], q_tiles[1])
    message = jnp.concatenate(approx + [gather_blocks(mine, t % GROUP)], axis=0)
    for chip in range(CHIPS):
        out[chip] = message


def finish_kernel(core_ref, gradient, feedback, momentum, own, other, new_feedback, new_momentum, q_out):
    first = core_ref[0] == 0

    def blocks(c, rows):
        parts = []
        for pair in range(GROUP // 2):
            chip = c * (GROUP // 2) + pair
            mine, theirs = own[chip, rows, :], other[chip, rows, :]
            parts += [jnp.where(first, mine, theirs), jnp.where(first, theirs, mine)]
        return swap_blocks(parts)

    for c in range(SHARD // LANES):
        for th in range(TP // GROUP):
            for tl, part in enumerate(blocks(c, slice(th * ROWS, (th + 1) * ROWS))):
                lanes = pl.ds((th * GROUP + tl) * SHARD + c * LANES, LANES)
                merged = gradient[0, :, lanes].astype(jnp.float32) + feedback[0, :, lanes]
                new_feedback[0, :, lanes] = merged - part
                new_momentum[:, lanes] = BETA * momentum[:, lanes] + part
        tail = blocks(c, slice(2 * ROWS, 2 * ROWS + 8))
        q_out[:, c * LANES : (c + 1) * LANES] = jnp.concatenate(tail, axis=0)


def local(kernel, *shapes, scalars=0, inputs=1, scratch=(), flops=100_000, moved=100_000):
    return pl.pallas_call(
        kernel,
        out_shape=[jax.ShapeDtypeStruct(shape, jnp.float32) for shape in shapes],
        in_specs=[pl.BlockSpec(memory_space=pltpu.SMEM)] * scalars
        + [pl.BlockSpec(memory_space=pltpu.VMEM)] * inputs,
        out_specs=[pl.BlockSpec(memory_space=pltpu.VMEM)] * len(shapes),
        scratch_shapes=list(scratch),
        cost_estimate=pl.CostEstimate(flops=flops, bytes_accessed=moved, transcendentals=0),
        compiler_params=pltpu.CompilerParams(vmem_limit_bytes=32 * 1024 * 1024),
    )


def exchange(parts, axis, groups=None):
    return lax.all_to_all(parts, axis, 0, 0, tiled=True, axis_index_groups=groups)


def swap_cores(parts):
    return lax.ppermute(parts, "dp", [(d, d ^ 1) for d in range(DP)])


def on_device(gradient, feedback, momentum, q_previous):
    d = lax.axis_index("dp").reshape(1)
    t = lax.axis_index("tensor").reshape(1)
    core = d % 2
    chips = [list(range(c, DP, 2)) for c in range(2)]
    q_parts = local(pack_q_kernel, (TP, 8, LANES), scalars=1)(d, q_previous)[0]
    q_parts = exchange(q_parts, "tensor")
    whole = (CHIPS, 2 * ROWS, LANES)
    keep, send = local(merge_kernel, whole, whole, scalars=1, inputs=2)(core, gradient, feedback)
    merged = local(add_kernel, whole, inputs=2)(keep, swap_cores(send))[0]
    merged = exchange(merged, "dp", chips)
    factor, total = local(
        factor_kernel, (DP, HALF, LANES), (2 * ROWS, LANES), inputs=2
    )(merged, q_parts)
    factor = exchange(factor, "dp")
    parts = local(project_kernel, (TP, HALF + 8, LANES), inputs=2)(factor, total)[0]
    parts = exchange(parts, "tensor")
    w_parts = local(chunk_kernel, (TP, 8, LANES))(parts)[0]
    w_parts = exchange(w_parts, "tensor")
    inverse, basis = local(
        basis_kernel,
        (RANK, RANK),
        (ROWS, RANK),
        scalars=1,
        scratch=[pltpu.VMEM((RANK, LANES), jnp.float32)],
    )(t, parts)
    own = local(approx_kernel, (CHIPS, 2 * ROWS + 8, LANES), scalars=1, inputs=3)(
        t, inverse, basis, w_parts
    )[0]
    own = exchange(own, "dp", chips)
    other = swap_cores(own)
    return tuple(
        local(
            finish_kernel, feedback.shape, momentum.shape, q_previous.shape, scalars=1, inputs=5
        )(core, gradient, feedback, momentum, own, other)
    )


def solution(mesh):
    placed = (
        P("dp", "tensor", None),
        P("dp", "tensor", None),
        P("tensor", None),
        P(None, "tensor"),
    )
    return jax.shard_map(
        on_device,
        mesh=mesh,
        in_specs=placed,
        out_specs=(P("dp", "tensor", None), P("tensor", None), P(None, "tensor")),
        check_vma=False,
    )
```

time: 154 us -> 129 us (0.84)
  blocking collectives: 82.9 us -> 60.9 us
  waiting for transfers between devices: 30.5 us -> 18.8 us
  starting transfers between devices: 22.2 us -> 32 us
    all_to_all x4, blocking collectives: 82.9 us -> 60.9 us  [exchange(): lax.all_to_all(parts, axis, 0, 0, tiled=True, axis_index_groups=groups)]
    ppermute x0 -> x2, starting transfers between devices: none -> 14.1 us  [swap_cores(): return lax.ppermute(parts, 'dp', [(d, d ^ 1) for d in range(DP)])]
    all_to_all x2, waiting for transfers between devices: 30.5 us -> 17.2 us  [exchange(): lax.all_to_all(parts, axis, 0, 0, tiled=True, axis_index_groups=groups)]
    all_to_all x2, starting transfers between devices: 22.2 us -> 17.8 us  [exchange(): lax.all_to_all(parts, axis, 0, 0, tiled=True, axis_index_groups=groups)]
    ppermute x0 -> x2, waiting for transfers between devices: none -> 1.61 us  [swap_cores(): return lax.ppermute(parts, 'dp', [(d, d ^ 1) for d in range(DP)])]
    pallas_call x6 -> x9, Pallas kernels: 13.7 us -> 14.2 us  [the longest x1 5.89 us: on_device(): local(basis_kernel, (RANK, RANK), (ROWS, RANK), scalars=1, scratch=[pltpu...]
  transfers between devices with their start and end apart: 2 -> 4, of which waited for: 2 -> 3; matrix products, arithmetic and copies ran while one was open for 0% -> 0% of each run, Pallas kernels for 1% -> 5%
where the time goes in v2:
time: 129 us
  blocking collectives  60.9 us (47%)
  starting transfers between devices  32 us (25%)
  waiting for transfers between devices  18.8 us (15%)
  Pallas kernels  14.2 us (11%)
  local copies, waits for them, and re-layouts  2.28 us (2%)
    all_to_all x4, blocking collectives, exchange(): lax.all_to_all(parts, axis, 0, 0, tiled=True, axis_index_groups=groups)  60.9 us
    all_to_all x2, starting transfers between devices, exchange(): lax.all_to_all(parts, axis, 0, 0, tiled=True, axis_index_groups=groups)  17.8 us
    all_to_all x2, waiting for transfers between devices, exchange(): lax.all_to_all(parts, axis, 0, 0, tiled=True, axis_index_groups=groups)  17.2 us
    ppermute x2, starting transfers between devices, swap_cores(): return lax.ppermute(parts, 'dp', [(d, d ^ 1) for d in range(DP)])  14.1 us
    pallas_call x1, Pallas kernels, on_device(): local(basis_kernel, (RANK, RANK), (ROWS, RANK), scalars=1, scratch=[pltpu...  5.89 us
    pallas_call x1, Pallas kernels, on_device(): local(finish_kernel, feedback.shape, momentum.shape, q_previous.shape, sc...  3.5 us
  transfers between devices with their start and end apart: 4, of which 3 were waited for; matrix products, arithmetic and copies ran while one was open for 0% of the time, Pallas kernels for 5%

profile of v2, /device:TPU:1, one launch (start us, length us, event | category | flops | bytes accessed | tf_op | source)
XLA Modules:
  0.0 128.9 jit_solution(935610917351900206)
XLA Ops:
  0.6 0.0 copy-start
  0.7 1.2 copy-done
  1.9 0.0 copy-start.2
  1.9 1.0 copy-done.2
  2.9 1.6 %shard_map.67 = (f32[16,64,128]{2,1,0:T(8,128)S(1)}, f32[16,64,128]{2,1,0:T(8,128)S(1)}) custom-call(s32[1]{0:T(128)S(6)} %select_n.7.core_ref, bf16[1,32,8192]{2,1,0:T(8,128)(2,1)S(1)} %copy-done.2, f32[1,32,8192]{2,1,0:T(8,128)S(1)} %copy-done), custom_call_target="tpu_custom_call" | custom-call | flops 100000 | bytes 100000 | tf_op jit(solution)/shard_map/pallas_call | solution.py:222
  4.5 8.8 %collective-permute-start = (f32[16,64,128]{2,1,0:T(8,128)S(1)}, f32[16,64,128]{2,1,0:T(8,128)S(1)}, u32[]{:S(2)}, u32[]{:S(2)}) collective-permute-start(f32[16,64,128]{2,1,0:T(8,128)S(1)} %get-tuple-element.10), channel_id=1, source_target_pairs={{0,16},{16,0},{32,48},{48,32},{64,80},{80,64},{96,112},{112,96},{1... | collective-permute-start | bytes 1572872 | tf_op jit(solution)/shard_map/ppermute | solution.py:211
  13.3 0.0 copy-done.5
  13.3 0.8 shard_map.69
  14.1 9.5 %all-to-all-start.1 = ((f32[16,8,128]{2,1,0:T(8,128)}), f32[16,8,128]{2,1,0:T(8,128)S(1)}, u32[]{:S(2)}, u32[]{:S(2)}) async-start(f32[16,8,128]{2,1,0:T(8,128)} %shard_map.69), calls=%async_computation.1 | async-start | bytes 131072 | tf_op jit(solution)/shard_map/all_to_all | solution.py:207
  23.6 0.0 collective-permute-done.right
  23.6 0.1 shard_map.68
  23.7 11.6 %all-to-all-done.1.q_parts = f32[16,8,128]{2,1,0:T(8,128)S(1)} async-done(((f32[16,8,128]{2,1,0:T(8,128)}), f32[16,8,128]{2,1,0:T(8,128)S(1)}, u32[]{:S(2)}, u32[]{:S(2)}) %all-to-all-start.1) | async-done | bytes 65568 | tf_op jit(solution)/shard_map/all_to_all | solution.py:207
  35.3 15.9 %all_to_all.30.merged = f32[16,64,128]{2,1,0:T(8,128)S(1)} all-to-all(f32[16,64,128]{2,1,0:T(8,128)S(1)} %shard_map.68), channel_id=1, replica_groups={{0,32,64,96,128,160,192,224,256,288,320,352,384,416,448,480},{16,48,80,..., dimensions={0} | all-to-all | bytes 1048576 | tf_op jit(solution)/shard_map/all_to_all | solution.py:207
  51.2 0.5 shard_map.70
  51.8 15.0 %all_to_all.31.factors = f32[32,16,128]{2,1,0:T(8,128)S(1)} all-to-all(f32[32,16,128]{2,1,0:T(8,128)S(1)} %get-tuple-element.11), channel_id=1, replica_groups=mesh['dp'=32,'tensor'=16] {'dp'}, dimensions={0} | all-to-all | bytes 524288 | tf_op jit(solution)/shard_map/all_to_all | solution.py:207
  66.8 0.6 shard_map.71
  67.4 0.0 copy-start.4
  67.4 17.0 %all_to_all.32.parts = f32[16,24,128]{2,1,0:T(8,128)S(1)} all-to-all(f32[16,24,128]{2,1,0:T(8,128)S(1)} %shard_map.71), channel_id=1, replica_groups=mesh['dp'=32,'tensor'=16] {'tensor'}, dimensions={0} | all-to-all | bytes 393216 | tf_op jit(solution)/shard_map/all_to_all | solution.py:207
  84.3 0.6 shard_map.73
  85.0 8.3 %all-to-all-start.4 = ((f32[16,8,128]{2,1,0:T(8,128)}), f32[16,8,128]{2,1,0:T(8,128)S(1)}, u32[]{:S(2)}, u32[]{:S(2)}) async-start(f32[16,8,128]{2,1,0:T(8,128)} %shard_map.73), calls=%async_computation.4 | async-start | bytes 131072 | tf_op jit(solution)/shard_map/all_to_all | solution.py:207
  93.3 0.0 copy-start.1
  93.3 5.9 %shard_map.72 = (f32[64,64]{1,0:T(8,128)S(1)}, f32[32,64]{1,0:T(8,128)S(1)}) custom-call(s32[1]{0:T(128)} %bitcast.1.t_ref, f32[16,24,128]{2,1,0:T(8,128)S(1)} %all_to_all.32.parts), custom_call_target="tpu_custom_call" | custom-call | flops 100000 | bytes 100000 | tf_op jit(solution)/shard_map/pallas_call | solution.py:233
  99.2 5.7 %all-to-all-done.4.w_parts = f32[16,8,128]{2,1,0:T(8,128)S(1)} async-done(((f32[16,8,128]{2,1,0:T(8,128)}), f32[16,8,128]{2,1,0:T(8,128)S(1)}, u32[]{:S(2)}, u32[]{:S(2)}) %all-to-all-start.4) | async-done | bytes 65568 | tf_op jit(solution)/shard_map/all_to_all | solution.py:207
  104.9 0.6 shard_map.74
  105.5 0.0 copy-start.3
  105.5 13.0 %all_to_all.33.own = f32[16,72,128]{2,1,0:T(8,128)S(1)} all-to-all(f32[16,72,128]{2,1,0:T(8,128)S(1)} %shard_map.74), channel_id=1, replica_groups={{0,32,64,96,128,160,192,224,256,288,320,352,384,416,448,480},{16,48,80,..., dimensions={0} | all-to-all | bytes 1179648 | tf_op jit(solution)/shard_map/all_to_all | solution.py:207
  118.5 5.3 %collective-permute-start.1 = (f32[16,72,128]{2,1,0:T(8,128)S(1)}, f32[16,72,128]{2,1,0:T(8,128)S(1)}, u32[]{:S(2)}, u32[]{:S(2)}) collective-permute-start(f32[16,72,128]{2,1,0:T(8,128)S(1)} %all_to_all.33.own), channel_id=1, source_target_pairs={{0,16},{16,0},{32,48},{48,32},{64,80},{80,64},{96,112},{112,96},{1... | collective-permute-start | bytes 1769480 | tf_op jit(solution)/shard_map/ppermute | solution.py:211
  123.8 1.6 %collective-permute-done.1.other = f32[16,72,128]{2,1,0:T(8,128)S(1)} collective-permute-done((f32[16,72,128]{2,1,0:T(8,128)S(1)}, f32[16,72,128]{2,1,0:T(8,128)S(1)}, u32[]{:S(2)}, u32[]{:S(2)}) %collective-permute-start.1) | collective-permute-done | bytes 589856 | tf_op jit(solution)/shard_map/ppermute | solution.py:211
  125.4 0.0 copy-done.4
  125.4 0.0 copy-done.1
  125.4 0.0 copy-done.3
  125.4 3.5 %shard_map.75 = (f32[1,32,8192]{2,1,0:T(8,128)}, f32[32,8192]{1,0:T(8,128)}, f32[64,512]{1,0:T(8,128)}) custom-call(s32[1]{0:T(128)S(6)} %select_n.7.core_ref, bf16[1,32,8192]{2,1,0:T(8,128)(2,1)S(1)} %copy-done.3, f32[1,32,8192]{2,1,0:T(8,128)S(1)} %copy-done.1, f32[32,8192]{1,0:T(8,128)S(1)} %copy-done.4, f32[16,72,128]{2,1,0:T(8,128)S(1)} %all_to_all.33.own, ...), custom_call_target="tpu_custom_call" | custom-call | flops 100000 | bytes 100000 | tf_op jit(solution)/shard_map/pallas_call | solution.py:246
  (1 shorter events, 0.0 us)
Async XLA Ops:
  0.6 1.2 copy-start
  1.9 1.0 copy-start.2
  2.9 10.4 %copy-start.5 = (f32[64,512]{1,0:T(8,128)S(1)}, f32[64,512]{1,0:T(8,128)}, u32[]{:S(2)}) copy-start(f32[64,512]{1,0:T(8,128)} %q_ref.1) | copy-start | bytes 393220
  4.5 19.1 %collective-permute-start = (f32[16,64,128]{2,1,0:T(8,128)S(1)}, f32[16,64,128]{2,1,0:T(8,128)S(1)}, u32[]{:S(2)}, u32[]{:S(2)}) collective-permute-start(f32[16,64,128]{2,1,0:T(8,128)S(1)} %get-tuple-element.10), channel_id=1, source_target_pairs={{0,16},{16,0},{32,48},{48,32},{64,80},{80,64},{96,112},{112,96},{1... | collective-permute-start | bytes 1572872 | tf_op jit(solution)/shard_map/ppermute | solution.py:211
  14.1 21.2 %all-to-all-start.1 = ((f32[16,8,128]{2,1,0:T(8,128)}), f32[16,8,128]{2,1,0:T(8,128)S(1)}, u32[]{:S(2)}, u32[]{:S(2)}) async-start(f32[16,8,128]{2,1,0:T(8,128)} %shard_map.69), calls=%async_computation.1 | async-start | bytes 131072 | tf_op jit(solution)/shard_map/all_to_all | solution.py:207
  67.4 58.1 %copy-start.4 = (f32[32,8192]{1,0:T(8,128)S(1)}, f32[32,8192]{1,0:T(8,128)}, u32[]{:S(2)}) copy-start(f32[32,8192]{1,0:T(8,128)} %momentum.1) | copy-start | bytes 3145732
  85.0 19.9 %all-to-all-start.4 = ((f32[16,8,128]{2,1,0:T(8,128)}), f32[16,8,128]{2,1,0:T(8,128)S(1)}, u32[]{:S(2)}, u32[]{:S(2)}) async-start(f32[16,8,128]{2,1,0:T(8,128)} %shard_map.73), calls=%async_computation.4 | async-start | bytes 131072 | tf_op jit(solution)/shard_map/all_to_all | solution.py:207
  93.3 32.1 %copy-start.1 = (f32[1,32,8192]{2,1,0:T(8,128)S(1)}, f32[1,32,8192]{2,1,0:T(8,128)}, u32[]{:S(2)}) copy-start(f32[1,32,8192]{2,1,0:T(8,128)} %feedback.3) | copy-start | bytes 3145732
  105.5 19.9 %copy-start.3 = (bf16[1,32,8192]{2,1,0:T(8,128)(2,1)S(1)}, bf16[1,32,8192]{2,1,0:T(8,128)(2,1)}, u32[]{:S(2)}) copy-start(bf16[1,32,8192]{2,1,0:T(8,128)(2,1)} %gradient.3) | copy-start | bytes 1572868
  118.5 6.9 %collective-permute-start.1 = (f32[16,72,128]{2,1,0:T(8,128)S(1)}, f32[16,72,128]{2,1,0:T(8,128)S(1)}, u32[]{:S(2)}, u32[]{:S(2)}) collective-permute-start(f32[16,72,128]{2,1,0:T(8,128)S(1)} %all_to_all.33.own), channel_id=1, source_target_pairs={{0,16},{16,0},{32,48},{48,32},{64,80},{80,64},{96,112},{112,96},{1... | collective-permute-start | bytes 1769480 | tf_op jit(solution)/shard_map/ppermute | solution.py:211

commit v3 on v2

--- a/solution.py
+++ b/solution.py
@@ -73,27 +73,35 @@
                 send[chip, rows, :] = jnp.where(first, odd, even)
 
 
-def add_kernel(left, right, out):
-    out[...] = left[...] + right[...]
-
-
-def pack_q_kernel(d_ref, q_ref, out):
-    d = d_ref[0]
-    tile = q_ref[:, pl.ds(pl.multiple_of(d // GROUP * LANES, LANES), LANES)]
-    packed = gather_blocks(tile, d % GROUP)
-    for t in range(TP):
-        out[t] = packed
+def copy_kernel(parts, out):
+    out[...] = parts[...]
+
+
+def add_kernel(left, right, q_parts, out):
+    out[:, : 2 * ROWS, :] = left[...] + right[...]
+    out[:, 2 * ROWS :, :] = q_parts[...]
+
+
+def pack_q_kernel(core_ref, q_ref, out):
+    first = core_ref[0] == 0
+    for c in range(SHARD // LANES):
+        lanes = slice(c * LANES, (c + 1) * LANES)
+        parts = swap_blocks([q_ref[kh * 8 : (kh + 1) * 8, lanes] for kh in range(GROUP)])
+        for pair in range(GROUP // 2):
+            out[c * (GROUP // 2) + pair] = jnp.where(first, parts[2 * pair], parts[2 * pair + 1])
 
 
 def unpack_blocks(parts, th):
     return jnp.concatenate(swap_blocks([parts[th * GROUP + tl] for tl in range(GROUP)]), axis=0)
 
 
-def factor_kernel(merged, q_parts, factor_out, sum_out):
-    total = merged[0]
+def factor_kernel(t_ref, merged, factor_out, sum_out):
+    total = merged[0, : 2 * ROWS, :]
     for chip in range(1, CHIPS):
-        total = total + merged[chip]
+        total = total + merged[chip, : 2 * ROWS, :]
     sum_out[...] = total
+    t = t_ref[0]
+    q_parts = [merged[(shard - t + TP) % TP, 2 * ROWS :, :] for shard in range(TP)]
     factor = jnp.zeros((ROWS, LANES), jnp.float32)
     for th in range(TP // GROUP):
         q_tile = unpack_blocks(q_parts, th)
@@ -211,20 +219,25 @@
     return lax.ppermute(parts, "dp", [(d, d ^ 1) for d in range(DP)])
 
 
+def fetch_shards(parts):
+    pairs = [(d * TP + (t + d // 2) % TP, d * TP + t) for d in range(DP) for t in range(TP)]
+    return lax.ppermute(parts, ("dp", "tensor"), pairs)
+
+
 def on_device(gradient, feedback, momentum, q_previous):
-    d = lax.axis_index("dp").reshape(1)
+    core = (lax.axis_index("dp") & 1).reshape(1)
     t = lax.axis_index("tensor").reshape(1)
-    core = d % 2
     chips = [list(range(c, DP, 2)) for c in range(2)]
-    q_parts = local(pack_q_kernel, (TP, 8, LANES), scalars=1)(d, q_previous)[0]
-    q_parts = exchange(q_parts, "tensor")
     whole = (CHIPS, 2 * ROWS, LANES)
+    q_parts = local(pack_q_kernel, (CHIPS, 8, LANES), scalars=1)(core, q_previous)[0]
+    q_parts = fetch_shards(q_parts)
+    q_parts = local(copy_kernel, (CHIPS, 8, LANES), flops=10_000_000_000)(q_parts)[0]
     keep, send = local(merge_kernel, whole, whole, scalars=1, inputs=2)(core, gradient, feedback)
-    merged = local(add_kernel, whole, inputs=2)(keep, swap_cores(send))[0]
+    merged = local(add_kernel, (CHIPS, 2 * ROWS + 8, LANES), inputs=3)(
+        keep, swap_cores(send), q_parts
+    )[0]
     merged = exchange(merged, "dp", chips)
-    factor, total = local(
-        factor_kernel, (DP, HALF, LANES), (2 * ROWS, LANES), inputs=2
-    )(merged, q_parts)
+    factor, total = local(factor_kernel, (DP, HALF, LANES), (2 * ROWS, LANES), scalars=1)(t, merged)
     factor = exchange(factor, "dp")
     parts = local(project_kernel, (TP, HALF + 8, LANES), inputs=2)(factor, total)[0]
     parts = exchange(parts, "tensor")

time: 129 us -> 129 us (level)
  blocking collectives: 60.9 us -> 51.5 us
  starting transfers between devices: 32 us -> 38.9 us
    all_to_all x4 -> x3, blocking collectives: 60.9 us -> 51.5 us  [exchange(): lax.all_to_all(parts, axis, 0, 0, tiled=True, axis_index_groups=groups)]
    all_to_all x2, starting transfers between devices: 17.8 us -> 24.1 us  [exchange(): lax.all_to_all(parts, axis, 0, 0, tiled=True, axis_index_groups=groups)]
    ppermute x2, waiting for transfers between devices: 1.61 us -> 3.1 us  [swap_cores(): return lax.ppermute(parts, 'dp', [(d, d ^ 1) for d in range(DP)])]
  transfers between devices with their start and end apart: 4 -> 5, of which waited for: 3 -> 4; matrix products, arithmetic and copies ran while one was open for 0% -> 0% of each run, Pallas kernels for 5% -> 6%
where the time goes in v3:
time: 129 us
  blocking collectives  51.5 us (40%)
  starting transfers between devices  38.9 us (30%)
  waiting for transfers between devices  19.9 us (15%)
  Pallas kernels  14.5 us (11%)
  local copies, waits for them, and re-layouts  3.18 us (2%)
    all_to_all x3, blocking collectives, exchange(): lax.all_to_all(parts, axis, 0, 0, tiled=True, axis_index_groups=groups)  51.5 us
    all_to_all x2, starting transfers between devices, exchange(): lax.all_to_all(parts, axis, 0, 0, tiled=True, axis_index_groups=groups)  24.1 us
    all_to_all x2, waiting for transfers between devices, exchange(): lax.all_to_all(parts, axis, 0, 0, tiled=True, axis_index_groups=groups)  16.8 us
    ppermute x2, starting transfers between devices, swap_cores(): return lax.ppermute(parts, 'dp', [(d, d ^ 1) for d in range(DP)])  14.1 us
    pallas_call x1, Pallas kernels, on_device(): local(basis_kernel, (RANK, RANK), (ROWS, RANK), scalars=1, scratch=[pltpu...  5.89 us
    pallas_call x1, Pallas kernels, on_device(): local(finish_kernel, feedback.shape, momentum.shape, q_previous.shape, sc...  3.5 us
    unnamed x12, local copies, waits for them, and re-layouts  3.18 us
    ppermute x2, waiting for transfers between devices, swap_cores(): return lax.ppermute(parts, 'dp', [(d, d ^ 1) for d in range(DP)])  3.1 us
  transfers between devices with their start and end apart: 5, of which 4 were waited for; matrix products, arithmetic and copies ran while one was open for 0% of the time, Pallas kernels for 6%

profile of v3, /device:TPU:1, one launch (start us, length us, event | category | flops | bytes accessed | tf_op | source)
XLA Modules:
  0.0 128.7 jit_solution(18004725580292791326)
XLA Ops:
  0.6 0.0 copy-start.5
  0.6 0.9 copy-done.5
  1.5 0.2 shard_map.68
  1.8 0.7 collective-permute-start.1
  2.5 0.0 copy-start
  2.5 1.2 copy-done
  3.7 1.0 copy-done.2
  4.7 1.6 %shard_map.67 = (f32[16,64,128]{2,1,0:T(8,128)S(1)}, f32[16,64,128]{2,1,0:T(8,128)S(1)}) custom-call(s32[1]{0:T(128)} %bitcast.core_ref, bf16[1,32,8192]{2,1,0:T(8,128)(2,1)S(1)} %copy-done.2, f32[1,32,8192]{2,1,0:T(8,128)S(1)} %copy-done), custom_call_target="tpu_custom_call" | custom-call | flops 100000 | bytes 100000 | tf_op jit(solution)/shard_map/pallas_call | solution.py:235
  6.3 8.8 %collective-permute-start = (f32[16,64,128]{2,1,0:T(8,128)S(1)}, f32[16,64,128]{2,1,0:T(8,128)S(1)}, u32[]{:S(2)}, u32[]{:S(2)}) collective-permute-start(f32[16,64,128]{2,1,0:T(8,128)S(1)} %get-tuple-element.10), channel_id=1, source_target_pairs={{0,16},{16,0},{32,48},{48,32},{64,80},{80,64},{96,112},{112,96},{1... | collective-permute-start | bytes 1572872 | tf_op jit(solution)/shard_map/ppermute | solution.py:219
  15.1 0.0 collective-permute-done.1.parts
  15.1 1.5 %collective-permute-done.right = f32[16,64,128]{2,1,0:T(8,128)S(1)} collective-permute-done((f32[16,64,128]{2,1,0:T(8,128)S(1)}, f32[16,64,128]{2,1,0:T(8,128)S(1)}, u32[]{:S(2)}, u32[]{:S(2)}) %collective-permute-start) | collective-permute-done | bytes 524320 | tf_op jit(solution)/shard_map/ppermute | solution.py:219
  16.6 0.9 shard_map.70
  17.5 15.8 %all-to-all-start = ((f32[16,72,128]{2,1,0:T(8,128)}), f32[16,72,128]{2,1,0:T(8,128)S(1)}, u32[]{:S(2)}, u32[]{:S(2)}) async-start(f32[16,72,128]{2,1,0:T(8,128)} %shard_map.70), calls=%async_computation | async-start | bytes 1179648 | tf_op jit(solution)/shard_map/all_to_all | solution.py:215
  33.3 11.1 %all-to-all-done.merged = f32[16,72,128]{2,1,0:T(8,128)S(1)} async-done(((f32[16,72,128]{2,1,0:T(8,128)}), f32[16,72,128]{2,1,0:T(8,128)S(1)}, u32[]{:S(2)}, u32[]{:S(2)}) %all-to-all-start) | async-done | bytes 589856 | tf_op jit(solution)/shard_map/all_to_all | solution.py:215
  44.4 0.6 shard_map.71
  45.0 14.0 %all_to_all.25.factors = f32[32,16,128]{2,1,0:T(8,128)S(1)} all-to-all(f32[32,16,128]{2,1,0:T(8,128)S(1)} %get-tuple-element.11), channel_id=1, replica_groups=mesh['dp'=32,'tensor'=16] {'dp'}, dimensions={0} | all-to-all | bytes 524288 | tf_op jit(solution)/shard_map/all_to_all | solution.py:215
  59.0 0.6 shard_map.72
  59.6 0.0 copy-start.4
  59.6 24.6 %all_to_all.26.parts = f32[16,24,128]{2,1,0:T(8,128)S(1)} all-to-all(f32[16,24,128]{2,1,0:T(8,128)S(1)} %shard_map.72), channel_id=1, replica_groups=mesh['dp'=32,'tensor'=16] {'tensor'}, dimensions={0} | all-to-all | bytes 393216 | tf_op jit(solution)/shard_map/all_to_all | solution.py:215
  84.1 0.6 shard_map.74
  84.8 8.3 %all-to-all-start.3 = ((f32[16,8,128]{2,1,0:T(8,128)}), f32[16,8,128]{2,1,0:T(8,128)S(1)}, u32[]{:S(2)}, u32[]{:S(2)}) async-start(f32[16,8,128]{2,1,0:T(8,128)} %shard_map.74), calls=%async_computation.3 | async-start | bytes 131072 | tf_op jit(solution)/shard_map/all_to_all | solution.py:215
  93.1 0.0 copy-start.1
  93.1 5.9 %shard_map.73 = (f32[64,64]{1,0:T(8,128)S(1)}, f32[32,64]{1,0:T(8,128)S(1)}) custom-call(s32[1]{0:T(128)} %bitcast.1.t_ref, f32[16,24,128]{2,1,0:T(8,128)S(1)} %all_to_all.26.parts), custom_call_target="tpu_custom_call" | custom-call | flops 100000 | bytes 100000 | tf_op jit(solution)/shard_map/pallas_call | solution.py:246
  99.0 5.7 %all-to-all-done.3.w_parts = f32[16,8,128]{2,1,0:T(8,128)S(1)} async-done(((f32[16,8,128]{2,1,0:T(8,128)}), f32[16,8,128]{2,1,0:T(8,128)S(1)}, u32[]{:S(2)}, u32[]{:S(2)}) %all-to-all-start.3) | async-done | bytes 65568 | tf_op jit(solution)/shard_map/all_to_all | solution.py:215
  104.7 0.6 shard_map.75
  105.3 0.0 copy-start.3
  105.3 13.0 %all_to_all.27.own = f32[16,72,128]{2,1,0:T(8,128)S(1)} all-to-all(f32[16,72,128]{2,1,0:T(8,128)S(1)} %shard_map.75), channel_id=1, replica_groups={{0,32,64,96,128,160,192,224,256,288,320,352,384,416,448,480},{16,48,80,..., dimensions={0} | all-to-all | bytes 1179648 | tf_op jit(solution)/shard_map/all_to_all | solution.py:215
  118.3 5.3 %collective-permute-start.2 = (f32[16,72,128]{2,1,0:T(8,128)S(1)}, f32[16,72,128]{2,1,0:T(8,128)S(1)}, u32[]{:S(2)}, u32[]{:S(2)}) collective-permute-start(f32[16,72,128]{2,1,0:T(8,128)S(1)} %all_to_all.27.own), channel_id=1, source_target_pairs={{0,16},{16,0},{32,48},{48,32},{64,80},{80,64},{96,112},{112,96},{1... | collective-permute-start | bytes 1769480 | tf_op jit(solution)/shard_map/ppermute | solution.py:219
  123.6 1.6 %collective-permute-done.2.other = f32[16,72,128]{2,1,0:T(8,128)S(1)} collective-permute-done((f32[16,72,128]{2,1,0:T(8,128)S(1)}, f32[16,72,128]{2,1,0:T(8,128)S(1)}, u32[]{:S(2)}, u32[]{:S(2)}) %collective-permute-start.2) | collective-permute-done | bytes 589856 | tf_op jit(solution)/shard_map/ppermute | solution.py:219
  125.2 0.0 copy-done.4
  125.2 0.0 copy-done.1
  125.2 3.5 %shard_map.76 = (f32[1,32,8192]{2,1,0:T(8,128)}, f32[32,8192]{1,0:T(8,128)}, f32[64,512]{1,0:T(8,128)}) custom-call(s32[1]{0:T(128)} %bitcast.core_ref, bf16[1,32,8192]{2,1,0:T(8,128)(2,1)S(1)} %copy-done.3, f32[1,32,8192]{2,1,0:T(8,128)S(1)} %copy-done.1, f32[32,8192]{1,0:T(8,128)S(1)} %copy-done.4, f32[16,72,128]{2,1,0:T(8,128)S(1)} %all_to_all.27.own, ...), custom_call_target="tpu_custom_call" | custom-call | flops 100000 | bytes 100000 | tf_op jit(solution)/shard_map/pallas_call | solution.py:259
  (3 shorter events, 0.0 us)
Async XLA Ops:
  0.6 0.9 copy-start.5
  1.8 13.3 %collective-permute-start.1 = (f32[16,8,128]{2,1,0:T(8,128)S(1)}, f32[16,8,128]{2,1,0:T(8,128)S(1)}, u32[]{:S(2)}, u32[]{:S(2)}) collective-permute-start(f32[16,8,128]{2,1,0:T(8,128)S(1)} %shard_map.68), channel_id=1, source_target_pairs={{0,0},{1,1},{2,2},{3,3},{4,4},{5,5},{6,6},{7,7},{8,8},{9,9},{10,10... | collective-permute-start | bytes 196616 | tf_op jit(solution)/shard_map/ppermute | solution.py:224
  2.5 1.2 copy-start
  3.7 1.0 copy-start.2
  6.3 10.3 %collective-permute-start = (f32[16,64,128]{2,1,0:T(8,128)S(1)}, f32[16,64,128]{2,1,0:T(8,128)S(1)}, u32[]{:S(2)}, u32[]{:S(2)}) collective-permute-start(f32[16,64,128]{2,1,0:T(8,128)S(1)} %get-tuple-element.10), channel_id=1, source_target_pairs={{0,16},{16,0},{32,48},{48,32},{64,80},{80,64},{96,112},{112,96},{1... | collective-permute-start | bytes 1572872 | tf_op jit(solution)/shard_map/ppermute | solution.py:219
  17.5 26.9 %all-to-all-start = ((f32[16,72,128]{2,1,0:T(8,128)}), f32[16,72,128]{2,1,0:T(8,128)S(1)}, u32[]{:S(2)}, u32[]{:S(2)}) async-start(f32[16,72,128]{2,1,0:T(8,128)} %shard_map.70), calls=%async_computation | async-start | bytes 1179648 | tf_op jit(solution)/shard_map/all_to_all | solution.py:215
  59.6 65.7 %copy-start.4 = (f32[32,8192]{1,0:T(8,128)S(1)}, f32[32,8192]{1,0:T(8,128)}, u32[]{:S(2)}) copy-start(f32[32,8192]{1,0:T(8,128)} %momentum.1) | copy-start | bytes 3145732
  84.8 19.9 %all-to-all-start.3 = ((f32[16,8,128]{2,1,0:T(8,128)}), f32[16,8,128]{2,1,0:T(8,128)S(1)}, u32[]{:S(2)}, u32[]{:S(2)}) async-start(f32[16,8,128]{2,1,0:T(8,128)} %shard_map.74), calls=%async_computation.3 | async-start | bytes 131072 | tf_op jit(solution)/shard_map/all_to_all | solution.py:215
  93.1 32.1 %copy-start.1 = (f32[1,32,8192]{2,1,0:T(8,128)S(1)}, f32[1,32,8192]{2,1,0:T(8,128)}, u32[]{:S(2)}) copy-start(f32[1,32,8192]{2,1,0:T(8,128)} %feedback.3) | copy-start | bytes 3145732
  105.3 19.9 %copy-start.3 = (bf16[1,32,8192]{2,1,0:T(8,128)(2,1)S(1)}, bf16[1,32,8192]{2,1,0:T(8,128)(2,1)}, u32[]{:S(2)}) copy-start(bf16[1,32,8192]{2,1,0:T(8,128)(2,1)} %gradient.3) | copy-start | bytes 1572868
  118.3 6.9 %collective-permute-start.2 = (f32[16,72,128]{2,1,0:T(8,128)S(1)}, f32[16,72,128]{2,1,0:T(8,128)S(1)}, u32[]{:S(2)}, u32[]{:S(2)}) collective-permute-start(f32[16,72,128]{2,1,0:T(8,128)S(1)} %all_to_all.27.own), channel_id=1, source_target_pairs={{0,16},{16,0},{32,48},{48,32},{64,80},{80,64},{96,112},{112,96},{1... | collective-permute-start | bytes 1769480 | tf_op jit(solution)/shard_map/ppermute | solution.py:219

commit v4 on v3

--- a/solution.py
+++ b/solution.py
@@ -73,40 +73,47 @@
                 send[chip, rows, :] = jnp.where(first, odd, even)
 
 
-def copy_kernel(parts, out):
-    out[...] = parts[...]
-
-
-def add_kernel(left, right, q_parts, out):
-    out[:, : 2 * ROWS, :] = left[...] + right[...]
-    out[:, 2 * ROWS :, :] = q_parts[...]
+def add_kernel(core_ref, t_ref, left, right, out):
+    for chip in range(CHIPS):
+        out[chip, : 2 * ROWS, :] = left[chip] + right[chip]
+    for th in range(TP // GROUP):
+        rows = slice(th * ROWS, (th + 1) * ROWS)
+        for h in range(2):
+            parts = [out[h * GROUP + k // 2 + k % 2 * (GROUP // 2), rows, :] for k in range(GROUP)]
+            for tl, part in enumerate(swap_blocks(parts)):
+                shard = th * GROUP + tl
+                chip = (shard - t_ref[0] + (2 - core_ref[0]) * (TP // 2)) % TP
+                out[chip, (2 + h) * ROWS : (3 + h) * ROWS, :] = part
 
 
 def pack_q_kernel(core_ref, q_ref, out):
     first = core_ref[0] == 0
-    for c in range(SHARD // LANES):
-        lanes = slice(c * LANES, (c + 1) * LANES)
-        parts = swap_blocks([q_ref[kh * 8 : (kh + 1) * 8, lanes] for kh in range(GROUP)])
-        for pair in range(GROUP // 2):
-            out[c * (GROUP // 2) + pair] = jnp.where(first, parts[2 * pair], parts[2 * pair + 1])
+    even = (lax.broadcasted_iota(jnp.int32, (RANK, LANES), 1) // BLOCK) % 2 == 0
+    for h in range(2):
+        left = q_ref[:, 2 * h * LANES : (2 * h + 1) * LANES]
+        right = q_ref[:, (2 * h + 1) * LANES : (2 * h + 2) * LANES]
+        for_first = jnp.where(even, left, pltpu.roll(right, BLOCK, 1))
+        for_second = jnp.where(even, pltpu.roll(left, LANES - BLOCK, 1), right)
+        out[h] = jnp.where(first, for_first, for_second)
+
+
+def twice_kernel(q_parts, out):
+    out[:, :RANK, :] = q_parts[...]
+    out[:, RANK:, :] = q_parts[...]
 
 
 def unpack_blocks(parts, th):
     return jnp.concatenate(swap_blocks([parts[th * GROUP + tl] for tl in range(GROUP)]), axis=0)
 
 
-def factor_kernel(t_ref, merged, factor_out, sum_out):
-    total = merged[0, : 2 * ROWS, :]
+def factor_kernel(merged, q_twice, factor_out, sum_out):
+    total = merged[0]
     for chip in range(1, CHIPS):
-        total = total + merged[chip, : 2 * ROWS, :]
-    sum_out[...] = total
-    t = t_ref[0]
-    q_parts = [merged[(shard - t + TP) % TP, 2 * ROWS :, :] for shard in range(TP)]
+        total = total + merged[chip]
+    sum_out[...] = total[: 2 * ROWS]
     factor = jnp.zeros((ROWS, LANES), jnp.float32)
-    for th in range(TP // GROUP):
-        q_tile = unpack_blocks(q_parts, th)
-        q_twice = jnp.concatenate([q_tile, q_tile], axis=0)
-        factor = factor + dot(total[th * ROWS : (th + 1) * ROWS], q_twice, 1, 1)
+    for h in range(2):
+        factor = factor + dot(total[(2 + h) * ROWS : (3 + h) * ROWS], q_twice[h], 1, 1)
     lane = lax.broadcasted_iota(jnp.int32, (HALF, LANES), 1)
     packed = jnp.where(lane < RANK, factor[:HALF], factor[HALF:])
     for d in range(DP):
@@ -220,7 +227,11 @@
 
 
 def fetch_shards(parts):
-    pairs = [(d * TP + (t + d // 2) % TP, d * TP + t) for d in range(DP) for t in range(TP)]
+    pairs = [
+        (d * TP + (t + d // 2 + d % 2 * (TP // 2)) % TP, d * TP + t)
+        for d in range(DP)
+        for t in range(TP)
+    ]
     return lax.ppermute(parts, ("dp", "tensor"), pairs)
 
 
@@ -229,15 +240,17 @@
     t = lax.axis_index("tensor").reshape(1)
     chips = [list(range(c, DP, 2)) for c in range(2)]
     whole = (CHIPS, 2 * ROWS, LANES)
-    q_parts = local(pack_q_kernel, (CHIPS, 8, LANES), scalars=1)(core, q_previous)[0]
+    q_parts = local(pack_q_kernel, (2, RANK, LANES), scalars=1)(core, q_previous)[0]
     q_parts = fetch_shards(q_parts)
-    q_parts = local(copy_kernel, (CHIPS, 8, LANES), flops=10_000_000_000)(q_parts)[0]
+    q_parts = local(twice_kernel, (2, 2 * RANK, LANES), flops=10_000_000_000)(q_parts)[0]
     keep, send = local(merge_kernel, whole, whole, scalars=1, inputs=2)(core, gradient, feedback)
-    merged = local(add_kernel, (CHIPS, 2 * ROWS + 8, LANES), inputs=3)(
-        keep, swap_cores(send), q_parts
+    merged = local(add_kernel, (CHIPS, 4 * ROWS, LANES), scalars=2, inputs=2)(
+        core, t, keep, swap_cores(send)
     )[0]
     merged = exchange(merged, "dp", chips)
-    factor, total = local(factor_kernel, (DP, HALF, LANES), (2 * ROWS, LANES), scalars=1)(t, merged)
+    factor, total = local(factor_kernel, (DP, HALF, LANES), (2 * ROWS, LANES), inputs=2)(
+        merged, q_parts
+    )
     factor = exchange(factor, "dp")
     parts = local(project_kernel, (TP, HALF + 8, LANES), inputs=2)(factor, total)[0]
     parts = exchange(parts, "tensor")

time: 129 us -> 125 us (0.969)
  blocking collectives: 51.5 us -> 41.5 us
  waiting for transfers between devices: 19.9 us -> 26.6 us
    all_to_all x3, blocking collectives: 51.5 us -> 41.5 us  [exchange(): lax.all_to_all(parts, axis, 0, 0, tiled=True, axis_index_groups=groups)]
    all_to_all x2, starting transfers between devices: 24.1 us -> 14.2 us  [exchange(): lax.all_to_all(parts, axis, 0, 0, tiled=True, axis_index_groups=groups)]
    ppermute x1, starting transfers between devices: 0.66 us -> 10.1 us  [fetch_shards(): return lax.ppermute(parts, ('dp', 'tensor'), pairs)]
    all_to_all x2, waiting for transfers between devices: 16.8 us -> 25 us  [exchange(): lax.all_to_all(parts, axis, 0, 0, tiled=True, axis_index_groups=groups)]
    ppermute x2, waiting for transfers between devices: 3.1 us -> 1.61 us  [swap_cores(): return lax.ppermute(parts, 'dp', [(d, d ^ 1) for d in range(DP)])]
  transfers between devices with their start and end apart: 5 -> 5, of which waited for: 4 -> 3; matrix products, arithmetic and copies ran while one was open for 0% -> 0% of each run, Pallas kernels for 6% -> 6%
where the time goes in v4:
time: 125 us
  blocking collectives  41.5 us (33%)
  starting transfers between devices  38.3 us (31%)
  waiting for transfers between devices  26.6 us (21%)
  Pallas kernels  15.2 us (12%)
  local copies, waits for them, and re-layouts  2.28 us (2%)
    all_to_all x3, blocking collectives, exchange(): lax.all_to_all(parts, axis, 0, 0, tiled=True, axis_index_groups=groups)  41.5 us
    all_to_all x2, waiting for transfers between devices, exchange(): lax.all_to_all(parts, axis, 0, 0, tiled=True, axis_index_groups=groups)  25 us
    all_to_all x2, starting transfers between devices, exchange(): lax.all_to_all(parts, axis, 0, 0, tiled=True, axis_index_groups=groups)  14.2 us
    ppermute x2, starting transfers between devices, swap_cores(): return lax.ppermute(parts, 'dp', [(d, d ^ 1) for d in range(DP)])  14.1 us
    ppermute x1, starting transfers between devices, fetch_shards(): return lax.ppermute(parts, ('dp', 'tensor'), pairs)  10.1 us
    pallas_call x1, Pallas kernels, on_device(): local(basis_kernel, (RANK, RANK), (ROWS, RANK), scalars=1, scratch=[pltpu...  5.9 us
    pallas_call x1, Pallas kernels, on_device(): local(finish_kernel, feedback.shape, momentum.shape, q_previous.shape, sc...  3.5 us
  transfers between devices with their start and end apart: 5, of which 3 were waited for; matrix products, arithmetic and copies ran while one was open for 0% of the time, Pallas kernels for 6%

profile of v4, /device:TPU:1, one launch (start us, length us, event | category | flops | bytes accessed | tf_op | source)
XLA Modules:
  0.0 124.7 jit_solution(7814651832921556152)
XLA Ops:
  0.6 0.0 copy-start
  0.6 1.2 copy-done
  1.9 1.0 copy-done.2
  2.9 1.6 %shard_map.67 = (f32[16,64,128]{2,1,0:T(8,128)S(1)}, f32[16,64,128]{2,1,0:T(8,128)S(1)}) custom-call(s32[1]{0:T(128)} %bitcast.core_ref, bf16[1,32,8192]{2,1,0:T(8,128)(2,1)S(1)} %copy-done.2, f32[1,32,8192]{2,1,0:T(8,128)S(1)} %copy-done), custom_call_target="tpu_custom_call" | custom-call | flops 100000 | bytes 100000 | tf_op jit(solution)/shard_map/pallas_call | solution.py:246
  4.5 8.8 %collective-permute-start = (f32[16,64,128]{2,1,0:T(8,128)S(1)}, f32[16,64,128]{2,1,0:T(8,128)S(1)}, u32[]{:S(2)}, u32[]{:S(2)}) collective-permute-start(f32[16,64,128]{2,1,0:T(8,128)S(1)} %get-tuple-element.10), channel_id=1, source_target_pairs={{0,16},{16,0},{32,48},{48,32},{64,80},{80,64},{96,112},{112,96},{1... | collective-permute-start | bytes 1572872 | tf_op jit(solution)/shard_map/ppermute | solution.py:226
  13.3 0.0 copy-done.5
  13.3 0.1 shard_map.69
  13.4 10.1 %collective-permute-start.1 = (f32[2,64,128]{2,1,0:T(8,128)S(1)}, f32[2,64,128]{2,1,0:T(8,128)S(1)}, u32[]{:S(2)}, u32[]{:S(2)}) collective-permute-start(f32[2,64,128]{2,1,0:T(8,128)S(1)} %shard_map.69), channel_id=1, source_target_pairs={{0,0},{1,1},{2,2},{3,3},{4,4},{5,5},{6,6},{7,7},{8,8},{9,9},{10,10... | collective-permute-start | bytes 196616 | tf_op jit(solution)/shard_map/ppermute | solution.py:235
  23.5 0.0 collective-permute-done.right
  23.5 1.9 %shard_map.68 = f32[16,128,128]{2,1,0:T(8,128)} custom-call(s32[1]{0:T(128)} %bitcast.core_ref, s32[1]{0:T(128)} %bitcast.1.t_ref, f32[16,64,128]{2,1,0:T(8,128)S(1)} %get-tuple-element.9.left, f32[16,64,128]{2,1,0:T(8,128)S(1)} %collective-permute-done.right), custom_call_target="tpu_custom_call" | custom-call | flops 100000 | bytes 100000 | tf_op jit(solution)/shard_map/pallas_call | solution.py:247
  25.4 5.9 %all-to-all-start = ((f32[16,128,128]{2,1,0:T(8,128)}), f32[16,128,128]{2,1,0:T(8,128)S(1)}, u32[]{:S(2)}, u32[]{:S(2)}) async-start(f32[16,128,128]{2,1,0:T(8,128)} %shard_map.68), calls=%async_computation | async-start | bytes 2097152 | tf_op jit(solution)/shard_map/all_to_all | solution.py:222
  31.3 0.0 collective-permute-done.1.q_parts
  31.3 19.3 %all-to-all-done.merged = f32[16,128,128]{2,1,0:T(8,128)S(1)} async-done(((f32[16,128,128]{2,1,0:T(8,128)}), f32[16,128,128]{2,1,0:T(8,128)S(1)}, u32[]{:S(2)}, u32[]{:S(2)}) %all-to-all-start) | async-done | bytes 1048608 | tf_op jit(solution)/shard_map/all_to_all | solution.py:222
  50.6 0.4 shard_map.71
  51.0 12.0 %all_to_all.25.factors = f32[32,16,128]{2,1,0:T(8,128)S(1)} all-to-all(f32[32,16,128]{2,1,0:T(8,128)S(1)} %get-tuple-element.11), channel_id=1, replica_groups=mesh['dp'=32,'tensor'=16] {'dp'}, dimensions={0} | all-to-all | bytes 524288 | tf_op jit(solution)/shard_map/all_to_all | solution.py:222
  63.0 0.6 shard_map.72
  63.6 0.0 copy-start.4
  63.6 16.5 %all_to_all.26.parts = f32[16,24,128]{2,1,0:T(8,128)S(1)} all-to-all(f32[16,24,128]{2,1,0:T(8,128)S(1)} %shard_map.72), channel_id=1, replica_groups=mesh['dp'=32,'tensor'=16] {'tensor'}, dimensions={0} | all-to-all | bytes 393216 | tf_op jit(solution)/shard_map/all_to_all | solution.py:222
  80.1 0.6 shard_map.74
  80.8 8.3 %all-to-all-start.3 = ((f32[16,8,128]{2,1,0:T(8,128)}), f32[16,8,128]{2,1,0:T(8,128)S(1)}, u32[]{:S(2)}, u32[]{:S(2)}) async-start(f32[16,8,128]{2,1,0:T(8,128)} %shard_map.74), calls=%async_computation.3 | async-start | bytes 131072 | tf_op jit(solution)/shard_map/all_to_all | solution.py:222
  89.1 0.0 copy-start.1
  89.1 5.9 %shard_map.73 = (f32[64,64]{1,0:T(8,128)S(1)}, f32[32,64]{1,0:T(8,128)S(1)}) custom-call(s32[1]{0:T(128)} %bitcast.1.t_ref, f32[16,24,128]{2,1,0:T(8,128)S(1)} %all_to_all.26.parts), custom_call_target="tpu_custom_call" | custom-call | flops 100000 | bytes 100000 | tf_op jit(solution)/shard_map/pallas_call | solution.py:259
  95.0 5.7 %all-to-all-done.3.w_parts = f32[16,8,128]{2,1,0:T(8,128)S(1)} async-done(((f32[16,8,128]{2,1,0:T(8,128)}), f32[16,8,128]{2,1,0:T(8,128)S(1)}, u32[]{:S(2)}, u32[]{:S(2)}) %all-to-all-start.3) | async-done | bytes 65568 | tf_op jit(solution)/shard_map/all_to_all | solution.py:222
  100.6 0.6 shard_map.75
  101.3 0.0 copy-start.3
  101.3 13.0 %all_to_all.27.own = f32[16,72,128]{2,1,0:T(8,128)S(1)} all-to-all(f32[16,72,128]{2,1,0:T(8,128)S(1)} %shard_map.75), channel_id=1, replica_groups={{0,32,64,96,128,160,192,224,256,288,320,352,384,416,448,480},{16,48,80,..., dimensions={0} | all-to-all | bytes 1179648 | tf_op jit(solution)/shard_map/all_to_all | solution.py:222
  114.3 5.3 %collective-permute-start.2 = (f32[16,72,128]{2,1,0:T(8,128)S(1)}, f32[16,72,128]{2,1,0:T(8,128)S(1)}, u32[]{:S(2)}, u32[]{:S(2)}) collective-permute-start(f32[16,72,128]{2,1,0:T(8,128)S(1)} %all_to_all.27.own), channel_id=1, source_target_pairs={{0,16},{16,0},{32,48},{48,32},{64,80},{80,64},{96,112},{112,96},{1... | collective-permute-start | bytes 1769480 | tf_op jit(solution)/shard_map/ppermute | solution.py:226
  119.6 1.6 %collective-permute-done.2.other = f32[16,72,128]{2,1,0:T(8,128)S(1)} collective-permute-done((f32[16,72,128]{2,1,0:T(8,128)S(1)}, f32[16,72,128]{2,1,0:T(8,128)S(1)}, u32[]{:S(2)}, u32[]{:S(2)}) %collective-permute-start.2) | collective-permute-done | bytes 589856 | tf_op jit(solution)/shard_map/ppermute | solution.py:226
  121.2 0.0 copy-done.4
  121.2 0.0 copy-done.1
  121.2 0.0 copy-done.3
  121.2 3.5 %shard_map.76 = (f32[1,32,8192]{2,1,0:T(8,128)}, f32[32,8192]{1,0:T(8,128)}, f32[64,512]{1,0:T(8,128)}) custom-call(s32[1]{0:T(128)} %bitcast.core_ref, bf16[1,32,8192]{2,1,0:T(8,128)(2,1)S(1)} %copy-done.3, f32[1,32,8192]{2,1,0:T(8,128)S(1)} %copy-done.1, f32[32,8192]{1,0:T(8,128)S(1)} %copy-done.4, f32[16,72,128]{2,1,0:T(8,128)S(1)} %all_to_all.27.own, ...), custom_call_target="tpu_custom_call" | custom-call | flops 100000 | bytes 100000 | tf_op jit(solution)/shard_map/pallas_call | solution.py:272
  (3 shorter events, 0.0 us)
Async XLA Ops:
  0.6 1.2 copy-start
  1.9 1.0 copy-start.2
  2.9 10.4 %copy-start.5 = (f32[64,512]{1,0:T(8,128)S(1)}, f32[64,512]{1,0:T(8,128)}, u32[]{:S(2)}) copy-start(f32[64,512]{1,0:T(8,128)} %q_ref.1) | copy-start | bytes 393220
  4.5 19.0 %collective-permute-start = (f32[16,64,128]{2,1,0:T(8,128)S(1)}, f32[16,64,128]{2,1,0:T(8,128)S(1)}, u32[]{:S(2)}, u32[]{:S(2)}) collective-permute-start(f32[16,64,128]{2,1,0:T(8,128)S(1)} %get-tuple-element.10), channel_id=1, source_target_pairs={{0,16},{16,0},{32,48},{48,32},{64,80},{80,64},{96,112},{112,96},{1... | collective-permute-start | bytes 1572872 | tf_op jit(solution)/shard_map/ppermute | solution.py:226
  13.4 17.9 %collective-permute-start.1 = (f32[2,64,128]{2,1,0:T(8,128)S(1)}, f32[2,64,128]{2,1,0:T(8,128)S(1)}, u32[]{:S(2)}, u32[]{:S(2)}) collective-permute-start(f32[2,64,128]{2,1,0:T(8,128)S(1)} %shard_map.69), channel_id=1, source_target_pairs={{0,0},{1,1},{2,2},{3,3},{4,4},{5,5},{6,6},{7,7},{8,8},{9,9},{10,10... | collective-permute-start | bytes 196616 | tf_op jit(solution)/shard_map/ppermute | solution.py:235
  25.4 25.2 %all-to-all-start = ((f32[16,128,128]{2,1,0:T(8,128)}), f32[16,128,128]{2,1,0:T(8,128)S(1)}, u32[]{:S(2)}, u32[]{:S(2)}) async-start(f32[16,128,128]{2,1,0:T(8,128)} %shard_map.68), calls=%async_computation | async-start | bytes 2097152 | tf_op jit(solution)/shard_map/all_to_all | solution.py:222
  63.6 57.6 %copy-start.4 = (f32[32,8192]{1,0:T(8,128)S(1)}, f32[32,8192]{1,0:T(8,128)}, u32[]{:S(2)}) copy-start(f32[32,8192]{1,0:T(8,128)} %momentum.1) | copy-start | bytes 3145732
  80.8 19.9 %all-to-all-start.3 = ((f32[16,8,128]{2,1,0:T(8,128)}), f32[16,8,128]{2,1,0:T(8,128)S(1)}, u32[]{:S(2)}, u32[]{:S(2)}) async-start(f32[16,8,128]{2,1,0:T(8,128)} %shard_map.74), calls=%async_computation.3 | async-start | bytes 131072 | tf_op jit(solution)/shard_map/all_to_all | solution.py:222
  89.1 32.1 %copy-start.1 = (f32[1,32,8192]{2,1,0:T(8,128)S(1)}, f32[1,32,8192]{2,1,0:T(8,128)}, u32[]{:S(2)}) copy-start(f32[1,32,8192]{2,1,0:T(8,128)} %feedback.3) | copy-start | bytes 3145732
  101.3 19.9 %copy-start.3 = (bf16[1,32,8192]{2,1,0:T(8,128)(2,1)S(1)}, bf16[1,32,8192]{2,1,0:T(8,128)(2,1)}, u32[]{:S(2)}) copy-start(bf16[1,32,8192]{2,1,0:T(8,128)(2,1)} %gradient.3) | copy-start | bytes 1572868
  114.3 6.9 %collective-permute-start.2 = (f32[16,72,128]{2,1,0:T(8,128)S(1)}, f32[16,72,128]{2,1,0:T(8,128)S(1)}, u32[]{:S(2)}, u32[]{:S(2)}) collective-permute-start(f32[16,72,128]{2,1,0:T(8,128)S(1)} %all_to_all.27.own), channel_id=1, source_target_pairs={{0,16},{16,0},{32,48},{48,32},{64,80},{80,64},{96,112},{112,96},{1... | collective-permute-start | bytes 1769480 | tf_op jit(solution)/shard_map/ppermute | solution.py:226

commit v5 on v2

v5 whole, which is shorter than its diff:
```python
import jax
import jax.numpy as jnp
from jax import lax
from jax.experimental import pallas as pl
from jax.experimental.pallas import tpu as pltpu
from jax.sharding import PartitionSpec as P

BETA = 0.9
HIGH = lax.Precision.HIGHEST

DP = 32
TP = 16
ROWS = 32
RANK = 64
LANES = 128
BLOCK = 16
GROUP = LANES // BLOCK
SPAN = BLOCK * TP
SHARD = DP * BLOCK
CHIPS = DP // 2
HALF = ROWS // 2


def dot(left, right, left_dim, right_dim):
    return lax.dot_general(
        left,
        right,
        (((left_dim,), (right_dim,)), ((), ())),
        precision=HIGH,
        preferred_element_type=jnp.float32,
    )


def swap_blocks(parts):
    parts = list(parts)
    block = lax.broadcasted_iota(jnp.int32, parts[0].shape, 1) // BLOCK
    for step in (1, 2, 4):
        upper = (block & step) != 0
        for i in range(GROUP):
            if i & step:
                continue
            a, b = parts[i], parts[i | step]
            parts[i] = jnp.where(upper, pltpu.roll(b, step * BLOCK, 1), a)
            parts[i | step] = jnp.where(upper, b, pltpu.roll(a, LANES - step * BLOCK, 1))
    return parts


def merge_kernel(core_ref, t_ref, gradient, feedback, keep, send):
    core, t = core_ref[0], t_ref[0]
    for shard in range(TP):
        for out, half in ((keep, core), (send, 1 - core)):
            lanes = pl.ds(pl.multiple_of(shard * SHARD + half * SPAN, SPAN), SPAN)
            chip = (shard - t + (4 - half) * (TP // 2)) % TP
            out[chip] = gradient[0, :, lanes].astype(jnp.float32) + feedback[0, :, lanes]


def add_kernel(left, right, out):
    out[...] = left[...] + right[...]


def half_kernel(core_ref, q_ref, out):
    out[...] = jnp.where(core_ref[0] == 0, q_ref[:, :SPAN], q_ref[:, SPAN:])


def twice_kernel(q_part, out):
    out[:RANK, :] = q_part[...]
    out[RANK:, :] = q_part[...]


def unpack_blocks(parts, th):
    return jnp.concatenate(swap_blocks([parts[th * GROUP + tl] for tl in range(GROUP)]), axis=0)


def factor_kernel(merged, q_twice, factor_out, sum_out):
    total = merged[0]
    for chip in range(1, CHIPS):
        total = total + merged[chip]
    sum_out[...] = total
    factor = dot(total, q_twice[...], 1, 1)
    lane = lax.broadcasted_iota(jnp.int32, (HALF, LANES), 1)
    packed = jnp.where(lane < RANK, factor[:HALF], factor[HALF:])
    for d in range(DP):
        factor_out[d] = packed


def unpack_rows(packed):
    return jnp.concatenate([packed[:, :RANK], packed[:, RANK:]], axis=0)


def project_kernel(factors, total, out):
    packed = factors[0]
    for d in range(1, DP):
        packed = packed + factors[d]
    rows = unpack_rows(packed)
    for th in range(TP // GROUP):
        term = dot(rows, total[:, th * LANES : (th + 1) * LANES], 0, 0)
        chunks = swap_blocks([term[kh * 8 : (kh + 1) * 8] for kh in range(GROUP)])
        for tl, chunk in enumerate(chunks):
            out[th * GROUP + tl, :HALF, :] = packed
            out[th * GROUP + tl, HALF:, :] = chunk


def chunk_kernel(parts, out, chunk_out):
    total = parts[0, HALF:, :]
    for t in range(1, TP):
        total = total + parts[t, HALF:, :]
    chunk_out[...] = total
    for t in range(TP):
        out[t] = total


def inverse_triangle(gram, rows_ref):
    row = lax.broadcasted_iota(jnp.int32, (RANK, LANES), 0)
    lane = lax.broadcasted_iota(jnp.int32, (RANK, LANES), 1)
    identity = jnp.where(lane == row + RANK, 1.0, 0.0)
    work = jnp.concatenate([gram, jnp.zeros_like(gram)], axis=1) + identity
    for k in range(RANK):
        pivot_row = work[k : k + 1, :]
        pivot = work[k : k + 1, k : k + 1]
        rows_ref[k : k + 1, :] = pivot_row * lax.rsqrt(pivot)
        if k + 1 < RANK:
            scaled = pivot_row * (1.0 / pivot)
            column = work[:, k : k + 1]
            work = work - jnp.where(row > k, column, 0.0) * scaled
    return rows_ref[:, RANK:]


def basis_kernel(t_ref, parts, inverse_out, basis_out, rows_ref):
    flat = parts[:, :HALF, :].reshape(TP * HALF, LANES)
    whole = unpack_rows(flat)
    inverse = inverse_triangle(dot(whole, whole, 0, 0), rows_ref)
    inverse_out[...] = inverse
    own = unpack_rows(parts[t_ref[0], :HALF, :])
    basis_out[...] = dot(own, inverse, 1, 1)


def approx_kernel(inverse, basis, w_parts, chunk, out):
    approx = []
    for th in range(TP // GROUP):
        q_tile = dot(inverse[...], unpack_blocks(w_parts, th), 1, 0) * (1.0 / DP)
        approx.append(dot(basis[...], q_tile, 1, 0))
    message = jnp.concatenate(approx + [chunk[...]], axis=0)
    for chip in range(CHIPS):
        out[chip] = message


def finish_kernel(
    core_ref, gradient, feedback, momentum, inverse, own, other, new_feedback, new_momentum, q_out
):
    first = core_ref[0] == 0
    for half in range(2):
        mine = first if half == 0 else jnp.logical_not(first)
        for shard in range(TP):
            for th in range(TP // GROUP):
                rows = slice(th * ROWS, (th + 1) * ROWS)
                part = jnp.where(mine, own[shard, rows, :], other[shard, rows, :])
                start = shard * SHARD + half * SPAN + th * LANES
                lanes = slice(start, start + LANES)
                merged = gradient[0, :, lanes].astype(jnp.float32) + feedback[0, :, lanes]
                new_feedback[0, :, lanes] = merged - part
                new_momentum[:, lanes] = BETA * momentum[:, lanes] + part
        for th in range(TP // GROUP):
            chunks = [
                jnp.where(mine, own[chip, 2 * ROWS :, :], other[chip, 2 * ROWS :, :])
                for chip in range(th * GROUP, (th + 1) * GROUP)
            ]
            w_tile = jnp.concatenate(swap_blocks(chunks), axis=0)
            start = half * SPAN + th * LANES
            q_out[:, start : start + LANES] = dot(inverse[...], w_tile, 1, 0) * (1.0 / DP)


def local(kernel, *shapes, scalars=0, inputs=1, scratch=(), flops=100_000, moved=100_000):
    return pl.pallas_call(
        kernel,
        out_shape=[jax.ShapeDtypeStruct(shape, jnp.float32) for shape in shapes],
        in_specs=[pl.BlockSpec(memory_space=pltpu.SMEM)] * scalars
        + [pl.BlockSpec(memory_space=pltpu.VMEM)] * inputs,
        out_specs=[pl.BlockSpec(memory_space=pltpu.VMEM)] * len(shapes),
        scratch_shapes=list(scratch),
        cost_estimate=pl.CostEstimate(flops=flops, bytes_accessed=moved, transcendentals=0),
        compiler_params=pltpu.CompilerParams(vmem_limit_bytes=32 * 1024 * 1024),
    )


def exchange(parts, axis, groups=None):
    return lax.all_to_all(parts, axis, 0, 0, tiled=True, axis_index_groups=groups)


def swap_cores(parts):
    return lax.ppermute(parts, "dp", [(d, d ^ 1) for d in range(DP)])


def permute(parts, target):
    pairs = []
    for d in range(DP):
        for t in range(TP):
            chip, plane = target(d // 2, d % 2, t)
            pairs.append((d * TP + t, (chip * 2 + d % 2) * TP + plane))
    return lax.ppermute(parts, ("dp", "tensor"), pairs)


def on_device(gradient, feedback, momentum, q_previous):
    core = (lax.axis_index("dp") & 1).reshape(1)
    t = lax.axis_index("tensor").reshape(1)
    chips = [list(range(c, DP, 2)) for c in range(2)]
    q_part = local(half_kernel, (RANK, SPAN), scalars=1)(core, q_previous)[0]
    q_part = permute(q_part, lambda chip, c, plane: (chip, (plane - chip - c * (TP // 2)) % TP))
    q_part = local(twice_kernel, (2 * RANK, SPAN), flops=10_000_000_000)(q_part)[0]
    whole = (CHIPS, ROWS, SPAN)
    keep, send = local(merge_kernel, whole, whole, scalars=2, inputs=2)(
        core, t, gradient, feedback
    )
    merged = local(add_kernel, whole, inputs=2)(keep, swap_cores(send))[0]
    merged = exchange(merged, "dp", chips)
    factor, total = local(factor_kernel, (DP, HALF, LANES), (ROWS, SPAN), inputs=2)(merged, q_part)
    total = permute(total, lambda chip, c, plane: ((plane + chip + c * (TP // 2)) % TP, plane))
    factor = exchange(factor, "dp")
    parts = local(project_kernel, (TP, HALF + 8, LANES), inputs=2)(factor, total)[0]
    parts = exchange(parts, "tensor")
    w_parts, chunk = local(chunk_kernel, (TP, 8, LANES), (8, LANES))(parts)
    w_parts = exchange(w_parts, "tensor")
    chunk = permute(chunk, lambda chip, c, plane: (plane, chip))
    inverse, basis = local(
        basis_kernel,
        (RANK, RANK),
        (ROWS, RANK),
        scalars=1,
        scratch=[pltpu.VMEM((RANK, LANES), jnp.float32)],
    )(t, parts)
    own = local(approx_kernel, (CHIPS, 2 * ROWS + 8, LANES), inputs=4)(
        inverse, basis, w_parts, chunk
    )[0]
    own = exchange(own, "dp", chips)
    other = swap_cores(own)
    return tuple(
        local(
            finish_kernel, feedback.shape, momentum.shape, q_previous.shape, scalars=1, inputs=6
        )(core, gradient, feedback, momentum, inverse, own, other)
    )


def solution(mesh):
    placed = (
        P("dp", "tensor", None),
        P("dp", "tensor", None),
        P("tensor", None),
        P(None, "tensor"),
    )
    return jax.shard_map(
        on_device,
        mesh=mesh,
        in_specs=placed,
        out_specs=(P("dp", "tensor", None), P("tensor", None), P(None, "tensor")),
        check_vma=False,
    )
```

time: 129 us -> 124 us (0.961)
  blocking collectives: 60.9 us -> 38.1 us
  starting transfers between devices: 32 us -> 48.1 us
  waiting for transfers between devices: 18.8 us -> 22 us
  Pallas kernels: 14.2 us -> 11.9 us
    all_to_all x4 -> x2, blocking collectives: 60.9 us -> 38.1 us  [exchange(): lax.all_to_all(parts, axis, 0, 0, tiled=True, axis_index_groups=groups)]
    ppermute x0 -> x3, starting transfers between devices: none -> 15.7 us  [permute(): return lax.ppermute(parts, ('dp', 'tensor'), pairs)]
    ppermute x0 -> x3, waiting for transfers between devices: none -> 1.67 us  [permute(): return lax.ppermute(parts, ('dp', 'tensor'), pairs)]
    pallas_call x5 -> x6, Pallas kernels: 4.18 us -> 2.54 us  [the longest x1 0.94 us: on_device(): local(factor_kernel, (DP, HALF, LANES), (ROWS, SPAN), inputs=2)]
    all_to_all x2 -> x3, waiting for transfers between devices: 17.2 us -> 18.7 us  [exchange(): lax.all_to_all(parts, axis, 0, 0, tiled=True, axis_index_groups=groups)]
    pallas_call x1, Pallas kernels: 3.5 us -> 2.02 us  [on_device(): local(finish_kernel, feedback.shape, momentum.shape, q_previous.shape, sc...]
    all_to_all x2 -> x3, starting transfers between devices: 17.8 us -> 17.6 us  [exchange(): lax.all_to_all(parts, axis, 0, 0, tiled=True, axis_index_groups=groups)]
  transfers between devices with their start and end apart: 4 -> 8, of which waited for: 3 -> 5; matrix products, arithmetic and copies ran while one was open for 0% -> 0% of each run, Pallas kernels for 5% -> 5%
where the time goes in v5:
time: 124 us; the launch traced here: 123 us
  starting transfers between devices  48.1 us (39%)
  blocking collectives  38.1 us (31%)
  waiting for transfers between devices  22 us (18%)
  Pallas kernels  11.9 us (10%)
  local copies, waits for them, and re-layouts  2.28 us (2%)
    all_to_all x2, blocking collectives, exchange(): lax.all_to_all(parts, axis, 0, 0, tiled=True, axis_index_groups=groups)  38.1 us
    all_to_all x3, waiting for transfers between devices, exchange(): lax.all_to_all(parts, axis, 0, 0, tiled=True, axis_index_groups=groups)  18.7 us
    all_to_all x3, starting transfers between devices, exchange(): lax.all_to_all(parts, axis, 0, 0, tiled=True, axis_index_groups=groups)  17.6 us
    ppermute x3, starting transfers between devices, permute(): return lax.ppermute(parts, ('dp', 'tensor'), pairs)  15.7 us
    ppermute x2, starting transfers between devices, swap_cores(): return lax.ppermute(parts, 'dp', [(d, d ^ 1) for d in range(DP)])  14.7 us
    pallas_call x1, Pallas kernels, on_device(): local(basis_kernel, (RANK, RANK), (ROWS, RANK), scalars=1, scratch=[pltpu...  5.9 us
  transfers between devices with their start and end apart: 8, of which 5 were waited for; matrix products, arithmetic and copies ran while one was open for 0% of the time, Pallas kernels for 5%

profile of v5, /device:TPU:1, one launch (start us, length us, event | category | flops | bytes accessed | tf_op | source)
XLA Modules:
  0.0 123.1 jit_solution(8345768157013636211)
XLA Ops:
  0.6 0.0 copy-start
  0.6 1.2 copy-done
  1.9 1.0 copy-done.2
  2.9 0.3 shard_map.67
  3.2 8.8 %collective-permute-start = (f32[16,32,256]{2,1,0:T(8,128)S(1)}, f32[16,32,256]{2,1,0:T(8,128)S(1)}, u32[]{:S(2)}, u32[]{:S(2)}) collective-permute-start(f32[16,32,256]{2,1,0:T(8,128)S(1)} %get-tuple-element.12), channel_id=1, source_target_pairs={{0,16},{16,0},{32,48},{48,32},{64,80},{80,64},{96,112},{112,96},{1... | collective-permute-start | bytes 1572872 | tf_op jit(solution)/shard_map/ppermute | solution.py:190
  12.0 10.1 %collective-permute-start.1 = (f32[64,256]{1,0:T(8,128)S(1)}, f32[64,256]{1,0:T(8,128)S(1)}, u32[]{:S(2)}, u32[]{:S(2)}) collective-permute-start(f32[64,256]{1,0:T(8,128)S(1)} %shard_map.69), channel_id=1, source_target_pairs={{0,0},{1,1},{2,2},{3,3},{4,4},{5,5},{6,6},{7,7},{8,8},{9,9},{10,10... | collective-permute-start | bytes 196616 | tf_op jit(solution)/shard_map/ppermute | solution.py:199
  22.1 0.0 collective-permute-done.right
  22.1 0.8 shard_map.68
  23.0 5.9 %all-to-all-start = ((f32[16,32,256]{2,1,0:T(8,128)}), f32[16,32,256]{2,1,0:T(8,128)S(1)}, u32[]{:S(2)}, u32[]{:S(2)}) async-start(f32[16,32,256]{2,1,0:T(8,128)} %shard_map.68), calls=%async_computation | async-start | bytes 1048576 | tf_op jit(solution)/shard_map/all_to_all | solution.py:186
  28.8 0.0 collective-permute-done.1.q_part
  28.9 11.4 %all-to-all-done.merged = f32[16,32,256]{2,1,0:T(8,128)S(1)} async-done(((f32[16,32,256]{2,1,0:T(8,128)}), f32[16,32,256]{2,1,0:T(8,128)S(1)}, u32[]{:S(2)}, u32[]{:S(2)}) %all-to-all-start) | async-done | bytes 524320 | tf_op jit(solution)/shard_map/all_to_all | solution.py:186
  40.2 0.9 shard_map.71
  41.2 4.0 %all-to-all-start.1 = ((f32[32,16,128]{2,1,0:T(8,128)}), f32[32,16,128]{2,1,0:T(8,128)S(1)}, u32[]{:S(2)}, u32[]{:S(2)}) async-start(f32[32,16,128]{2,1,0:T(8,128)} %get-tuple-element.13), calls=%async_computation.1 | async-start | bytes 524288 | tf_op jit(solution)/shard_map/all_to_all | solution.py:186
  45.2 4.8 %collective-permute-start.2 = (f32[32,256]{1,0:T(8,128)S(1)}, f32[32,256]{1,0:T(8,128)S(1)}, u32[]{:S(2)}, u32[]{:S(2)}) collective-permute-start(f32[32,256]{1,0:T(8,128)S(1)} %get-tuple-element.14), channel_id=1, source_target_pairs={{0,0},{1,33},{2,66},{3,99},{4,132},{5,165},{6,198},{7,231},{8,264}... | collective-permute-start | bytes 98312 | tf_op jit(solution)/shard_map/ppermute | solution.py:199
  50.0 1.7 %collective-permute-done.2.total = f32[32,256]{1,0:T(8,128)S(1)} collective-permute-done((f32[32,256]{1,0:T(8,128)S(1)}, f32[32,256]{1,0:T(8,128)S(1)}, u32[]{:S(2)}, u32[]{:S(2)}) %collective-permute-start.2) | collective-permute-done | bytes 32800 | tf_op jit(solution)/shard_map/ppermute | solution.py:199
  51.7 2.4 %all-to-all-done.1.factors = f32[32,16,128]{2,1,0:T(8,128)S(1)} async-done(((f32[32,16,128]{2,1,0:T(8,128)}), f32[32,16,128]{2,1,0:T(8,128)S(1)}, u32[]{:S(2)}, u32[]{:S(2)}) %all-to-all-start.1) | async-done | bytes 262176 | tf_op jit(solution)/shard_map/all_to_all | solution.py:186
  54.1 0.6 shard_map.72
  54.7 0.0 copy-start.4
  54.7 17.6 %all_to_all.25.parts = f32[16,24,128]{2,1,0:T(8,128)S(1)} all-to-all(f32[16,24,128]{2,1,0:T(8,128)S(1)} %shard_map.72), channel_id=1, replica_groups=mesh['dp'=32,'tensor'=16] {'tensor'}, dimensions={0} | all-to-all | bytes 393216 | tf_op jit(solution)/shard_map/all_to_all | solution.py:186
  72.3 0.7 shard_map.74
  72.9 7.8 %all-to-all-start.3 = ((f32[16,8,128]{2,1,0:T(8,128)}), f32[16,8,128]{2,1,0:T(8,128)S(1)}, u32[]{:S(2)}, u32[]{:S(2)}) async-start(f32[16,8,128]{2,1,0:T(8,128)} %get-tuple-element.17), calls=%async_computation.3 | async-start | bytes 131072 | tf_op jit(solution)/shard_map/all_to_all | solution.py:186
  80.7 0.0 copy-start.1
  80.7 0.8 collective-permute-start.3
  81.5 5.9 %shard_map.73 = (f32[64,64]{1,0:T(8,128)S(1)}, f32[32,64]{1,0:T(8,128)S(1)}) custom-call(s32[1]{0:T(128)} %bitcast.1.t_ref, f32[16,24,128]{2,1,0:T(8,128)S(1)} %all_to_all.25.parts), custom_call_target="tpu_custom_call" | custom-call | flops 100000 | bytes 100000 | tf_op jit(solution)/shard_map/pallas_call | solution.py:223
  87.4 0.0 collective-permute-done.3.chunk
  87.4 4.9 %all-to-all-done.3.w_parts = f32[16,8,128]{2,1,0:T(8,128)S(1)} async-done(((f32[16,8,128]{2,1,0:T(8,128)}), f32[16,8,128]{2,1,0:T(8,128)S(1)}, u32[]{:S(2)}, u32[]{:S(2)}) %all-to-all-start.3) | async-done | bytes 65568 | tf_op jit(solution)/shard_map/all_to_all | solution.py:186
  92.4 0.6 shard_map.75
  93.0 0.0 copy-start.3
  93.0 20.5 %all_to_all.26.own = f32[16,72,128]{2,1,0:T(8,128)S(1)} all-to-all(f32[16,72,128]{2,1,0:T(8,128)S(1)} %shard_map.75), channel_id=1, replica_groups={{0,32,64,96,128,160,192,224,256,288,320,352,384,416,448,480},{16,48,80,..., dimensions={0} | all-to-all | bytes 1179648 | tf_op jit(solution)/shard_map/all_to_all | solution.py:186
  113.5 5.9 %collective-permute-start.4 = (f32[16,72,128]{2,1,0:T(8,128)S(1)}, f32[16,72,128]{2,1,0:T(8,128)S(1)}, u32[]{:S(2)}, u32[]{:S(2)}) collective-permute-start(f32[16,72,128]{2,1,0:T(8,128)S(1)} %all_to_all.26.own), channel_id=1, source_target_pairs={{0,16},{16,0},{32,48},{48,32},{64,80},{80,64},{96,112},{112,96},{1... | collective-permute-start | bytes 1769480 | tf_op jit(solution)/shard_map/ppermute | solution.py:190
  119.5 1.6 %collective-permute-done.4.other = f32[16,72,128]{2,1,0:T(8,128)S(1)} collective-permute-done((f32[16,72,128]{2,1,0:T(8,128)S(1)}, f32[16,72,128]{2,1,0:T(8,128)S(1)}, u32[]{:S(2)}, u32[]{:S(2)}) %collective-permute-start.4) | collective-permute-done | bytes 589856 | tf_op jit(solution)/shard_map/ppermute | solution.py:190
  121.1 2.0 %shard_map.76 = (f32[1,32,8192]{2,1,0:T(8,128)}, f32[32,8192]{1,0:T(8,128)}, f32[64,512]{1,0:T(8,128)}) custom-call(s32[1]{0:T(128)} %bitcast.core_ref, bf16[1,32,8192]{2,1,0:T(8,128)(2,1)S(1)} %copy-done.3, f32[1,32,8192]{2,1,0:T(8,128)S(1)} %copy-done.1, f32[32,8192]{1,0:T(8,128)S(1)} %copy-done.4, f32[64,64]{1,0:T(8,128)S(1)} %get-tuple-element.15.inverse, ...), custom_call_target="tpu_custom_call" | custom-call | flops 100000 | bytes 100000 | tf_op jit(solution)/shard_map/pallas_call | solution.py:236
  (8 shorter events, 0.0 us)
Async XLA Ops:
  0.6 1.2 copy-start
  1.9 1.0 copy-start.2
  2.9 9.1 %copy-start.5 = (f32[64,512]{1,0:T(8,128)S(1)}, f32[64,512]{1,0:T(8,128)}, u32[]{:S(2)}) copy-start(f32[64,512]{1,0:T(8,128)} %q_ref.1) | copy-start | bytes 393220
  3.2 18.9 %collective-permute-start = (f32[16,32,256]{2,1,0:T(8,128)S(1)}, f32[16,32,256]{2,1,0:T(8,128)S(1)}, u32[]{:S(2)}, u32[]{:S(2)}) collective-permute-start(f32[16,32,256]{2,1,0:T(8,128)S(1)} %get-tuple-element.12), channel_id=1, source_target_pairs={{0,16},{16,0},{32,48},{48,32},{64,80},{80,64},{96,112},{112,96},{1... | collective-permute-start | bytes 1572872 | tf_op jit(solution)/shard_map/ppermute | solution.py:190
  12.0 16.8 %collective-permute-start.1 = (f32[64,256]{1,0:T(8,128)S(1)}, f32[64,256]{1,0:T(8,128)S(1)}, u32[]{:S(2)}, u32[]{:S(2)}) collective-permute-start(f32[64,256]{1,0:T(8,128)S(1)} %shard_map.69), channel_id=1, source_target_pairs={{0,0},{1,1},{2,2},{3,3},{4,4},{5,5},{6,6},{7,7},{8,8},{9,9},{10,10... | collective-permute-start | bytes 196616 | tf_op jit(solution)/shard_map/ppermute | solution.py:199
  23.0 17.3 %all-to-all-start = ((f32[16,32,256]{2,1,0:T(8,128)}), f32[16,32,256]{2,1,0:T(8,128)S(1)}, u32[]{:S(2)}, u32[]{:S(2)}) async-start(f32[16,32,256]{2,1,0:T(8,128)} %shard_map.68), calls=%async_computation | async-start | bytes 1048576 | tf_op jit(solution)/shard_map/all_to_all | solution.py:186
  41.2 12.9 %all-to-all-start.1 = ((f32[32,16,128]{2,1,0:T(8,128)}), f32[32,16,128]{2,1,0:T(8,128)S(1)}, u32[]{:S(2)}, u32[]{:S(2)}) async-start(f32[32,16,128]{2,1,0:T(8,128)} %get-tuple-element.13), calls=%async_computation.1 | async-start | bytes 524288 | tf_op jit(solution)/shard_map/all_to_all | solution.py:186
  45.2 6.5 %collective-permute-start.2 = (f32[32,256]{1,0:T(8,128)S(1)}, f32[32,256]{1,0:T(8,128)S(1)}, u32[]{:S(2)}, u32[]{:S(2)}) collective-permute-start(f32[32,256]{1,0:T(8,128)S(1)} %get-tuple-element.14), channel_id=1, source_target_pairs={{0,0},{1,33},{2,66},{3,99},{4,132},{5,165},{6,198},{7,231},{8,264}... | collective-permute-start | bytes 98312 | tf_op jit(solution)/shard_map/ppermute | solution.py:199
  54.7 66.4 %copy-start.4 = (f32[32,8192]{1,0:T(8,128)S(1)}, f32[32,8192]{1,0:T(8,128)}, u32[]{:S(2)}) copy-start(f32[32,8192]{1,0:T(8,128)} %momentum.1) | copy-start | bytes 3145732
  72.9 19.4 %all-to-all-start.3 = ((f32[16,8,128]{2,1,0:T(8,128)}), f32[16,8,128]{2,1,0:T(8,128)S(1)}, u32[]{:S(2)}, u32[]{:S(2)}) async-start(f32[16,8,128]{2,1,0:T(8,128)} %get-tuple-element.17), calls=%async_computation.3 | async-start | bytes 131072 | tf_op jit(solution)/shard_map/all_to_all | solution.py:186
  80.7 40.4 %copy-start.1 = (f32[1,32,8192]{2,1,0:T(8,128)S(1)}, f32[1,32,8192]{2,1,0:T(8,128)}, u32[]{:S(2)}) copy-start(f32[1,32,8192]{2,1,0:T(8,128)} %feedback.3) | copy-start | bytes 3145732
  80.7 6.7 %collective-permute-start.3 = (f32[8,128]{1,0:T(8,128)S(1)}, f32[8,128]{1,0:T(8,128)S(1)}, u32[]{:S(2)}, u32[]{:S(2)}) collective-permute-start(f32[8,128]{1,0:T(8,128)S(1)} %get-tuple-element.18), channel_id=1, source_target_pairs={{0,0},{1,32},{2,64},{3,96},{4,128},{5,160},{6,192},{7,224},{8,256}... | collective-permute-start | bytes 12296 | tf_op jit(solution)/shard_map/ppermute | solution.py:199
  93.0 28.1 %copy-start.3 = (bf16[1,32,8192]{2,1,0:T(8,128)(2,1)S(1)}, bf16[1,32,8192]{2,1,0:T(8,128)(2,1)}, u32[]{:S(2)}) copy-start(bf16[1,32,8192]{2,1,0:T(8,128)(2,1)} %gradient.3) | copy-start | bytes 1572868
  113.5 7.6 %collective-permute-start.4 = (f32[16,72,128]{2,1,0:T(8,128)S(1)}, f32[16,72,128]{2,1,0:T(8,128)S(1)}, u32[]{:S(2)}, u32[]{:S(2)}) collective-permute-start(f32[16,72,128]{2,1,0:T(8,128)S(1)} %all_to_all.26.own), channel_id=1, source_target_pairs={{0,16},{16,0},{32,48},{48,32},{64,80},{80,64},{96,112},{112,96},{1... | collective-permute-start | bytes 1769480 | tf_op jit(solution)/shard_map/ppermute | solution.py:190

commit v6 on v5

--- a/solution.py
+++ b/solution.py
@@ -71,29 +71,45 @@
     return jnp.concatenate(swap_blocks([parts[th * GROUP + tl] for tl in range(GROUP)]), axis=0)
 
 
-def factor_kernel(merged, q_twice, factor_out, sum_out):
+def factor_kernel(merged, q_twice, out):
     total = merged[0]
     for chip in range(1, CHIPS):
         total = total + merged[chip]
-    sum_out[...] = total
     factor = dot(total, q_twice[...], 1, 1)
     lane = lax.broadcasted_iota(jnp.int32, (HALF, LANES), 1)
     packed = jnp.where(lane < RANK, factor[:HALF], factor[HALF:])
+    pieces = swap_blocks(
+        [
+            total[g * 8 : (g + 1) * 8, h * LANES : (h + 1) * LANES]
+            for h in range(2)
+            for g in range(ROWS // 8)
+        ]
+    )
     for d in range(DP):
-        factor_out[d] = packed
+        out[d, :HALF, :] = packed
+        out[d, HALF:, :] = pieces[d // 2 % GROUP]
 
 
 def unpack_rows(packed):
     return jnp.concatenate([packed[:, :RANK], packed[:, RANK:]], axis=0)
 
 
-def project_kernel(factors, total, out):
-    packed = factors[0]
+def project_kernel(core_ref, chip_ref, t_ref, parts, out):
+    packed = parts[0, :HALF, :]
     for d in range(1, DP):
-        packed = packed + factors[d]
+        packed = packed + parts[d, :HALF, :]
     rows = unpack_rows(packed)
+    low = chip_ref[0] < GROUP
     for th in range(TP // GROUP):
-        term = dot(rows, total[:, th * LANES : (th + 1) * LANES], 0, 0)
+        pieces = []
+        for tl in range(GROUP):
+            source = (th * GROUP + tl - t_ref[0] + (4 - core_ref[0]) * (TP // 2)) % TP
+            pieces.append(parts[source * 2 + core_ref[0], HALF:, :])
+        pieces = swap_blocks(pieces)
+        total = jnp.concatenate(
+            [jnp.where(low, pieces[g], pieces[g + ROWS // 8]) for g in range(ROWS // 8)], axis=0
+        )
+        term = dot(rows, total, 0, 0)
         chunks = swap_blocks([term[kh * 8 : (kh + 1) * 8] for kh in range(GROUP)])
         for tl, chunk in enumerate(chunks):
             out[th * GROUP + tl, :HALF, :] = packed
@@ -150,15 +166,19 @@
     first = core_ref[0] == 0
     for half in range(2):
         mine = first if half == 0 else jnp.logical_not(first)
-        for shard in range(TP):
-            for th in range(TP // GROUP):
-                rows = slice(th * ROWS, (th + 1) * ROWS)
-                part = jnp.where(mine, own[shard, rows, :], other[shard, rows, :])
-                start = shard * SHARD + half * SPAN + th * LANES
-                lanes = slice(start, start + LANES)
-                merged = gradient[0, :, lanes].astype(jnp.float32) + feedback[0, :, lanes]
-                new_feedback[0, :, lanes] = merged - part
-                new_momentum[:, lanes] = BETA * momentum[:, lanes] + part
+        for th in range(TP // GROUP):
+            rows = slice(th * ROWS, (th + 1) * ROWS)
+            for group in range(CHIPS // GROUP):
+                parts = [
+                    jnp.where(mine, own[chip, rows, :], other[chip, rows, :])
+                    for chip in range(group * GROUP, (group + 1) * GROUP)
+                ]
+                for tl, part in enumerate(swap_blocks(parts)):
+                    start = (th * GROUP + tl) * SHARD + half * SPAN + group * LANES
+                    lanes = slice(start, start + LANES)
+                    merged = gradient[0, :, lanes].astype(jnp.float32) + feedback[0, :, lanes]
+                    new_feedback[0, :, lanes] = merged - part
+                    new_momentum[:, lanes] = BETA * momentum[:, lanes] + part
         for th in range(TP // GROUP):
             chunks = [
                 jnp.where(mine, own[chip, 2 * ROWS :, :], other[chip, 2 * ROWS :, :])
@@ -200,26 +220,25 @@
 
 
 def on_device(gradient, feedback, momentum, q_previous):
-    core = (lax.axis_index("dp") & 1).reshape(1)
+    d = lax.axis_index("dp").reshape(1)
+    core, chip = d & 1, d >> 1
     t = lax.axis_index("tensor").reshape(1)
     chips = [list(range(c, DP, 2)) for c in range(2)]
     q_part = local(half_kernel, (RANK, SPAN), scalars=1)(core, q_previous)[0]
     q_part = permute(q_part, lambda chip, c, plane: (chip, (plane - chip - c * (TP // 2)) % TP))
-    q_part = local(twice_kernel, (2 * RANK, SPAN), flops=10_000_000_000)(q_part)[0]
+    q_part = local(twice_kernel, (2 * RANK, SPAN))(q_part)[0]
     whole = (CHIPS, ROWS, SPAN)
     keep, send = local(merge_kernel, whole, whole, scalars=2, inputs=2)(
         core, t, gradient, feedback
     )
     merged = local(add_kernel, whole, inputs=2)(keep, swap_cores(send))[0]
     merged = exchange(merged, "dp", chips)
-    factor, total = local(factor_kernel, (DP, HALF, LANES), (ROWS, SPAN), inputs=2)(merged, q_part)
-    total = permute(total, lambda chip, c, plane: ((plane + chip + c * (TP // 2)) % TP, plane))
+    factor = local(factor_kernel, (DP, HALF + 8, LANES), inputs=2)(merged, q_part)[0]
     factor = exchange(factor, "dp")
-    parts = local(project_kernel, (TP, HALF + 8, LANES), inputs=2)(factor, total)[0]
+    parts = local(project_kernel, (TP, HALF + 8, LANES), scalars=3)(core, chip, t, factor)[0]
     parts = exchange(parts, "tensor")
     w_parts, chunk = local(chunk_kernel, (TP, 8, LANES), (8, LANES))(parts)
     w_parts = exchange(w_parts, "tensor")
-    chunk = permute(chunk, lambda chip, c, plane: (plane, chip))
     inverse, basis = local(
         basis_kernel,
         (RANK, RANK),

time: 124 us -> 125 us (level)
  Pallas kernels: 11.9 us -> 13.4 us
  waiting for transfers between devices: 22 us -> 20.6 us
    all_to_all x3, starting transfers between devices: 17.6 us -> 22 us  [exchange(): lax.all_to_all(parts, axis, 0, 0, tiled=True, axis_index_groups=groups)]
    all_to_all x3, waiting for transfers between devices: 18.7 us -> 15.8 us  [exchange(): lax.all_to_all(parts, axis, 0, 0, tiled=True, axis_index_groups=groups)]
    ppermute x3 -> x1, starting transfers between devices: 15.7 us -> 13.2 us  [permute(): return lax.ppermute(parts, ('dp', 'tensor'), pairs)]
    ppermute x2, waiting for transfers between devices: 1.61 us -> 3.12 us  [swap_cores(): return lax.ppermute(parts, 'dp', [(d, d ^ 1) for d in range(DP)])]
    pallas_call x1, Pallas kernels: 2.02 us -> 3.47 us  [on_device(): local(finish_kernel, feedback.shape, momentum.shape, q_previous.shape, sc...]
  transfers between devices with their start and end apart: 8 -> 6, of which waited for: 5 -> 5; matrix products, arithmetic and copies ran while one was open for 0% -> 0% of each run, Pallas kernels for 5% -> 5%
where the time goes in v6:
time: 125 us; the launch traced here: 124 us
  starting transfers between devices  49.2 us (39%)
  blocking collectives  38 us (30%)
  waiting for transfers between devices  20.6 us (16%)
  Pallas kernels  13.4 us (11%)
  local copies, waits for them, and re-layouts  2.28 us (2%)
    all_to_all x2, blocking collectives, exchange(): lax.all_to_all(parts, axis, 0, 0, tiled=True, axis_index_groups=groups)  38 us
    all_to_all x3, starting transfers between devices, exchange(): lax.all_to_all(parts, axis, 0, 0, tiled=True, axis_index_groups=groups)  22 us
    all_to_all x3, waiting for transfers between devices, exchange(): lax.all_to_all(parts, axis, 0, 0, tiled=True, axis_index_groups=groups)  15.8 us
    ppermute x2, starting transfers between devices, swap_cores(): return lax.ppermute(parts, 'dp', [(d, d ^ 1) for d in range(DP)])  14 us
    ppermute x1, starting transfers between devices, permute(): return lax.ppermute(parts, ('dp', 'tensor'), pairs)  13.2 us
    pallas_call x1, Pallas kernels, on_device(): local(basis_kernel, (RANK, RANK), (ROWS, RANK), scalars=1, scratch=[pltpu...  5.9 us
    pallas_call x1, Pallas kernels, on_device(): local(finish_kernel, feedback.shape, momentum.shape, q_previous.shape, sc...  3.47 us
    ppermute x2, waiting for transfers between devices, swap_cores(): return lax.ppermute(parts, 'dp', [(d, d ^ 1) for d in range(DP)])  3.12 us
  transfers between devices with their start and end apart: 6, of which 5 were waited for; matrix products, arithmetic and copies ran while one was open for 0% of the time, Pallas kernels for 5%

profile of v6, /device:TPU:1, one launch (start us, length us, event | category | flops | bytes accessed | tf_op | source)
XLA Modules:
  0.0 124.4 jit_solution(8985735443530279922)
XLA Ops:
  0.6 0.0 copy-start
  0.6 1.2 copy-done
  1.9 1.0 copy-done.2
  2.9 0.2 shard_map.67
  3.1 8.8 %collective-permute-start = (f32[16,32,256]{2,1,0:T(8,128)S(1)}, f32[16,32,256]{2,1,0:T(8,128)S(1)}, u32[]{:S(2)}, u32[]{:S(2)}) collective-permute-start(f32[16,32,256]{2,1,0:T(8,128)S(1)} %get-tuple-element.10), channel_id=1, source_target_pairs={{0,16},{16,0},{32,48},{48,32},{64,80},{80,64},{96,112},{112,96},{1... | collective-permute-start | bytes 1572872 | tf_op jit(solution)/shard_map/ppermute | solution.py:210
  11.9 1.5 %collective-permute-done.right = f32[16,32,256]{2,1,0:T(8,128)S(1)} collective-permute-done((f32[16,32,256]{2,1,0:T(8,128)S(1)}, f32[16,32,256]{2,1,0:T(8,128)S(1)}, u32[]{:S(2)}, u32[]{:S(2)}) %collective-permute-start) | collective-permute-done | bytes 524320 | tf_op jit(solution)/shard_map/ppermute | solution.py:210
  13.4 0.9 shard_map.68
  14.3 3.7 %all-to-all-start = ((f32[16,32,256]{2,1,0:T(8,128)}), f32[16,32,256]{2,1,0:T(8,128)S(1)}, u32[]{:S(2)}, u32[]{:S(2)}) async-start(f32[16,32,256]{2,1,0:T(8,128)} %shard_map.68), calls=%async_computation | async-start | bytes 1048576 | tf_op jit(solution)/shard_map/all_to_all | solution.py:206
  18.0 0.0 copy-done.5
  18.0 13.2 %collective-permute-start.1 = (f32[64,256]{1,0:T(8,128)S(1)}, f32[64,256]{1,0:T(8,128)S(1)}, u32[]{:S(2)}, u32[]{:S(2)}) collective-permute-start(f32[64,256]{1,0:T(8,128)S(1)} %shard_map.69), channel_id=1, source_target_pairs={{0,0},{1,1},{2,2},{3,3},{4,4},{5,5},{6,6},{7,7},{8,8},{9,9},{10,10... | collective-permute-start | bytes 196616 | tf_op jit(solution)/shard_map/ppermute | solution.py:219
  31.3 1.6 %collective-permute-done.1.q_part = f32[64,256]{1,0:T(8,128)S(1)} collective-permute-done((f32[64,256]{1,0:T(8,128)S(1)}, f32[64,256]{1,0:T(8,128)S(1)}, u32[]{:S(2)}, u32[]{:S(2)}) %collective-permute-start.1) | collective-permute-done | bytes 65568 | tf_op jit(solution)/shard_map/ppermute | solution.py:219
  32.9 0.0 all-to-all-done.merged
  33.0 1.0 shard_map.71
  34.0 9.8 %all-to-all-start.1 = ((f32[32,24,128]{2,1,0:T(8,128)}), f32[32,24,128]{2,1,0:T(8,128)S(1)}, u32[]{:S(2)}, u32[]{:S(2)}) async-start(f32[32,24,128]{2,1,0:T(8,128)} %shard_map.71), calls=%async_computation.1 | async-start | bytes 786432 | tf_op jit(solution)/shard_map/all_to_all | solution.py:206
  43.8 10.2 %all-to-all-done.1.parts = f32[32,24,128]{2,1,0:T(8,128)S(1)} async-done(((f32[32,24,128]{2,1,0:T(8,128)}), f32[32,24,128]{2,1,0:T(8,128)S(1)}, u32[]{:S(2)}, u32[]{:S(2)}) %all-to-all-start.1) | async-done | bytes 393248 | tf_op jit(solution)/shard_map/all_to_all | solution.py:206
  54.0 0.7 shard_map.72
  54.7 0.0 copy-start.4
  54.7 24.7 %all_to_all.25.parts = f32[16,24,128]{2,1,0:T(8,128)S(1)} all-to-all(f32[16,24,128]{2,1,0:T(8,128)S(1)} %shard_map.72), channel_id=1, replica_groups=mesh['dp'=32,'tensor'=16] {'tensor'}, dimensions={0} | all-to-all | bytes 393216 | tf_op jit(solution)/shard_map/all_to_all | solution.py:206
  79.4 0.7 shard_map.74
  80.0 8.5 %all-to-all-start.3 = ((f32[16,8,128]{2,1,0:T(8,128)}), f32[16,8,128]{2,1,0:T(8,128)S(1)}, u32[]{:S(2)}, u32[]{:S(2)}) async-start(f32[16,8,128]{2,1,0:T(8,128)} %get-tuple-element.13), calls=%async_computation.3 | async-start | bytes 131072 | tf_op jit(solution)/shard_map/all_to_all | solution.py:206
  88.5 0.0 copy-start.1
  88.5 5.9 %shard_map.73 = (f32[64,64]{1,0:T(8,128)S(1)}, f32[32,64]{1,0:T(8,128)S(1)}) custom-call(s32[1]{0:T(128)} %bitcast.1.t_ref, f32[16,24,128]{2,1,0:T(8,128)S(1)} %all_to_all.25.parts), custom_call_target="tpu_custom_call" | custom-call | flops 100000 | bytes 100000 | tf_op jit(solution)/shard_map/pallas_call | solution.py:242
  94.4 5.7 %all-to-all-done.3.w_parts = f32[16,8,128]{2,1,0:T(8,128)S(1)} async-done(((f32[16,8,128]{2,1,0:T(8,128)}), f32[16,8,128]{2,1,0:T(8,128)S(1)}, u32[]{:S(2)}, u32[]{:S(2)}) %all-to-all-start.3) | async-done | bytes 65568 | tf_op jit(solution)/shard_map/all_to_all | solution.py:206
  100.1 0.6 shard_map.75
  100.7 0.0 copy-start.3
  100.7 13.3 %all_to_all.26.own = f32[16,72,128]{2,1,0:T(8,128)S(1)} all-to-all(f32[16,72,128]{2,1,0:T(8,128)S(1)} %shard_map.75), channel_id=1, replica_groups={{0,32,64,96,128,160,192,224,256,288,320,352,384,416,448,480},{16,48,80,..., dimensions={0} | all-to-all | bytes 1179648 | tf_op jit(solution)/shard_map/all_to_all | solution.py:206
  114.1 5.2 %collective-permute-start.2 = (f32[16,72,128]{2,1,0:T(8,128)S(1)}, f32[16,72,128]{2,1,0:T(8,128)S(1)}, u32[]{:S(2)}, u32[]{:S(2)}) collective-permute-start(f32[16,72,128]{2,1,0:T(8,128)S(1)} %all_to_all.26.own), channel_id=1, source_target_pairs={{0,16},{16,0},{32,48},{48,32},{64,80},{80,64},{96,112},{112,96},{1... | collective-permute-start | bytes 1769480 | tf_op jit(solution)/shard_map/ppermute | solution.py:210
  119.3 1.6 %collective-permute-done.2.other = f32[16,72,128]{2,1,0:T(8,128)S(1)} collective-permute-done((f32[16,72,128]{2,1,0:T(8,128)S(1)}, f32[16,72,128]{2,1,0:T(8,128)S(1)}, u32[]{:S(2)}, u32[]{:S(2)}) %collective-permute-start.2) | collective-permute-done | bytes 589856 | tf_op jit(solution)/shard_map/ppermute | solution.py:210
  120.9 0.0 copy-done.4
  120.9 0.0 copy-done.1
  120.9 0.0 copy-done.3
  120.9 3.5 %shard_map.76 = (f32[1,32,8192]{2,1,0:T(8,128)}, f32[32,8192]{1,0:T(8,128)}, f32[64,512]{1,0:T(8,128)}) custom-call(s32[1]{0:T(128)} %bitcast.core_ref, bf16[1,32,8192]{2,1,0:T(8,128)(2,1)S(1)} %copy-done.3, f32[1,32,8192]{2,1,0:T(8,128)S(1)} %copy-done.1, f32[32,8192]{1,0:T(8,128)S(1)} %copy-done.4, f32[64,64]{1,0:T(8,128)S(1)} %get-tuple-element.11.inverse, ...), custom_call_target="tpu_custom_call" | custom-call | flops 100000 | bytes 100000 | tf_op jit(solution)/shard_map/pallas_call | solution.py:255
  (4 shorter events, 0.0 us)
Async XLA Ops:
  0.6 1.2 copy-start
  1.9 1.0 copy-start.2
  3.1 10.3 %collective-permute-start = (f32[16,32,256]{2,1,0:T(8,128)S(1)}, f32[16,32,256]{2,1,0:T(8,128)S(1)}, u32[]{:S(2)}, u32[]{:S(2)}) collective-permute-start(f32[16,32,256]{2,1,0:T(8,128)S(1)} %get-tuple-element.10), channel_id=1, source_target_pairs={{0,16},{16,0},{32,48},{48,32},{64,80},{80,64},{96,112},{112,96},{1... | collective-permute-start | bytes 1572872 | tf_op jit(solution)/shard_map/ppermute | solution.py:210
  14.3 3.7 %copy-start.5 = (f32[64,512]{1,0:T(8,128)S(1)}, f32[64,512]{1,0:T(8,128)}, u32[]{:S(2)}) copy-start(f32[64,512]{1,0:T(8,128)} %q_ref.1) | copy-start | bytes 393220
  14.3 18.7 %all-to-all-start = ((f32[16,32,256]{2,1,0:T(8,128)}), f32[16,32,256]{2,1,0:T(8,128)S(1)}, u32[]{:S(2)}, u32[]{:S(2)}) async-start(f32[16,32,256]{2,1,0:T(8,128)} %shard_map.68), calls=%async_computation | async-start | bytes 1048576 | tf_op jit(solution)/shard_map/all_to_all | solution.py:206
  18.0 14.9 %collective-permute-start.1 = (f32[64,256]{1,0:T(8,128)S(1)}, f32[64,256]{1,0:T(8,128)S(1)}, u32[]{:S(2)}, u32[]{:S(2)}) collective-permute-start(f32[64,256]{1,0:T(8,128)S(1)} %shard_map.69), channel_id=1, source_target_pairs={{0,0},{1,1},{2,2},{3,3},{4,4},{5,5},{6,6},{7,7},{8,8},{9,9},{10,10... | collective-permute-start | bytes 196616 | tf_op jit(solution)/shard_map/ppermute | solution.py:219
  34.0 20.0 %all-to-all-start.1 = ((f32[32,24,128]{2,1,0:T(8,128)}), f32[32,24,128]{2,1,0:T(8,128)S(1)}, u32[]{:S(2)}, u32[]{:S(2)}) async-start(f32[32,24,128]{2,1,0:T(8,128)} %shard_map.71), calls=%async_computation.1 | async-start | bytes 786432 | tf_op jit(solution)/shard_map/all_to_all | solution.py:206
  54.7 66.2 %copy-start.4 = (f32[32,8192]{1,0:T(8,128)S(1)}, f32[32,8192]{1,0:T(8,128)}, u32[]{:S(2)}) copy-start(f32[32,8192]{1,0:T(8,128)} %momentum.1) | copy-start | bytes 3145732
  80.0 20.0 %all-to-all-start.3 = ((f32[16,8,128]{2,1,0:T(8,128)}), f32[16,8,128]{2,1,0:T(8,128)S(1)}, u32[]{:S(2)}, u32[]{:S(2)}) async-start(f32[16,8,128]{2,1,0:T(8,128)} %get-tuple-element.13), calls=%async_computation.3 | async-start | bytes 131072 | tf_op jit(solution)/shard_map/all_to_all | solution.py:206
  88.5 32.4 %copy-start.1 = (f32[1,32,8192]{2,1,0:T(8,128)S(1)}, f32[1,32,8192]{2,1,0:T(8,128)}, u32[]{:S(2)}) copy-start(f32[1,32,8192]{2,1,0:T(8,128)} %feedback.3) | copy-start | bytes 3145732
  100.7 20.2 %copy-start.3 = (bf16[1,32,8192]{2,1,0:T(8,128)(2,1)S(1)}, bf16[1,32,8192]{2,1,0:T(8,128)(2,1)}, u32[]{:S(2)}) copy-start(bf16[1,32,8192]{2,1,0:T(8,128)(2,1)} %gradient.3) | copy-start | bytes 1572868
  114.1 6.8 %collective-permute-start.2 = (f32[16,72,128]{2,1,0:T(8,128)S(1)}, f32[16,72,128]{2,1,0:T(8,128)S(1)}, u32[]{:S(2)}, u32[]{:S(2)}) collective-permute-start(f32[16,72,128]{2,1,0:T(8,128)S(1)} %all_to_all.26.own), channel_id=1, source_target_pairs={{0,16},{16,0},{32,48},{48,32},{64,80},{80,64},{96,112},{112,96},{1... | collective-permute-start | bytes 1769480 | tf_op jit(solution)/shard_map/ppermute | solution.py:210

commit v7 on v6

--- a/solution.py
+++ b/solution.py
@@ -1,3 +1,5 @@
+import functools
+
 import jax
 import jax.numpy as jnp
 from jax import lax
@@ -45,17 +47,48 @@
     return parts
 
 
-def merge_kernel(core_ref, t_ref, gradient, feedback, keep, send):
-    core, t = core_ref[0], t_ref[0]
+def columns(shard, half):
+    return pl.ds(pl.multiple_of(shard * SHARD + half * SPAN, SPAN), SPAN)
+
+
+def merge_kernel(half_ref, t_ref, gradient, feedback, out, gradient_part, feedback_part, sems):
+    half, t = half_ref[0], t_ref[0]
+    copies = []
     for shard in range(TP):
-        for out, half in ((keep, core), (send, 1 - core)):
-            lanes = pl.ds(pl.multiple_of(shard * SHARD + half * SPAN, SPAN), SPAN)
-            chip = (shard - t + (4 - half) * (TP // 2)) % TP
-            out[chip] = gradient[0, :, lanes].astype(jnp.float32) + feedback[0, :, lanes]
-
-
-def add_kernel(left, right, out):
-    out[...] = left[...] + right[...]
+        lanes = columns(shard, half)
+        copies.append(
+            [
+                pltpu.make_async_copy(source.at[0, :, lanes], target.at[shard], sems.at[i, shard])
+                for i, (source, target) in enumerate(
+                    ((gradient, gradient_part), (feedback, feedback_part))
+                )
+            ]
+        )
+    for pair in copies:
+        for copy in pair:
+            copy.start()
+    for shard in range(TP):
+        for copy in copies[shard]:
+            copy.wait()
+        chip = (shard - t + (4 - half) * (TP // 2)) % TP
+        out[chip] = gradient_part[shard].astype(jnp.float32) + feedback_part[shard]
+
+
+def add_kernel(left, right, out, left_part, sems):
+    copies = [
+        pltpu.make_async_copy(left.at[chip], left_part.at[chip], sems.at[0, chip])
+        for chip in range(CHIPS)
+    ]
+    for copy in copies:
+        copy.start()
+    results = []
+    for chip in range(CHIPS):
+        copies[chip].wait()
+        left_part[chip] = left_part[chip] + right[chip]
+        results.append(pltpu.make_async_copy(left_part.at[chip], out.at[chip], sems.at[1, chip]))
+        results[chip].start()
+    for copy in results:
+        copy.wait()
 
 
 def half_kernel(core_ref, q_ref, out):
@@ -160,45 +193,66 @@
         out[chip] = message
 
 
-def finish_kernel(
-    core_ref, gradient, feedback, momentum, inverse, own, other, new_feedback, new_momentum, q_out
-):
-    first = core_ref[0] == 0
-    for half in range(2):
-        mine = first if half == 0 else jnp.logical_not(first)
-        for th in range(TP // GROUP):
-            rows = slice(th * ROWS, (th + 1) * ROWS)
-            for group in range(CHIPS // GROUP):
-                parts = [
-                    jnp.where(mine, own[chip, rows, :], other[chip, rows, :])
-                    for chip in range(group * GROUP, (group + 1) * GROUP)
-                ]
-                for tl, part in enumerate(swap_blocks(parts)):
-                    start = (th * GROUP + tl) * SHARD + half * SPAN + group * LANES
-                    lanes = slice(start, start + LANES)
-                    merged = gradient[0, :, lanes].astype(jnp.float32) + feedback[0, :, lanes]
-                    new_feedback[0, :, lanes] = merged - part
-                    new_momentum[:, lanes] = BETA * momentum[:, lanes] + part
-        for th in range(TP // GROUP):
-            chunks = [
-                jnp.where(mine, own[chip, 2 * ROWS :, :], other[chip, 2 * ROWS :, :])
-                for chip in range(th * GROUP, (th + 1) * GROUP)
+def finish_half(half_ref, gradient, feedback, momentum, inverse, parts, outs, scratch, sems):
+    half = half_ref[0]
+    new_feedback, new_momentum, q_out = outs
+    feedback_part, momentum_part, q_part = scratch
+    copies = []
+    for th in range(TP // GROUP):
+        rows = slice(th * ROWS, (th + 1) * ROWS)
+        for group in range(CHIPS // GROUP):
+            chips = range(group * GROUP, (group + 1) * GROUP)
+            place = slice(group * LANES, (group + 1) * LANES)
+            for tl, part in enumerate(swap_blocks([parts[chip, rows, :] for chip in chips])):
+                shard = th * GROUP + tl
+                start = shard * SHARD + half * SPAN + group * LANES
+                lanes = pl.ds(pl.multiple_of(start, LANES), LANES)
+                merged = gradient[0, :, lanes].astype(jnp.float32) + feedback[0, :, lanes]
+                feedback_part[shard, :, place] = merged - part
+                momentum_part[shard, :, place] = BETA * momentum[:, lanes] + part
+        for shard in range(th * GROUP, (th + 1) * GROUP):
+            lanes = columns(shard, half)
+            copies += [
+                pltpu.make_async_copy(
+                    feedback_part.at[shard], new_feedback.at[0, :, lanes], sems.at[0, shard]
+                ),
+                pltpu.make_async_copy(
+                    momentum_part.at[shard], new_momentum.at[:, lanes], sems.at[1, shard]
+                ),
             ]
-            w_tile = jnp.concatenate(swap_blocks(chunks), axis=0)
-            start = half * SPAN + th * LANES
-            q_out[:, start : start + LANES] = dot(inverse[...], w_tile, 1, 0) * (1.0 / DP)
-
-
-def local(kernel, *shapes, scalars=0, inputs=1, scratch=(), flops=100_000, moved=100_000):
+            copies[-2].start()
+            copies[-1].start()
+    for group in range(CHIPS // GROUP):
+        chips = range(group * GROUP, (group + 1) * GROUP)
+        w_tile = jnp.concatenate(swap_blocks([parts[chip, 2 * ROWS :, :] for chip in chips]), axis=0)
+        place = slice(group * LANES, (group + 1) * LANES)
+        q_part[:, place] = dot(inverse[...], w_tile, 1, 0) * (1.0 / DP)
+    copies.append(pltpu.make_async_copy(q_part, q_out.at[:, columns(0, half)], sems.at[2, 0]))
+    copies[-1].start()
+    for copy in copies:
+        copy.wait()
+
+
+def finish_own_kernel(half_ref, gradient, feedback, momentum, inverse, parts, *refs):
+    finish_half(half_ref, gradient, feedback, momentum, inverse, parts, refs[:3], refs[3:6], refs[6])
+
+
+def finish_other_kernel(half_ref, gradient, feedback, momentum, inverse, parts, *refs):
+    finish_half(half_ref, gradient, feedback, momentum, inverse, parts, refs[3:6], refs[6:9], refs[9])
+
+
+def local(kernel, *shapes, scalars=0, inputs=1, scratch=(), flops=100_000, far=(), far_out=False, alias=None, room=32):
+    vmem, anywhere = pl.BlockSpec(memory_space=pltpu.VMEM), pl.BlockSpec(memory_space=pltpu.HBM)
     return pl.pallas_call(
         kernel,
         out_shape=[jax.ShapeDtypeStruct(shape, jnp.float32) for shape in shapes],
         in_specs=[pl.BlockSpec(memory_space=pltpu.SMEM)] * scalars
-        + [pl.BlockSpec(memory_space=pltpu.VMEM)] * inputs,
-        out_specs=[pl.BlockSpec(memory_space=pltpu.VMEM)] * len(shapes),
+        + [anywhere if i in far else vmem for i in range(inputs)],
+        out_specs=[anywhere if far_out else vmem] * len(shapes),
         scratch_shapes=list(scratch),
-        cost_estimate=pl.CostEstimate(flops=flops, bytes_accessed=moved, transcendentals=0),
-        compiler_params=pltpu.CompilerParams(vmem_limit_bytes=32 * 1024 * 1024),
+        input_output_aliases=alias or {},
+        cost_estimate=pl.CostEstimate(flops=flops, bytes_accessed=100_000, transcendentals=0),
+        compiler_params=pltpu.CompilerParams(vmem_limit_bytes=room * 1024 * 1024),
     )
 
 
@@ -226,12 +280,32 @@
     chips = [list(range(c, DP, 2)) for c in range(2)]
     q_part = local(half_kernel, (RANK, SPAN), scalars=1)(core, q_previous)[0]
     q_part = permute(q_part, lambda chip, c, plane: (chip, (plane - chip - c * (TP // 2)) % TP))
-    q_part = local(twice_kernel, (2 * RANK, SPAN))(q_part)[0]
+    q_part = local(twice_kernel, (2 * RANK, SPAN), flops=10_000_000_000)(q_part)[0]
     whole = (CHIPS, ROWS, SPAN)
-    keep, send = local(merge_kernel, whole, whole, scalars=2, inputs=2)(
-        core, t, gradient, feedback
-    )
-    merged = local(add_kernel, whole, inputs=2)(keep, swap_cores(send))[0]
+    merge = functools.partial(
+        local,
+        merge_kernel,
+        whole,
+        scalars=2,
+        inputs=2,
+        far=(0, 1),
+        scratch=[
+            pltpu.VMEM((TP, ROWS, SPAN), jnp.bfloat16),
+            pltpu.VMEM((TP, ROWS, SPAN), jnp.float32),
+            pltpu.SemaphoreType.DMA((2, TP)),
+        ],
+    )
+    send = merge(room=60)(1 - core, t, gradient, feedback)[0]
+    keep = merge(room=32)(core, t, gradient, feedback)[0]
+    merged = local(
+        add_kernel,
+        whole,
+        inputs=2,
+        far=(0,),
+        far_out=True,
+        room=32,
+        scratch=[pltpu.VMEM(whole, jnp.float32), pltpu.SemaphoreType.DMA((2, CHIPS))],
+    )(keep, swap_cores(send))[0]
     merged = exchange(merged, "dp", chips)
     factor = local(factor_kernel, (DP, HALF + 8, LANES), inputs=2)(merged, q_part)[0]
     factor = exchange(factor, "dp")
@@ -251,11 +325,27 @@
     )[0]
     own = exchange(own, "dp", chips)
     other = swap_cores(own)
-    return tuple(
-        local(
-            finish_kernel, feedback.shape, momentum.shape, q_previous.shape, scalars=1, inputs=6
-        )(core, gradient, feedback, momentum, inverse, own, other)
-    )
+    shapes = (feedback.shape, momentum.shape, q_previous.shape)
+    scratch = [
+        pltpu.VMEM((TP, ROWS, SPAN), jnp.float32),
+        pltpu.VMEM((TP, ROWS, SPAN), jnp.float32),
+        pltpu.VMEM((RANK, SPAN), jnp.float32),
+        pltpu.SemaphoreType.DMA((3, TP)),
+    ]
+    outs = local(
+        finish_own_kernel, *shapes, scalars=1, inputs=5, scratch=scratch, far_out=True
+    )(core, gradient, feedback, momentum, inverse, own)
+    outs = local(
+        finish_other_kernel,
+        *shapes,
+        scalars=1,
+        inputs=8,
+        scratch=scratch,
+        far=(5, 6, 7),
+        far_out=True,
+        alias={6: 0, 7: 1, 8: 2},
+    )(1 - core, gradient, feedback, momentum, inverse, other, *outs)
+    return tuple(outs)
 
 
 def solution(mesh):

time: 125 us -> 120 us (0.960)
  blocking collectives: 38 us -> 31 us
  starting transfers between devices: 49.2 us -> 42.4 us
  waiting for transfers between devices: 20.6 us -> 27.2 us
  Pallas kernels: 13.4 us -> 18 us
  local copies, waits for them, and re-layouts: 2.28 us -> 0.02 us
    all_to_all x3, waiting for transfers between devices: 15.8 us -> 27.2 us  [exchange(): lax.all_to_all(parts, axis, 0, 0, tiled=True, axis_index_groups=groups)]
    all_to_all x2, blocking collectives: 38 us -> 31 us  [exchange(): lax.all_to_all(parts, axis, 0, 0, tiled=True, axis_index_groups=groups)]
    pallas_call x4 -> x6, Pallas kernels: 4.55 us -> 9.09 us  [the longest x1 2.3 us: on_device(): send = merge(room=60)(1 - core, t, gradient, feedback)[0]]
    all_to_all x3, starting transfers between devices: 22 us -> 18.3 us  [exchange(): lax.all_to_all(parts, axis, 0, 0, tiled=True, axis_index_groups=groups)]
    ppermute x1, starting transfers between devices: 13.2 us -> 10.1 us  [permute(): return lax.ppermute(parts, ('dp', 'tensor'), pairs)]
    ppermute x2, waiting for transfers between devices: 3.12 us -> 0.01 us  [swap_cores(): return lax.ppermute(parts, 'dp', [(d, d ^ 1) for d in range(DP)])]
    unnamed x12 -> x8, local copies, waits for them, and re-layouts: 2.28 us -> 0.02 us
    ppermute x1, waiting for transfers between devices: 1.64 us -> 0.01 us  [permute(): return lax.ppermute(parts, ('dp', 'tensor'), pairs)]
  transfers between devices with their start and end apart: 6 -> 6, of which waited for: 5 -> 3; matrix products, arithmetic and copies ran while one was open for 0% -> 0% of each run, Pallas kernels for 5% -> 9%
where the time goes in v7:
time: 120 us; the launch traced here: 119 us
  starting transfers between devices  42.4 us (35%)
  blocking collectives  31 us (26%)
  waiting for transfers between devices  27.2 us (23%)
  Pallas kernels  18 us (15%)
    all_to_all x2, blocking collectives, exchange(): lax.all_to_all(parts, axis, 0, 0, tiled=True, axis_index_groups=groups)  31 us
    all_to_all x3, waiting for transfers between devices, exchange(): lax.all_to_all(parts, axis, 0, 0, tiled=True, axis_index_groups=groups)  27.2 us
    all_to_all x3, starting transfers between devices, exchange(): lax.all_to_all(parts, axis, 0, 0, tiled=True, axis_index_groups=groups)  18.3 us
    ppermute x2, starting transfers between devices, swap_cores(): return lax.ppermute(parts, 'dp', [(d, d ^ 1) for d in range(DP)])  14 us
    ppermute x1, starting transfers between devices, permute(): return lax.ppermute(parts, ('dp', 'tensor'), pairs)  10.1 us
    pallas_call x1, Pallas kernels, on_device(): local(basis_kernel, (RANK, RANK), (ROWS, RANK), scalars=1, scratch=[pltpu...  5.9 us
  transfers between devices with their start and end apart: 6, of which 3 were waited for; matrix products, arithmetic and copies ran while one was open for 0% of the time, Pallas kernels for 9%

profile of v7, /device:TPU:1, one launch (start us, length us, event | category | flops | bytes accessed | tf_op | source)
XLA Modules:
  0.0 119.4 jit_solution(7326063886297685510)
XLA Ops:
  0.6 0.0 copy-start.3
  0.6 0.0 copy-start
  0.7 0.0 copy-start.1
  0.7 2.3 %shard_map.68 = f32[16,32,256]{2,1,0:T(8,128)} custom-call(s32[1]{0:T(128)S(6)} %sub.4.half_ref, s32[1]{0:T(128)} %bitcast.1.t_ref, bf16[1,32,8192]{2,1,0:T(8,128)(2,1)} %gradient.7, f32[1,32,8192]{2,1,0:T(8,128)} %feedback.7), custom_call_target="tpu_custom_call" | custom-call | flops 100000 | bytes 100000 | tf_op jit(solution)/shard_map/pallas_call | solution.py:298
  3.0 8.8 %collective-permute-start = (f32[16,32,256]{2,1,0:T(8,128)}, f32[16,32,256]{2,1,0:T(8,128)S(1)}, u32[]{:S(2)}, u32[]{:S(2)}) collective-permute-start(f32[16,32,256]{2,1,0:T(8,128)} %shard_map.68), channel_id=1, source_target_pairs={{0,16},{16,0},{32,48},{48,32},{64,80},{80,64},{96,112},{112,96},{1... | collective-permute-start | bytes 1572872 | tf_op jit(solution)/shard_map/ppermute | solution.py:264
  11.8 0.0 copy-done.3
  11.8 10.1 %collective-permute-start.1 = (f32[64,256]{1,0:T(8,128)S(1)}, f32[64,256]{1,0:T(8,128)S(1)}, u32[]{:S(2)}, u32[]{:S(2)}) collective-permute-start(f32[64,256]{1,0:T(8,128)S(1)} %shard_map.70), channel_id=1, source_target_pairs={{0,0},{1,1},{2,2},{3,3},{4,4},{5,5},{6,6},{7,7},{8,8},{9,9},{10,10... | collective-permute-start | bytes 196616 | tf_op jit(solution)/shard_map/ppermute | solution.py:273
  21.9 0.0 copy-done
  21.9 0.0 copy-done.1
  21.9 0.7 shard_map.67.left
  22.6 0.0 collective-permute-done.right
  22.6 1.7 %shard_map.69 = f32[16,32,256]{2,1,0:T(8,128)} custom-call(f32[16,32,256]{2,1,0:T(8,128)S(1)} %shard_map.67.left, f32[16,32,256]{2,1,0:T(8,128)S(1)} %collective-permute-done.right), custom_call_target="tpu_custom_call" | custom-call | flops 100000 | bytes 100000 | tf_op jit(solution)/shard_map/pallas_call | solution.py:300
  24.4 5.9 %all-to-all-start = ((f32[16,32,256]{2,1,0:T(8,128)}), f32[16,32,256]{2,1,0:T(8,128)S(1)}, u32[]{:S(2)}, u32[]{:S(2)}) async-start(f32[16,32,256]{2,1,0:T(8,128)} %shard_map.69), calls=%async_computation | async-start | bytes 1048576 | tf_op jit(solution)/shard_map/all_to_all | solution.py:260
  30.3 0.0 collective-permute-done.1.q_part
  30.3 11.4 %all-to-all-done.merged = f32[16,32,256]{2,1,0:T(8,128)S(1)} async-done(((f32[16,32,256]{2,1,0:T(8,128)}), f32[16,32,256]{2,1,0:T(8,128)S(1)}, u32[]{:S(2)}, u32[]{:S(2)}) %all-to-all-start) | async-done | bytes 524320 | tf_op jit(solution)/shard_map/all_to_all | solution.py:260
  41.7 1.0 shard_map.72
  42.7 4.0 %all-to-all-start.1 = ((f32[32,24,128]{2,1,0:T(8,128)}), f32[32,24,128]{2,1,0:T(8,128)S(1)}, u32[]{:S(2)}, u32[]{:S(2)}) async-start(f32[32,24,128]{2,1,0:T(8,128)} %shard_map.72), calls=%async_computation.1 | async-start | bytes 786432 | tf_op jit(solution)/shard_map/all_to_all | solution.py:260
  46.7 10.2 %all-to-all-done.1.parts = f32[32,24,128]{2,1,0:T(8,128)S(1)} async-done(((f32[32,24,128]{2,1,0:T(8,128)}), f32[32,24,128]{2,1,0:T(8,128)S(1)}, u32[]{:S(2)}, u32[]{:S(2)}) %all-to-all-start.1) | async-done | bytes 393248 | tf_op jit(solution)/shard_map/all_to_all | solution.py:260
  56.9 0.7 shard_map.73
  57.6 17.8 %all_to_all.25.parts = f32[16,24,128]{2,1,0:T(8,128)S(1)} all-to-all(f32[16,24,128]{2,1,0:T(8,128)S(1)} %shard_map.73), channel_id=1, replica_groups=mesh['dp'=32,'tensor'=16] {'tensor'}, dimensions={0} | all-to-all | bytes 393216 | tf_op jit(solution)/shard_map/all_to_all | solution.py:260
  75.4 0.7 shard_map.75
  76.1 8.4 %all-to-all-start.3 = ((f32[16,8,128]{2,1,0:T(8,128)}), f32[16,8,128]{2,1,0:T(8,128)S(1)}, u32[]{:S(2)}, u32[]{:S(2)}) async-start(f32[16,8,128]{2,1,0:T(8,128)} %get-tuple-element.12), calls=%async_computation.3 | async-start | bytes 131072 | tf_op jit(solution)/shard_map/all_to_all | solution.py:260
  84.5 0.0 copy-start.2
  84.5 5.9 %shard_map.74 = (f32[64,64]{1,0:T(8,128)S(1)}, f32[32,64]{1,0:T(8,128)S(1)}) custom-call(s32[1]{0:T(128)} %bitcast.1.t_ref, f32[16,24,128]{2,1,0:T(8,128)S(1)} %all_to_all.25.parts), custom_call_target="tpu_custom_call" | custom-call | flops 100000 | bytes 100000 | tf_op jit(solution)/shard_map/pallas_call | solution.py:316
  90.4 5.7 %all-to-all-done.3.w_parts = f32[16,8,128]{2,1,0:T(8,128)S(1)} async-done(((f32[16,8,128]{2,1,0:T(8,128)}), f32[16,8,128]{2,1,0:T(8,128)S(1)}, u32[]{:S(2)}, u32[]{:S(2)}) %all-to-all-start.3) | async-done | bytes 65568 | tf_op jit(solution)/shard_map/all_to_all | solution.py:260
  96.1 0.6 shard_map.76
  96.7 13.2 %all_to_all.26.parts = f32[16,72,128]{2,1,0:T(8,128)S(1)} all-to-all(f32[16,72,128]{2,1,0:T(8,128)S(1)} %shard_map.76), channel_id=1, replica_groups={{0,32,64,96,128,160,192,224,256,288,320,352,384,416,448,480},{16,48,80,..., dimensions={0} | all-to-all | bytes 1179648 | tf_op jit(solution)/shard_map/all_to_all | solution.py:260
  109.9 5.2 %collective-permute-start.2 = (f32[16,72,128]{2,1,0:T(8,128)S(1)}, f32[16,72,128]{2,1,0:T(8,128)S(1)}, u32[]{:S(2)}, u32[]{:S(2)}) collective-permute-start(f32[16,72,128]{2,1,0:T(8,128)S(1)} %all_to_all.26.parts), channel_id=1, source_target_pairs={{0,16},{16,0},{32,48},{48,32},{64,80},{80,64},{96,112},{112,96},{1... | collective-permute-start | bytes 1769480 | tf_op jit(solution)/shard_map/ppermute | solution.py:264
  115.1 0.0 copy-done.2
  115.1 2.2 %shard_map.77 = (f32[1,32,8192]{2,1,0:T(8,128)}, f32[32,8192]{1,0:T(8,128)}, f32[64,512]{1,0:T(8,128)}) custom-call(s32[1]{0:T(128)} %bitcast.half_ref.core_ref, bf16[1,32,8192]{2,1,0:T(8,128)(2,1)S(1)} %copy-done.1, f32[1,32,8192]{2,1,0:T(8,128)S(1)} %copy-done, f32[32,8192]{1,0:T(8,128)S(1)} %copy-done.2, f32[64,64]{1,0:T(8,128)S(1)} %get-tuple-element.10.inverse, ...), custom_call_target="tpu_custom_call" | custom-call | flops 100000 | bytes 100000 | tf_op jit(solution)/shard_map/pallas_call | solution.py:335
  117.3 0.0 collective-permute-done.2.parts
  117.3 2.2 %shard_map.78 = (f32[1,32,8192]{2,1,0:T(8,128)}, f32[32,8192]{1,0:T(8,128)}, f32[64,512]{1,0:T(8,128)}) custom-call(s32[1]{0:T(128)S(6)} %sub.4.half_ref, bf16[1,32,8192]{2,1,0:T(8,128)(2,1)S(1)} %copy-done.1, f32[1,32,8192]{2,1,0:T(8,128)S(1)} %copy-done, f32[32,8192]{1,0:T(8,128)S(1)} %copy-done.2, ...), custom_call_target="tpu_custom_call", output_to_operand_aliasing={{0}: (6, {}), {1}: (7, {}), {2}: (8, {})} | custom-call | flops 100000 | bytes 100000 | tf_op jit(solution)/shard_map/pallas_call | solution.py:338
  (2 shorter events, 0.0 us)
Async XLA Ops:
  0.6 11.1 %copy-start.3 = (f32[64,512]{1,0:T(8,128)S(1)}, f32[64,512]{1,0:T(8,128)}, u32[]{:S(2)}) copy-start(f32[64,512]{1,0:T(8,128)} %q_ref.1) | copy-start | bytes 393220
  0.6 21.2 %copy-start = (f32[1,32,8192]{2,1,0:T(8,128)S(1)}, f32[1,32,8192]{2,1,0:T(8,128)}, u32[]{:S(2)}) copy-start(f32[1,32,8192]{2,1,0:T(8,128)} %feedback.7) | copy-start | bytes 3145732
  0.7 21.2 %copy-start.1 = (bf16[1,32,8192]{2,1,0:T(8,128)(2,1)S(1)}, bf16[1,32,8192]{2,1,0:T(8,128)(2,1)}, u32[]{:S(2)}) copy-start(bf16[1,32,8192]{2,1,0:T(8,128)(2,1)} %gradient.7) | copy-start | bytes 1572868
  3.0 19.7 %collective-permute-start = (f32[16,32,256]{2,1,0:T(8,128)}, f32[16,32,256]{2,1,0:T(8,128)S(1)}, u32[]{:S(2)}, u32[]{:S(2)}) collective-permute-start(f32[16,32,256]{2,1,0:T(8,128)} %shard_map.68), channel_id=1, source_target_pairs={{0,16},{16,0},{32,48},{48,32},{64,80},{80,64},{96,112},{112,96},{1... | collective-permute-start | bytes 1572872 | tf_op jit(solution)/shard_map/ppermute | solution.py:264
  11.8 18.5 %collective-permute-start.1 = (f32[64,256]{1,0:T(8,128)S(1)}, f32[64,256]{1,0:T(8,128)S(1)}, u32[]{:S(2)}, u32[]{:S(2)}) collective-permute-start(f32[64,256]{1,0:T(8,128)S(1)} %shard_map.70), channel_id=1, source_target_pairs={{0,0},{1,1},{2,2},{3,3},{4,4},{5,5},{6,6},{7,7},{8,8},{9,9},{10,10... | collective-permute-start | bytes 196616 | tf_op jit(solution)/shard_map/ppermute | solution.py:273
  24.4 17.3 %all-to-all-start = ((f32[16,32,256]{2,1,0:T(8,128)}), f32[16,32,256]{2,1,0:T(8,128)S(1)}, u32[]{:S(2)}, u32[]{:S(2)}) async-start(f32[16,32,256]{2,1,0:T(8,128)} %shard_map.69), calls=%async_computation | async-start | bytes 1048576 | tf_op jit(solution)/shard_map/all_to_all | solution.py:260
  42.7 14.2 %all-to-all-start.1 = ((f32[32,24,128]{2,1,0:T(8,128)}), f32[32,24,128]{2,1,0:T(8,128)S(1)}, u32[]{:S(2)}, u32[]{:S(2)}) async-start(f32[32,24,128]{2,1,0:T(8,128)} %shard_map.72), calls=%async_computation.1 | async-start | bytes 786432 | tf_op jit(solution)/shard_map/all_to_all | solution.py:260
  76.1 20.0 %all-to-all-start.3 = ((f32[16,8,128]{2,1,0:T(8,128)}), f32[16,8,128]{2,1,0:T(8,128)S(1)}, u32[]{:S(2)}, u32[]{:S(2)}) async-start(f32[16,8,128]{2,1,0:T(8,128)} %get-tuple-element.12), calls=%async_computation.3 | async-start | bytes 131072 | tf_op jit(solution)/shard_map/all_to_all | solution.py:260
  84.5 30.6 %copy-start.2 = (f32[32,8192]{1,0:T(8,128)S(1)}, f32[32,8192]{1,0:T(8,128)}, u32[]{:S(2)}) copy-start(f32[32,8192]{1,0:T(8,128)} %momentum.3) | copy-start | bytes 3145732
  109.9 7.4 %collective-permute-start.2 = (f32[16,72,128]{2,1,0:T(8,128)S(1)}, f32[16,72,128]{2,1,0:T(8,128)S(1)}, u32[]{:S(2)}, u32[]{:S(2)}) collective-permute-start(f32[16,72,128]{2,1,0:T(8,128)S(1)} %all_to_all.26.parts), channel_id=1, source_target_pairs={{0,16},{16,0},{32,48},{48,32},{64,80},{80,64},{96,112},{112,96},{1... | collective-permute-start | bytes 1769480 | tf_op jit(solution)/shard_map/ppermute | solution.py:264

commit v8 on v7

--- a/solution.py
+++ b/solution.py
@@ -18,6 +18,7 @@
 BLOCK = 16
 GROUP = LANES // BLOCK
 SPAN = BLOCK * TP
+CHUNKS = 4
 SHARD = DP * BLOCK
 CHIPS = DP // 2
 HALF = ROWS // 2
@@ -51,42 +52,37 @@
     return pl.ds(pl.multiple_of(shard * SHARD + half * SPAN, SPAN), SPAN)
 
 
-def merge_kernel(half_ref, t_ref, gradient, feedback, out, gradient_part, feedback_part, sems):
-    half, t = half_ref[0], t_ref[0]
+def merge_kernel(t_ref, gradient, feedback, out, gradient_part, feedback_part, merged, sems):
+    t = t_ref[0]
+    wide = TP // CHUNKS * SHARD
     copies = []
-    for shard in range(TP):
-        lanes = columns(shard, half)
+    for chunk in range(CHUNKS):
+        lanes = pl.ds(chunk * wide, wide)
         copies.append(
             [
-                pltpu.make_async_copy(source.at[0, :, lanes], target.at[shard], sems.at[i, shard])
+                pltpu.make_async_copy(source.at[0, :, lanes], target.at[:, lanes], sems.at[i, chunk])
                 for i, (source, target) in enumerate(
                     ((gradient, gradient_part), (feedback, feedback_part))
                 )
             ]
         )
-    for pair in copies:
-        for copy in pair:
+        for copy in copies[chunk]:
             copy.start()
+    results = []
     for shard in range(TP):
-        for copy in copies[shard]:
-            copy.wait()
-        chip = (shard - t + (4 - half) * (TP // 2)) % TP
-        out[chip] = gradient_part[shard].astype(jnp.float32) + feedback_part[shard]
-
-
-def add_kernel(left, right, out, left_part, sems):
-    copies = [
-        pltpu.make_async_copy(left.at[chip], left_part.at[chip], sems.at[0, chip])
-        for chip in range(CHIPS)
-    ]
-    for copy in copies:
-        copy.start()
-    results = []
-    for chip in range(CHIPS):
-        copies[chip].wait()
-        left_part[chip] = left_part[chip] + right[chip]
-        results.append(pltpu.make_async_copy(left_part.at[chip], out.at[chip], sems.at[1, chip]))
-        results[chip].start()
+        if shard % (TP // CHUNKS) == 0:
+            for copy in copies[shard // (TP // CHUNKS)]:
+                copy.wait()
+        for half in range(2):
+            start = shard * SHARD + half * SPAN
+            lanes = slice(start, start + SPAN)
+            place = shard * 2 + half
+            merged[place] = gradient_part[:, lanes].astype(jnp.float32) + feedback_part[:, lanes]
+            chip = (shard - t + (4 - half) * (TP // 2)) % TP
+            results.append(
+                pltpu.make_async_copy(merged.at[place], out.at[chip * 2 + half], sems.at[2, place])
+            )
+            results[place].start()
     for copy in results:
         copy.wait()
 
@@ -106,8 +102,8 @@
 
 def factor_kernel(merged, q_twice, out):
     total = merged[0]
-    for chip in range(1, CHIPS):
-        total = total + merged[chip]
+    for d in range(1, DP):
+        total = total + merged[d]
     factor = dot(total, q_twice[...], 1, 1)
     lane = lax.broadcasted_iota(jnp.int32, (HALF, LANES), 1)
     packed = jnp.where(lane < RANK, factor[:HALF], factor[HALF:])
@@ -197,7 +193,13 @@
     half = half_ref[0]
     new_feedback, new_momentum, q_out = outs
     feedback_part, momentum_part, q_part = scratch
-    copies = []
+    for group in range(CHIPS // GROUP):
+        chips = range(group * GROUP, (group + 1) * GROUP)
+        w_tile = jnp.concatenate(swap_blocks([parts[chip, 2 * ROWS :, :] for chip in chips]), axis=0)
+        place = slice(group * LANES, (group + 1) * LANES)
+        q_part[:, place] = dot(inverse[...], w_tile, 1, 0) * (1.0 / DP)
+    copies = [pltpu.make_async_copy(q_part, q_out.at[:, columns(0, half)], sems.at[2, 0])]
+    copies[0].start()
     for th in range(TP // GROUP):
         rows = slice(th * ROWS, (th + 1) * ROWS)
         for group in range(CHIPS // GROUP):
@@ -222,13 +224,6 @@
             ]
             copies[-2].start()
             copies[-1].start()
-    for group in range(CHIPS // GROUP):
-        chips = range(group * GROUP, (group + 1) * GROUP)
-        w_tile = jnp.concatenate(swap_blocks([parts[chip, 2 * ROWS :, :] for chip in chips]), axis=0)
-        place = slice(group * LANES, (group + 1) * LANES)
-        q_part[:, place] = dot(inverse[...], w_tile, 1, 0) * (1.0 / DP)
-    copies.append(pltpu.make_async_copy(q_part, q_out.at[:, columns(0, half)], sems.at[2, 0]))
-    copies[-1].start()
     for copy in copies:
         copy.wait()
 
@@ -280,33 +275,23 @@
     chips = [list(range(c, DP, 2)) for c in range(2)]
     q_part = local(half_kernel, (RANK, SPAN), scalars=1)(core, q_previous)[0]
     q_part = permute(q_part, lambda chip, c, plane: (chip, (plane - chip - c * (TP // 2)) % TP))
-    q_part = local(twice_kernel, (2 * RANK, SPAN), flops=10_000_000_000)(q_part)[0]
-    whole = (CHIPS, ROWS, SPAN)
-    merge = functools.partial(
-        local,
+    q_part = local(twice_kernel, (2 * RANK, SPAN), flops=100_000)(q_part)[0]
+    merged = local(
         merge_kernel,
-        whole,
-        scalars=2,
+        (DP, ROWS, SPAN),
+        scalars=1,
         inputs=2,
         far=(0, 1),
+        far_out=True,
+        room=60,
         scratch=[
-            pltpu.VMEM((TP, ROWS, SPAN), jnp.bfloat16),
-            pltpu.VMEM((TP, ROWS, SPAN), jnp.float32),
-            pltpu.SemaphoreType.DMA((2, TP)),
+            pltpu.VMEM(gradient.shape[1:], jnp.bfloat16),
+            pltpu.VMEM(feedback.shape[1:], jnp.float32),
+            pltpu.VMEM((DP, ROWS, SPAN), jnp.float32),
+            pltpu.SemaphoreType.DMA((3, DP)),
         ],
-    )
-    send = merge(room=60)(1 - core, t, gradient, feedback)[0]
-    keep = merge(room=32)(core, t, gradient, feedback)[0]
-    merged = local(
-        add_kernel,
-        whole,
-        inputs=2,
-        far=(0,),
-        far_out=True,
-        room=32,
-        scratch=[pltpu.VMEM(whole, jnp.float32), pltpu.SemaphoreType.DMA((2, CHIPS))],
-    )(keep, swap_cores(send))[0]
-    merged = exchange(merged, "dp", chips)
+    )(t, gradient, feedback)[0]
+    merged = exchange(merged, "dp")
     factor = local(factor_kernel, (DP, HALF + 8, LANES), inputs=2)(merged, q_part)[0]
     factor = exchange(factor, "dp")
     parts = local(project_kernel, (TP, HALF + 8, LANES), scalars=3)(core, chip, t, factor)[0]

time: 120 us -> 120 us (level)
  waiting for transfers between devices: 27.2 us -> 19.5 us
  blocking collectives: 31 us -> 37.4 us
  starting transfers between devices: 42.4 us -> 45.8 us
  Pallas kernels: 18 us -> 16.1 us
    all_to_all x3, waiting for transfers between devices: 27.2 us -> 17.8 us  [exchange(): lax.all_to_all(parts, axis, 0, 0, tiled=True, axis_index_groups=groups)]
    ppermute x2 -> x1, starting transfers between devices: 14 us -> 5.22 us  [swap_cores(): return lax.ppermute(parts, 'dp', [(d, d ^ 1) for d in range(DP)])]
    all_to_all x3, starting transfers between devices: 18.3 us -> 27 us  [exchange(): lax.all_to_all(parts, axis, 0, 0, tiled=True, axis_index_groups=groups)]
    all_to_all x2, blocking collectives: 31 us -> 37.4 us  [exchange(): lax.all_to_all(parts, axis, 0, 0, tiled=True, axis_index_groups=groups)]
    ppermute x1, starting transfers between devices: 10.1 us -> 13.6 us  [permute(): return lax.ppermute(parts, ('dp', 'tensor'), pairs)]
    pallas_call x4 -> x2, Pallas kernels: 4.79 us -> 2.97 us  [the longest x1 2.96 us: on_device(): local(merge_kernel, (DP, ROWS, SPAN), scalars=1, inputs=2, far=(0, 1), fa...]
    ppermute x1, waiting for transfers between devices: 0.01 us -> 1.64 us  [permute(): return lax.ppermute(parts, ('dp', 'tensor'), pairs)]
  transfers between devices with their start and end apart: 6 -> 5, of which waited for: 3 -> 4; matrix products, arithmetic and copies ran while one was open for 0% -> 0% of each run, Pallas kernels for 9% -> 7%
where the time goes in v8:
time: 120 us
  starting transfers between devices  45.8 us (38%)
  blocking collectives  37.4 us (31%)
  waiting for transfers between devices  19.5 us (16%)
  Pallas kernels  16.1 us (13%)
    all_to_all x2, blocking collectives, exchange(): lax.all_to_all(parts, axis, 0, 0, tiled=True, axis_index_groups=groups)  37.4 us
    all_to_all x3, starting transfers between devices, exchange(): lax.all_to_all(parts, axis, 0, 0, tiled=True, axis_index_groups=groups)  27 us
    all_to_all x3, waiting for transfers between devices, exchange(): lax.all_to_all(parts, axis, 0, 0, tiled=True, axis_index_groups=groups)  17.8 us
    ppermute x1, starting transfers between devices, permute(): return lax.ppermute(parts, ('dp', 'tensor'), pairs)  13.6 us
    pallas_call x1, Pallas kernels, on_device(): local(basis_kernel, (RANK, RANK), (ROWS, RANK), scalars=1, scratch=[pltpu...  5.9 us
    ppermute x1, starting transfers between devices, swap_cores(): return lax.ppermute(parts, 'dp', [(d, d ^ 1) for d in range(DP)])  5.22 us
    pallas_call x1, Pallas kernels, on_device(): local(merge_kernel, (DP, ROWS, SPAN), scalars=1, inputs=2, far=(0, 1), fa...  2.96 us
  transfers between devices with their start and end apart: 5, of which 4 were waited for; matrix products, arithmetic and copies ran while one was open for 0% of the time, Pallas kernels for 7%

profile of v8, /device:TPU:1, one launch (start us, length us, event | category | flops | bytes accessed | tf_op | source)
XLA Modules:
  0.0 119.6 jit_solution(10220193233877432746)
XLA Ops:
  0.6 3.0 %shard_map.67 = f32[32,32,256]{2,1,0:T(8,128)} custom-call(s32[1]{0:T(128)} %bitcast.1.t_ref, bf16[1,32,8192]{2,1,0:T(8,128)(2,1)} %gradient.5, f32[1,32,8192]{2,1,0:T(8,128)} %feedback.5), custom_call_target="tpu_custom_call" | custom-call | flops 100000 | bytes 100000 | tf_op jit(solution)/shard_map/pallas_call | solution.py:279
  3.6 0.0 copy-start.3
  3.6 10.6 %all-to-all-start = ((f32[32,32,256]{2,1,0:T(8,128)}), f32[32,32,256]{2,1,0:T(8,128)S(1)}, u32[]{:S(2)}, u32[]{:S(2)}) async-start(f32[32,32,256]{2,1,0:T(8,128)} %shard_map.67), calls=%async_computation | async-start | bytes 2097152 | tf_op jit(solution)/shard_map/all_to_all | solution.py:255
  14.2 0.0 copy-done.3
  14.3 13.6 %collective-permute-start = (f32[64,256]{1,0:T(8,128)S(1)}, f32[64,256]{1,0:T(8,128)S(1)}, u32[]{:S(2)}, u32[]{:S(2)}) collective-permute-start(f32[64,256]{1,0:T(8,128)S(1)} %shard_map.68), channel_id=1, source_target_pairs={{0,0},{1,1},{2,2},{3,3},{4,4},{5,5},{6,6},{7,7},{8,8},{9,9},{10,10... | collective-permute-start | bytes 196616 | tf_op jit(solution)/shard_map/ppermute | solution.py:268
  27.8 1.6 %collective-permute-done.q_part = f32[64,256]{1,0:T(8,128)S(1)} collective-permute-done((f32[64,256]{1,0:T(8,128)S(1)}, f32[64,256]{1,0:T(8,128)S(1)}, u32[]{:S(2)}, u32[]{:S(2)}) %collective-permute-start) | collective-permute-done | bytes 65568 | tf_op jit(solution)/shard_map/ppermute | solution.py:268
  29.5 2.0 %all-to-all-done.merged = f32[32,32,256]{2,1,0:T(8,128)S(1)} async-done(((f32[32,32,256]{2,1,0:T(8,128)}), f32[32,32,256]{2,1,0:T(8,128)S(1)}, u32[]{:S(2)}, u32[]{:S(2)}) %all-to-all-start) | async-done | bytes 1048608 | tf_op jit(solution)/shard_map/all_to_all | solution.py:255
  31.5 1.0 shard_map.70
  32.5 7.9 %all-to-all-start.1 = ((f32[32,24,128]{2,1,0:T(8,128)}), f32[32,24,128]{2,1,0:T(8,128)S(1)}, u32[]{:S(2)}, u32[]{:S(2)}) async-start(f32[32,24,128]{2,1,0:T(8,128)} %shard_map.70), calls=%async_computation.1 | async-start | bytes 786432 | tf_op jit(solution)/shard_map/all_to_all | solution.py:255
  40.5 10.2 %all-to-all-done.1.parts = f32[32,24,128]{2,1,0:T(8,128)S(1)} async-done(((f32[32,24,128]{2,1,0:T(8,128)}), f32[32,24,128]{2,1,0:T(8,128)S(1)}, u32[]{:S(2)}, u32[]{:S(2)}) %all-to-all-start.1) | async-done | bytes 393248 | tf_op jit(solution)/shard_map/all_to_all | solution.py:255
  50.7 0.7 shard_map.71
  51.3 0.0 copy-start.2
  51.4 24.0 %all_to_all.25.parts = f32[16,24,128]{2,1,0:T(8,128)S(1)} all-to-all(f32[16,24,128]{2,1,0:T(8,128)S(1)} %shard_map.71), channel_id=1, replica_groups=mesh['dp'=32,'tensor'=16] {'tensor'}, dimensions={0} | all-to-all | bytes 393216 | tf_op jit(solution)/shard_map/all_to_all | solution.py:255
  75.4 0.7 shard_map.73
  76.1 8.5 %all-to-all-start.3 = ((f32[16,8,128]{2,1,0:T(8,128)}), f32[16,8,128]{2,1,0:T(8,128)S(1)}, u32[]{:S(2)}, u32[]{:S(2)}) async-start(f32[16,8,128]{2,1,0:T(8,128)} %get-tuple-element.12), calls=%async_computation.3 | async-start | bytes 131072 | tf_op jit(solution)/shard_map/all_to_all | solution.py:255
  84.5 0.0 copy-start
  84.5 5.9 %shard_map.72 = (f32[64,64]{1,0:T(8,128)S(1)}, f32[32,64]{1,0:T(8,128)S(1)}) custom-call(s32[1]{0:T(128)} %bitcast.1.t_ref, f32[16,24,128]{2,1,0:T(8,128)S(1)} %all_to_all.25.parts), custom_call_target="tpu_custom_call" | custom-call | flops 100000 | bytes 100000 | tf_op jit(solution)/shard_map/pallas_call | solution.py:301
  90.4 5.7 %all-to-all-done.3.w_parts = f32[16,8,128]{2,1,0:T(8,128)S(1)} async-done(((f32[16,8,128]{2,1,0:T(8,128)}), f32[16,8,128]{2,1,0:T(8,128)S(1)}, u32[]{:S(2)}, u32[]{:S(2)}) %all-to-all-start.3) | async-done | bytes 65568 | tf_op jit(solution)/shard_map/all_to_all | solution.py:255
  96.1 0.6 shard_map.74
  96.7 0.0 copy-start.1
  96.7 13.4 %all_to_all.26.parts = f32[16,72,128]{2,1,0:T(8,128)S(1)} all-to-all(f32[16,72,128]{2,1,0:T(8,128)S(1)} %shard_map.74), channel_id=1, replica_groups={{0,32,64,96,128,160,192,224,256,288,320,352,384,416,448,480},{16,48,80,..., dimensions={0} | all-to-all | bytes 1179648 | tf_op jit(solution)/shard_map/all_to_all | solution.py:255
  110.1 5.2 %collective-permute-start.1 = (f32[16,72,128]{2,1,0:T(8,128)S(1)}, f32[16,72,128]{2,1,0:T(8,128)S(1)}, u32[]{:S(2)}, u32[]{:S(2)}) collective-permute-start(f32[16,72,128]{2,1,0:T(8,128)S(1)} %all_to_all.26.parts), channel_id=1, source_target_pairs={{0,16},{16,0},{32,48},{48,32},{64,80},{80,64},{96,112},{112,96},{1... | collective-permute-start | bytes 1769480 | tf_op jit(solution)/shard_map/ppermute | solution.py:259
  115.3 0.0 copy-done.2
  115.3 0.0 copy-done
  115.3 0.0 copy-done.1
  115.3 2.1 %shard_map.75 = (f32[1,32,8192]{2,1,0:T(8,128)}, f32[32,8192]{1,0:T(8,128)}, f32[64,512]{1,0:T(8,128)}) custom-call(s32[1]{0:T(128)} %bitcast.core_ref.half_ref, bf16[1,32,8192]{2,1,0:T(8,128)(2,1)S(1)} %copy-done.1, f32[1,32,8192]{2,1,0:T(8,128)S(1)} %copy-done, f32[32,8192]{1,0:T(8,128)S(1)} %copy-done.2, f32[64,64]{1,0:T(8,128)S(1)} %get-tuple-element.10.inverse, ...), custom_call_target="tpu_custom_call" | custom-call | flops 100000 | bytes 100000 | tf_op jit(solution)/shard_map/pallas_call | solution.py:320
  117.4 0.0 collective-permute-done.1.parts
  117.5 2.1 %shard_map.76 = (f32[1,32,8192]{2,1,0:T(8,128)}, f32[32,8192]{1,0:T(8,128)}, f32[64,512]{1,0:T(8,128)}) custom-call(s32[1]{0:T(128)S(6)} %sub.3.half_ref, bf16[1,32,8192]{2,1,0:T(8,128)(2,1)S(1)} %copy-done.1, f32[1,32,8192]{2,1,0:T(8,128)S(1)} %copy-done, f32[32,8192]{1,0:T(8,128)S(1)} %copy-done.2, ...), custom_call_target="tpu_custom_call", output_to_operand_aliasing={{0}: (6, {}), {1}: (7, {}), {2}: (8, {})} | custom-call | flops 100000 | bytes 100000 | tf_op jit(solution)/shard_map/pallas_call | solution.py:323
  (2 shorter events, 0.0 us)
Async XLA Ops:
  3.6 10.6 %copy-start.3 = (f32[64,512]{1,0:T(8,128)S(1)}, f32[64,512]{1,0:T(8,128)}, u32[]{:S(2)}) copy-start(f32[64,512]{1,0:T(8,128)} %q_ref.1) | copy-start | bytes 393220
  3.6 27.9 %all-to-all-start = ((f32[32,32,256]{2,1,0:T(8,128)}), f32[32,32,256]{2,1,0:T(8,128)S(1)}, u32[]{:S(2)}, u32[]{:S(2)}) async-start(f32[32,32,256]{2,1,0:T(8,128)} %shard_map.67), calls=%async_computation | async-start | bytes 2097152 | tf_op jit(solution)/shard_map/all_to_all | solution.py:255
  14.3 15.2 %collective-permute-start = (f32[64,256]{1,0:T(8,128)S(1)}, f32[64,256]{1,0:T(8,128)S(1)}, u32[]{:S(2)}, u32[]{:S(2)}) collective-permute-start(f32[64,256]{1,0:T(8,128)S(1)} %shard_map.68), channel_id=1, source_target_pairs={{0,0},{1,1},{2,2},{3,3},{4,4},{5,5},{6,6},{7,7},{8,8},{9,9},{10,10... | collective-permute-start | bytes 196616 | tf_op jit(solution)/shard_map/ppermute | solution.py:268
  32.5 18.1 %all-to-all-start.1 = ((f32[32,24,128]{2,1,0:T(8,128)}), f32[32,24,128]{2,1,0:T(8,128)S(1)}, u32[]{:S(2)}, u32[]{:S(2)}) async-start(f32[32,24,128]{2,1,0:T(8,128)} %shard_map.70), calls=%async_computation.1 | async-start | bytes 786432 | tf_op jit(solution)/shard_map/all_to_all | solution.py:255
  51.3 64.0 %copy-start.2 = (f32[32,8192]{1,0:T(8,128)S(1)}, f32[32,8192]{1,0:T(8,128)}, u32[]{:S(2)}) copy-start(f32[32,8192]{1,0:T(8,128)} %momentum.3) | copy-start | bytes 3145732
  76.1 20.0 %all-to-all-start.3 = ((f32[16,8,128]{2,1,0:T(8,128)}), f32[16,8,128]{2,1,0:T(8,128)S(1)}, u32[]{:S(2)}, u32[]{:S(2)}) async-start(f32[16,8,128]{2,1,0:T(8,128)} %get-tuple-element.12), calls=%async_computation.3 | async-start | bytes 131072 | tf_op jit(solution)/shard_map/all_to_all | solution.py:255
  84.5 30.8 %copy-start = (f32[1,32,8192]{2,1,0:T(8,128)S(1)}, f32[1,32,8192]{2,1,0:T(8,128)}, u32[]{:S(2)}) copy-start(f32[1,32,8192]{2,1,0:T(8,128)} %feedback.5) | copy-start | bytes 3145732
  96.7 18.6 %copy-start.1 = (bf16[1,32,8192]{2,1,0:T(8,128)(2,1)S(1)}, bf16[1,32,8192]{2,1,0:T(8,128)(2,1)}, u32[]{:S(2)}) copy-start(bf16[1,32,8192]{2,1,0:T(8,128)(2,1)} %gradient.5) | copy-start | bytes 1572868
  110.1 7.4 %collective-permute-start.1 = (f32[16,72,128]{2,1,0:T(8,128)S(1)}, f32[16,72,128]{2,1,0:T(8,128)S(1)}, u32[]{:S(2)}, u32[]{:S(2)}) collective-permute-start(f32[16,72,128]{2,1,0:T(8,128)S(1)} %all_to_all.26.parts), channel_id=1, source_target_pairs={{0,16},{16,0},{32,48},{48,32},{64,80},{80,64},{96,112},{112,96},{1... | collective-permute-start | bytes 1769480 | tf_op jit(solution)/shard_map/ppermute | solution.py:259

commit v9 on v8

--- a/solution.py
+++ b/solution.py
@@ -46,6 +46,18 @@
             parts[i] = jnp.where(upper, pltpu.roll(b, step * BLOCK, 1), a)
             parts[i | step] = jnp.where(upper, b, pltpu.roll(a, LANES - step * BLOCK, 1))
     return parts
+
+
+def gather_blocks(matrix, lane_block):
+    block = lax.broadcasted_iota(jnp.int32, (8, LANES), 1) // BLOCK
+    moved = pltpu.roll(matrix, (GROUP - lane_block) % GROUP * BLOCK, 1)
+    out = jnp.zeros((8, LANES), jnp.float32)
+    for kh in range(GROUP):
+        piece = moved[kh * 8 : (kh + 1) * 8, :]
+        if kh:
+            piece = pltpu.roll(piece, kh * BLOCK, 1)
+        out = jnp.where(block == kh, piece, out)
+    return out
 
 
 def columns(shard, half):
@@ -96,10 +108,6 @@
     out[RANK:, :] = q_part[...]
 
 
-def unpack_blocks(parts, th):
-    return jnp.concatenate(swap_blocks([parts[th * GROUP + tl] for tl in range(GROUP)]), axis=0)
-
-
 def factor_kernel(merged, q_twice, out):
     total = merged[0]
     for d in range(1, DP):
@@ -127,7 +135,7 @@
     packed = parts[0, :HALF, :]
     for d in range(1, DP):
         packed = packed + parts[d, :HALF, :]
-    rows = unpack_rows(packed)
+    out[:HALF, :] = packed
     low = chip_ref[0] < GROUP
     for th in range(TP // GROUP):
         pieces = []
@@ -135,69 +143,79 @@
             source = (th * GROUP + tl - t_ref[0] + (4 - core_ref[0]) * (TP // 2)) % TP
             pieces.append(parts[source * 2 + core_ref[0], HALF:, :])
         pieces = swap_blocks(pieces)
-        total = jnp.concatenate(
-            [jnp.where(low, pieces[g], pieces[g + ROWS // 8]) for g in range(ROWS // 8)], axis=0
-        )
-        term = dot(rows, total, 0, 0)
-        chunks = swap_blocks([term[kh * 8 : (kh + 1) * 8] for kh in range(GROUP)])
-        for tl, chunk in enumerate(chunks):
-            out[th * GROUP + tl, :HALF, :] = packed
-            out[th * GROUP + tl, HALF:, :] = chunk
-
-
-def chunk_kernel(parts, out, chunk_out):
-    total = parts[0, HALF:, :]
-    for t in range(1, TP):
-        total = total + parts[t, HALF:, :]
-    chunk_out[...] = total
-    for t in range(TP):
-        out[t] = total
-
-
-def inverse_triangle(gram, rows_ref):
+        start = HALF + th * ROWS
+        for g in range(ROWS // 8):
+            out[start + g * 8 : start + (g + 1) * 8, :] = jnp.where(
+                low, pieces[g], pieces[g + ROWS // 8]
+            )
+
+
+def inverse_triangle(gram):
+    size = 8
+    count = RANK // size
     row = lax.broadcasted_iota(jnp.int32, (RANK, LANES), 0)
     lane = lax.broadcasted_iota(jnp.int32, (RANK, LANES), 1)
     identity = jnp.where(lane == row + RANK, 1.0, 0.0)
     work = jnp.concatenate([gram, jnp.zeros_like(gram)], axis=1) + identity
-    for k in range(RANK):
-        pivot_row = work[k : k + 1, :]
-        pivot = work[k : k + 1, k : k + 1]
-        rows_ref[k : k + 1, :] = pivot_row * lax.rsqrt(pivot)
-        if k + 1 < RANK:
-            scaled = pivot_row * (1.0 / pivot)
-            column = work[:, k : k + 1]
-            work = work - jnp.where(row > k, column, 0.0) * scaled
-    return rows_ref[:, RANK:]
-
-
-def basis_kernel(t_ref, parts, inverse_out, basis_out, rows_ref):
-    flat = parts[:, :HALF, :].reshape(TP * HALF, LANES)
-    whole = unpack_rows(flat)
-    inverse = inverse_triangle(dot(whole, whole, 0, 0), rows_ref)
-    inverse_out[...] = inverse
-    own = unpack_rows(parts[t_ref[0], :HALF, :])
-    basis_out[...] = dot(own, inverse, 1, 1)
-
-
-def approx_kernel(inverse, basis, w_parts, chunk, out):
-    approx = []
+    work = [work[g * size : (g + 1) * size, :] for g in range(count)]
+    row = lax.broadcasted_iota(jnp.int32, (size, LANES), 0)
+    for b in range(count):
+        spread = {
+            g: [
+                jnp.broadcast_to(work[g][:, b * size + k : b * size + k + 1], (size, LANES))
+                for k in range(size)
+            ]
+            for g in range(b, count)
+        }
+        pivots = jnp.zeros((size, LANES), jnp.float32)
+        for k in range(size):
+            pivot_row = work[b][k : k + 1, :]
+            heads = [spread[b][j][k : k + 1, :] for j in range(size)]
+            pivots = jnp.where(row == k, heads[k], pivots)
+            reciprocal = 1.0 / heads[k]
+            for g in range(b, count):
+                factor = spread[g][k] * reciprocal
+                if g == b:
+                    factor = jnp.where(row > k, factor, 0.0)
+                work[g] = work[g] - factor * pivot_row
+                for j in range(k + 1, size):
+                    spread[g][j] = spread[g][j] - factor * heads[j]
+        work[b] = work[b] * lax.rsqrt(pivots)
+    return jnp.concatenate(work, axis=0)[:, RANK:]
+
+
+def solve_kernel(t_ref, parts, out):
+    t = t_ref[0]
+    whole = unpack_rows(parts[:, :HALF, :].reshape(TP * HALF, LANES))
+    whole_t = whole.T
+    inverse = inverse_triangle(dot(whole_t, whole, 1, 0))
+    basis = dot(unpack_rows(parts[t, :HALF, :]), inverse, 1, 1)
+    approx, q_tiles = [], []
     for th in range(TP // GROUP):
-        q_tile = dot(inverse[...], unpack_blocks(w_parts, th), 1, 0) * (1.0 / DP)
-        approx.append(dot(basis[...], q_tile, 1, 0))
-    message = jnp.concatenate(approx + [chunk[...]], axis=0)
+        start = HALF + th * ROWS
+        sums = jnp.concatenate(
+            [
+                parts[:, start + h * HALF : start + (h + 1) * HALF, :].reshape(TP * HALF, LANES)
+                for h in range(2)
+            ],
+            axis=0,
+        )
+        q_tiles.append(dot(inverse, dot(whole_t, sums, 1, 0), 1, 0) * (1.0 / DP))
+        approx.append(dot(basis, q_tiles[th], 1, 0))
+    mine = jnp.where(t // GROUP == 0, q_tiles[0], q_tiles[1])
+    message = jnp.concatenate(approx + [gather_blocks(mine, t % GROUP)], axis=0)
     for chip in range(CHIPS):
         out[chip] = message
 
 
-def finish_half(half_ref, gradient, feedback, momentum, inverse, parts, outs, scratch, sems):
+def finish_half(half_ref, gradient, feedback, momentum, parts, outs, scratch, sems):
     half = half_ref[0]
     new_feedback, new_momentum, q_out = outs
     feedback_part, momentum_part, q_part = scratch
     for group in range(CHIPS // GROUP):
         chips = range(group * GROUP, (group + 1) * GROUP)
-        w_tile = jnp.concatenate(swap_blocks([parts[chip, 2 * ROWS :, :] for chip in chips]), axis=0)
-        place = slice(group * LANES, (group + 1) * LANES)
-        q_part[:, place] = dot(inverse[...], w_tile, 1, 0) * (1.0 / DP)
+        chunks = swap_blocks([parts[chip, 2 * ROWS :, :] for chip in chips])
+        q_part[:, group * LANES : (group + 1) * LANES] = jnp.concatenate(chunks, axis=0)
     copies = [pltpu.make_async_copy(q_part, q_out.at[:, columns(0, half)], sems.at[2, 0])]
     copies[0].start()
     for th in range(TP // GROUP):
@@ -228,12 +246,12 @@
         copy.wait()
 
 
-def finish_own_kernel(half_ref, gradient, feedback, momentum, inverse, parts, *refs):
-    finish_half(half_ref, gradient, feedback, momentum, inverse, parts, refs[:3], refs[3:6], refs[6])
-
-
-def finish_other_kernel(half_ref, gradient, feedback, momentum, inverse, parts, *refs):
-    finish_half(half_ref, gradient, feedback, momentum, inverse, parts, refs[3:6], refs[6:9], refs[9])
+def finish_own_kernel(half_ref, gradient, feedback, momentum, parts, *refs):
+    finish_half(half_ref, gradient, feedback, momentum, parts, refs[:3], refs[3:6], refs[6])
+
+
+def finish_other_kernel(half_ref, gradient, feedback, momentum, parts, *refs):
+    finish_half(half_ref, gradient, feedback, momentum, parts, refs[3:6], refs[6:9], refs[9])
 
 
 def local(kernel, *shapes, scalars=0, inputs=1, scratch=(), flops=100_000, far=(), far_out=False, alias=None, room=32):
@@ -294,20 +312,9 @@
     merged = exchange(merged, "dp")
     factor = local(factor_kernel, (DP, HALF + 8, LANES), inputs=2)(merged, q_part)[0]
     factor = exchange(factor, "dp")
-    parts = local(project_kernel, (TP, HALF + 8, LANES), scalars=3)(core, chip, t, factor)[0]
-    parts = exchange(parts, "tensor")
-    w_parts, chunk = local(chunk_kernel, (TP, 8, LANES), (8, LANES))(parts)
-    w_parts = exchange(w_parts, "tensor")
-    inverse, basis = local(
-        basis_kernel,
-        (RANK, RANK),
-        (ROWS, RANK),
-        scalars=1,
-        scratch=[pltpu.VMEM((RANK, LANES), jnp.float32)],
-    )(t, parts)
-    own = local(approx_kernel, (CHIPS, 2 * ROWS + 8, LANES), inputs=4)(
-        inverse, basis, w_parts, chunk
-    )[0]
+    parts = local(project_kernel, (HALF + 2 * ROWS, LANES), scalars=3)(core, chip, t, factor)[0]
+    parts = lax.all_gather(parts, "tensor")
+    own = local(solve_kernel, (CHIPS, 2 * ROWS + 8, LANES), scalars=1)(t, parts)[0]
     own = exchange(own, "dp", chips)
     other = swap_cores(own)
     shapes = (feedback.shape, momentum.shape, q_previous.shape)
@@ -318,18 +325,18 @@
         pltpu.SemaphoreType.DMA((3, TP)),
     ]
     outs = local(
-        finish_own_kernel, *shapes, scalars=1, inputs=5, scratch=scratch, far_out=True
-    )(core, gradient, feedback, momentum, inverse, own)
+        finish_own_kernel, *shapes, scalars=1, inputs=4, scratch=scratch, far_out=True
+    )(core, gradient, feedback, momentum, own)
     outs = local(
         finish_other_kernel,
         *shapes,
         scalars=1,
-        inputs=8,
+        inputs=7,
         scratch=scratch,
-        far=(5, 6, 7),
+        far=(4, 5, 6),
         far_out=True,
-        alias={6: 0, 7: 1, 8: 2},
-    )(1 - core, gradient, feedback, momentum, inverse, other, *outs)
+        alias={5: 0, 6: 1, 7: 2},
+    )(1 - core, gradient, feedback, momentum, other, *outs)
     return tuple(outs)
 
 

time: 120 us -> 109 us (0.908)
  waiting for transfers between devices: 19.5 us -> 13.8 us
  Pallas kernels: 16.1 us -> 11.6 us
  starting transfers between devices: 45.8 us -> 41.8 us
  blocking collectives: 37.4 us -> 40.1 us
    all_gather x0 -> x1, blocking collectives: none -> 26.7 us  [on_device(): parts = lax.all_gather(parts, 'tensor')]
    all_to_all x2 -> x1, blocking collectives: 37.4 us -> 13.4 us  [exchange(): lax.all_to_all(parts, axis, 0, 0, tiled=True, axis_index_groups=groups)]
    all_to_all x3 -> x2, starting transfers between devices: 27 us -> 18.5 us  [exchange(): lax.all_to_all(parts, axis, 0, 0, tiled=True, axis_index_groups=groups)]
    all_to_all x3 -> x2, waiting for transfers between devices: 17.8 us -> 12.2 us  [exchange(): lax.all_to_all(parts, axis, 0, 0, tiled=True, axis_index_groups=groups)]
    ppermute x1, starting transfers between devices: 5.22 us -> 9.74 us  [swap_cores(): return lax.ppermute(parts, 'dp', [(d, d ^ 1) for d in range(DP)])]
    pallas_call x6 -> x4, Pallas kernels: 12.1 us -> 7.62 us  [the longest x1 3.22 us: on_device(): local(solve_kernel, (CHIPS, 2 * ROWS + 8, LANES), scalars=1)(t, parts)[0]]
  transfers between devices with their start and end apart: 5 -> 4, of which waited for: 4 -> 3; matrix products, arithmetic and copies ran while one was open for 0% -> 0% of each run, Pallas kernels for 7% -> 2%
where the time goes in v9:
time: 109 us; the launch traced here: 108 us
  starting transfers between devices  41.8 us (38%)
  blocking collectives  40.1 us (37%)
  waiting for transfers between devices  13.8 us (13%)
  Pallas kernels  11.6 us (11%)
    all_gather x1, blocking collectives, on_device(): parts = lax.all_gather(parts, 'tensor')  26.7 us
    all_to_all x2, starting transfers between devices, exchange(): lax.all_to_all(parts, axis, 0, 0, tiled=True, axis_index_groups=groups)  18.5 us
    ppermute x1, starting transfers between devices, permute(): return lax.ppermute(parts, ('dp', 'tensor'), pairs)  13.6 us
    all_to_all x1, blocking collectives, exchange(): lax.all_to_all(parts, axis, 0, 0, tiled=True, axis_index_groups=groups)  13.4 us
    all_to_all x2, waiting for transfers between devices, exchange(): lax.all_to_all(parts, axis, 0, 0, tiled=True, axis_index_groups=groups)  12.2 us
    ppermute x1, starting transfers between devices, swap_cores(): return lax.ppermute(parts, 'dp', [(d, d ^ 1) for d in range(DP)])  9.74 us
    pallas_call x1, Pallas kernels, on_device(): local(solve_kernel, (CHIPS, 2 * ROWS + 8, LANES), scalars=1)(t, parts)[0]  3.22 us
    pallas_call x1, Pallas kernels, on_device(): local(merge_kernel, (DP, ROWS, SPAN), scalars=1, inputs=2, far=(0, 1), fa...  2.96 us
  transfers between devices with their start and end apart: 4, of which 3 were waited for; matrix products, arithmetic and copies ran while one was open for 0% of the time, Pallas kernels for 2%

profile of v9, /device:TPU:1, one launch (start us, length us, event | category | flops | bytes accessed | tf_op | source)
XLA Modules:
  0.0 108.2 jit_solution(5134139541576949934)
XLA Ops:
  0.6 3.0 %shard_map.67 = f32[32,32,256]{2,1,0:T(8,128)} custom-call(s32[1]{0:T(128)} %bitcast.1.t_ref, bf16[1,32,8192]{2,1,0:T(8,128)(2,1)} %gradient.5, f32[1,32,8192]{2,1,0:T(8,128)} %feedback.5), custom_call_target="tpu_custom_call" | custom-call | flops 100000 | bytes 100000 | tf_op jit(solution)/shard_map/pallas_call | solution.py:297
  3.6 0.0 copy-start.3
  3.6 10.6 %all-to-all-start = ((f32[32,32,256]{2,1,0:T(8,128)}), f32[32,32,256]{2,1,0:T(8,128)S(1)}, u32[]{:S(2)}, u32[]{:S(2)}) async-start(f32[32,32,256]{2,1,0:T(8,128)} %shard_map.67), calls=%async_computation | async-start | bytes 2097152 | tf_op jit(solution)/shard_map/all_to_all | solution.py:273
  14.2 0.0 copy-done.3
  14.3 13.6 %collective-permute-start = (f32[64,256]{1,0:T(8,128)S(1)}, f32[64,256]{1,0:T(8,128)S(1)}, u32[]{:S(2)}, u32[]{:S(2)}) collective-permute-start(f32[64,256]{1,0:T(8,128)S(1)} %shard_map.68), channel_id=1, source_target_pairs={{0,0},{1,1},{2,2},{3,3},{4,4},{5,5},{6,6},{7,7},{8,8},{9,9},{10,10... | collective-permute-start | bytes 196616 | tf_op jit(solution)/shard_map/ppermute | solution.py:286
  27.8 1.6 %collective-permute-done.q_part = f32[64,256]{1,0:T(8,128)S(1)} collective-permute-done((f32[64,256]{1,0:T(8,128)S(1)}, f32[64,256]{1,0:T(8,128)S(1)}, u32[]{:S(2)}, u32[]{:S(2)}) %collective-permute-start) | collective-permute-done | bytes 65568 | tf_op jit(solution)/shard_map/ppermute | solution.py:286
  29.5 2.0 %all-to-all-done.merged = f32[32,32,256]{2,1,0:T(8,128)S(1)} async-done(((f32[32,32,256]{2,1,0:T(8,128)}), f32[32,32,256]{2,1,0:T(8,128)S(1)}, u32[]{:S(2)}, u32[]{:S(2)}) %all-to-all-start) | async-done | bytes 1048608 | tf_op jit(solution)/shard_map/all_to_all | solution.py:273
  31.5 1.0 shard_map.70
  32.5 7.9 %all-to-all-start.1 = ((f32[32,24,128]{2,1,0:T(8,128)}), f32[32,24,128]{2,1,0:T(8,128)S(1)}, u32[]{:S(2)}, u32[]{:S(2)}) async-start(f32[32,24,128]{2,1,0:T(8,128)} %shard_map.70), calls=%async_computation.1 | async-start | bytes 786432 | tf_op jit(solution)/shard_map/all_to_all | solution.py:273
  40.5 10.2 %all-to-all-done.1.parts = f32[32,24,128]{2,1,0:T(8,128)S(1)} async-done(((f32[32,24,128]{2,1,0:T(8,128)}), f32[32,24,128]{2,1,0:T(8,128)S(1)}, u32[]{:S(2)}, u32[]{:S(2)}) %all-to-all-start.1) | async-done | bytes 393248 | tf_op jit(solution)/shard_map/all_to_all | solution.py:273
  50.7 0.3 shard_map.71
  50.9 0.0 copy-start.2
  50.9 26.7 %all-gather = f32[1280,128]{1,0:T(8,128)S(1)} all-gather(f32[80,128]{1,0:T(8,128)S(1)} %shard_map.71), channel_id=2, replica_groups=mesh['dp'=32,'tensor'=16] {'tensor'}, dimensions={0}, use_global_device_ids=true | all-gather | bytes 696320 | tf_op jit(solution)/shard_map/all_gather | solution.py:316
  77.7 0.0 copy-start
  77.7 3.2 %shard_map.72 = f32[16,72,128]{2,1,0:T(8,128)S(1)} custom-call(s32[1]{0:T(128)} %bitcast.1.t_ref, f32[16,80,128]{2,1,0:T(8,128)S(1)} %bitcast.4), custom_call_target="tpu_custom_call" | custom-call | flops 100000 | bytes 100000 | tf_op jit(solution)/shard_map/pallas_call | solution.py:317
  80.9 0.0 copy-start.1
  80.9 13.4 %all_to_all.15.parts = f32[16,72,128]{2,1,0:T(8,128)S(1)} all-to-all(f32[16,72,128]{2,1,0:T(8,128)S(1)} %shard_map.72), channel_id=1, replica_groups={{0,32,64,96,128,160,192,224,256,288,320,352,384,416,448,480},{16,48,80,..., dimensions={0} | all-to-all | bytes 1179648 | tf_op jit(solution)/shard_map/all_to_all | solution.py:273
  94.3 9.7 %collective-permute-start.1 = (f32[16,72,128]{2,1,0:T(8,128)S(1)}, f32[16,72,128]{2,1,0:T(8,128)S(1)}, u32[]{:S(2)}, u32[]{:S(2)}) collective-permute-start(f32[16,72,128]{2,1,0:T(8,128)S(1)} %all_to_all.15.parts), channel_id=1, source_target_pairs={{0,16},{16,0},{32,48},{48,32},{64,80},{80,64},{96,112},{112,96},{1... | collective-permute-start | bytes 1769480 | tf_op jit(solution)/shard_map/ppermute | solution.py:277
  104.1 0.0 copy-done.2
  104.1 0.0 copy-done
  104.1 0.0 copy-done.1
  104.1 2.1 %shard_map.73 = (f32[1,32,8192]{2,1,0:T(8,128)}, f32[32,8192]{1,0:T(8,128)}, f32[64,512]{1,0:T(8,128)}) custom-call(s32[1]{0:T(128)} %bitcast.core_ref.half_ref, bf16[1,32,8192]{2,1,0:T(8,128)(2,1)S(1)} %copy-done.1, f32[1,32,8192]{2,1,0:T(8,128)S(1)} %copy-done, f32[32,8192]{1,0:T(8,128)S(1)} %copy-done.2, f32[16,72,128]{2,1,0:T(8,128)S(1)} %all_to_all.15.parts), custom_call_target="tpu_custom_call" | custom-call | flops 100000 | bytes 100000 | tf_op jit(solution)/shard_map/pallas_call | solution.py:327
  106.2 0.0 collective-permute-done.1.parts
  106.2 2.1 %shard_map.74 = (f32[1,32,8192]{2,1,0:T(8,128)}, f32[32,8192]{1,0:T(8,128)}, f32[64,512]{1,0:T(8,128)}) custom-call(s32[1]{0:T(128)S(6)} %sub.3.half_ref, bf16[1,32,8192]{2,1,0:T(8,128)(2,1)S(1)} %copy-done.1, f32[1,32,8192]{2,1,0:T(8,128)S(1)} %copy-done, f32[32,8192]{1,0:T(8,128)S(1)} %copy-done.2, ...), custom_call_target="tpu_custom_call", output_to_operand_aliasing={{0}: (5, {}), {1}: (6, {}), {2}: (7, {})} | custom-call | flops 100000 | bytes 100000 | tf_op jit(solution)/shard_map/pallas_call | solution.py:330
  (2 shorter events, 0.0 us)
Async XLA Ops:
  3.6 10.6 %copy-start.3 = (f32[64,512]{1,0:T(8,128)S(1)}, f32[64,512]{1,0:T(8,128)}, u32[]{:S(2)}) copy-start(f32[64,512]{1,0:T(8,128)} %q_ref.1) | copy-start | bytes 393220
  3.6 27.9 %all-to-all-start = ((f32[32,32,256]{2,1,0:T(8,128)}), f32[32,32,256]{2,1,0:T(8,128)S(1)}, u32[]{:S(2)}, u32[]{:S(2)}) async-start(f32[32,32,256]{2,1,0:T(8,128)} %shard_map.67), calls=%async_computation | async-start | bytes 2097152 | tf_op jit(solution)/shard_map/all_to_all | solution.py:273
  14.3 15.2 %collective-permute-start = (f32[64,256]{1,0:T(8,128)S(1)}, f32[64,256]{1,0:T(8,128)S(1)}, u32[]{:S(2)}, u32[]{:S(2)}) collective-permute-start(f32[64,256]{1,0:T(8,128)S(1)} %shard_map.68), channel_id=1, source_target_pairs={{0,0},{1,1},{2,2},{3,3},{4,4},{5,5},{6,6},{7,7},{8,8},{9,9},{10,10... | collective-permute-start | bytes 196616 | tf_op jit(solution)/shard_map/ppermute | solution.py:286
  32.5 18.1 %all-to-all-start.1 = ((f32[32,24,128]{2,1,0:T(8,128)}), f32[32,24,128]{2,1,0:T(8,128)S(1)}, u32[]{:S(2)}, u32[]{:S(2)}) async-start(f32[32,24,128]{2,1,0:T(8,128)} %shard_map.70), calls=%async_computation.1 | async-start | bytes 786432 | tf_op jit(solution)/shard_map/all_to_all | solution.py:273
  50.9 53.1 %copy-start.2 = (f32[32,8192]{1,0:T(8,128)S(1)}, f32[32,8192]{1,0:T(8,128)}, u32[]{:S(2)}) copy-start(f32[32,8192]{1,0:T(8,128)} %momentum.3) | copy-start | bytes 3145732
  77.7 26.4 %copy-start = (f32[1,32,8192]{2,1,0:T(8,128)S(1)}, f32[1,32,8192]{2,1,0:T(8,128)}, u32[]{:S(2)}) copy-start(f32[1,32,8192]{2,1,0:T(8,128)} %feedback.5) | copy-start | bytes 3145732
  80.9 23.2 %copy-start.1 = (bf16[1,32,8192]{2,1,0:T(8,128)(2,1)S(1)}, bf16[1,32,8192]{2,1,0:T(8,128)(2,1)}, u32[]{:S(2)}) copy-start(bf16[1,32,8192]{2,1,0:T(8,128)(2,1)} %gradient.5) | copy-start | bytes 1572868
  94.3 11.9 %collective-permute-start.1 = (f32[16,72,128]{2,1,0:T(8,128)S(1)}, f32[16,72,128]{2,1,0:T(8,128)S(1)}, u32[]{:S(2)}, u32[]{:S(2)}) collective-permute-start(f32[16,72,128]{2,1,0:T(8,128)S(1)} %all_to_all.15.parts), channel_id=1, source_target_pairs={{0,16},{16,0},{32,48},{48,32},{64,80},{80,64},{96,112},{112,96},{1... | collective-permute-start | bytes 1769480 | tf_op jit(solution)/shard_map/ppermute | solution.py:277

commit v10 on v9

--- a/solution.py
+++ b/solution.py
@@ -92,15 +92,17 @@
             merged[place] = gradient_part[:, lanes].astype(jnp.float32) + feedback_part[:, lanes]
             chip = (shard - t + (4 - half) * (TP // 2)) % TP
             results.append(
-                pltpu.make_async_copy(merged.at[place], out.at[chip * 2 + half], sems.at[2, place])
+                pltpu.make_async_copy(
+                    merged.at[place], out.at[chip * 2 + (half ^ (t & 1))], sems.at[2, place]
+                )
             )
             results[place].start()
     for copy in results:
         copy.wait()
 
 
-def half_kernel(core_ref, q_ref, out):
-    out[...] = jnp.where(core_ref[0] == 0, q_ref[:, :SPAN], q_ref[:, SPAN:])
+def half_kernel(half_ref, q_ref, out):
+    out[...] = jnp.where(half_ref[0] == 0, q_ref[:, :SPAN], q_ref[:, SPAN:])
 
 
 def twice_kernel(q_part, out):
@@ -132,6 +134,7 @@
 
 
 def project_kernel(core_ref, chip_ref, t_ref, parts, out):
+    half = core_ref[0] ^ (t_ref[0] & 1)
     packed = parts[0, :HALF, :]
     for d in range(1, DP):
         packed = packed + parts[d, :HALF, :]
@@ -140,7 +143,7 @@
     for th in range(TP // GROUP):
         pieces = []
         for tl in range(GROUP):
-            source = (th * GROUP + tl - t_ref[0] + (4 - core_ref[0]) * (TP // 2)) % TP
+            source = (th * GROUP + tl - t_ref[0] + (4 - half) * (TP // 2)) % TP
             pieces.append(parts[source * 2 + core_ref[0], HALF:, :])
         pieces = swap_blocks(pieces)
         start = HALF + th * ROWS
@@ -277,13 +280,20 @@
     return lax.ppermute(parts, "dp", [(d, d ^ 1) for d in range(DP)])
 
 
-def permute(parts, target):
+def fetch_shards(parts):
     pairs = []
     for d in range(DP):
         for t in range(TP):
-            chip, plane = target(d // 2, d % 2, t)
-            pairs.append((d * TP + t, (chip * 2 + d % 2) * TP + plane))
+            plane = (t + d // 2 + (d & 1 ^ t & 1) * (TP // 2)) % TP
+            pairs.append((d * TP + plane, d * TP + t))
     return lax.ppermute(parts, ("dp", "tensor"), pairs)
+
+
+def gather_lines(parts):
+    lines = [
+        [(chip * 2 + (t + v) % 2) * TP + t for t in range(TP)] for chip in range(CHIPS) for v in range(2)
+    ]
+    return lax.all_gather(parts, ("dp", "tensor"), axis_index_groups=lines)
 
 
 def on_device(gradient, feedback, momentum, q_previous):
@@ -291,8 +301,9 @@
     core, chip = d & 1, d >> 1
     t = lax.axis_index("tensor").reshape(1)
     chips = [list(range(c, DP, 2)) for c in range(2)]
-    q_part = local(half_kernel, (RANK, SPAN), scalars=1)(core, q_previous)[0]
-    q_part = permute(q_part, lambda chip, c, plane: (chip, (plane - chip - c * (TP // 2)) % TP))
+    half = core ^ (t & 1)
+    q_part = local(half_kernel, (RANK, SPAN), scalars=1)(core ^ ((t - chip) & 1), q_previous)[0]
+    q_part = fetch_shards(q_part)
     q_part = local(twice_kernel, (2 * RANK, SPAN), flops=100_000)(q_part)[0]
     merged = local(
         merge_kernel,
@@ -313,7 +324,7 @@
     factor = local(factor_kernel, (DP, HALF + 8, LANES), inputs=2)(merged, q_part)[0]
     factor = exchange(factor, "dp")
     parts = local(project_kernel, (HALF + 2 * ROWS, LANES), scalars=3)(core, chip, t, factor)[0]
-    parts = lax.all_gather(parts, "tensor")
+    parts = gather_lines(parts)
     own = local(solve_kernel, (CHIPS, 2 * ROWS + 8, LANES), scalars=1)(t, parts)[0]
     own = exchange(own, "dp", chips)
     other = swap_cores(own)
@@ -326,7 +337,7 @@
     ]
     outs = local(
         finish_own_kernel, *shapes, scalars=1, inputs=4, scratch=scratch, far_out=True
-    )(core, gradient, feedback, momentum, own)
+    )(half, gradient, feedback, momentum, own)
     outs = local(
         finish_other_kernel,
         *shapes,
@@ -336,7 +347,7 @@
         far=(4, 5, 6),
         far_out=True,
         alias={5: 0, 6: 1, 7: 2},
-    )(1 - core, gradient, feedback, momentum, other, *outs)
+    )(1 - half, gradient, feedback, momentum, other, *outs)
     return tuple(outs)
 
 

time: 109 us -> 107 us (0.982)
  blocking collectives: 40.1 us -> 63.4 us
  starting transfers between devices: 41.8 us -> 27.9 us
  waiting for transfers between devices: 13.8 us -> 3.66 us
    all_to_all x1 -> x2, blocking collectives: 13.4 us -> 31.1 us  [exchange(): lax.all_to_all(parts, axis, 0, 0, tiled=True, axis_index_groups=groups)]
    all_to_all x2 -> x1, waiting for transfers between devices: 12.2 us -> 2.01 us  [exchange(): lax.all_to_all(parts, axis, 0, 0, tiled=True, axis_index_groups=groups)]
    all_to_all x2 -> x1, starting transfers between devices: 18.5 us -> 10.6 us  [exchange(): lax.all_to_all(parts, axis, 0, 0, tiled=True, axis_index_groups=groups)]
    ppermute x1, starting transfers between devices: 9.74 us -> 3.72 us  [swap_cores(): return lax.ppermute(parts, 'dp', [(d, d ^ 1) for d in range(DP)])]
    all_gather x1, blocking collectives: 26.7 us -> 32.3 us  [gather_lines(): return lax.all_gather(parts, ('dp', 'tensor'), axis_index_groups=lines)]
  transfers between devices with their start and end apart: 4 -> 3, of which waited for: 3 -> 2; matrix products, arithmetic and copies ran while one was open for 0% -> 0% of each run, Pallas kernels for 2% -> 2%
where the time goes in v10:
time: 107 us
  blocking collectives  63.4 us (59%)
  starting transfers between devices  27.9 us (26%)
  Pallas kernels  10.9 us (10%)
  waiting for transfers between devices  3.66 us (3%)
    all_gather x1, blocking collectives, gather_lines(): return lax.all_gather(parts, ('dp', 'tensor'), axis_index_groups=lines)  32.3 us
    all_to_all x2, blocking collectives, exchange(): lax.all_to_all(parts, axis, 0, 0, tiled=True, axis_index_groups=groups)  31.1 us
    ppermute x1, starting transfers between devices, fetch_shards(): return lax.ppermute(parts, ('dp', 'tensor'), pairs)  13.6 us
    all_to_all x1, starting transfers between devices, exchange(): lax.all_to_all(parts, axis, 0, 0, tiled=True, axis_index_groups=groups)  10.6 us
    ppermute x1, starting transfers between devices, swap_cores(): return lax.ppermute(parts, 'dp', [(d, d ^ 1) for d in range(DP)])  3.72 us
    pallas_call x1, Pallas kernels, on_device(): local(solve_kernel, (CHIPS, 2 * ROWS + 8, LANES), scalars=1)(t, parts)[0]  3.22 us
    pallas_call x1, Pallas kernels, on_device(): local(merge_kernel, (DP, ROWS, SPAN), scalars=1, inputs=2, far=(0, 1), fa...  2.96 us
  transfers between devices with their start and end apart: 3, of which 2 were waited for; matrix products, arithmetic and copies ran while one was open for 0% of the time, Pallas kernels for 2%

profile of v10, /device:TPU:1, one launch (start us, length us, event | category | flops | bytes accessed | tf_op | source)
XLA Modules:
  0.0 106.7 jit_solution(2206432901407455295)
XLA Ops:
  0.6 3.0 %shard_map.67 = f32[32,32,256]{2,1,0:T(8,128)} custom-call(s32[1]{0:T(128)} %bitcast.1.t_ref, bf16[1,32,8192]{2,1,0:T(8,128)(2,1)} %gradient.5, f32[1,32,8192]{2,1,0:T(8,128)} %feedback.5), custom_call_target="tpu_custom_call" | custom-call | flops 100000 | bytes 100000 | tf_op jit(solution)/shard_map/pallas_call | solution.py:308
  3.6 0.0 copy-start.3
  3.6 10.6 %all-to-all-start = ((f32[32,32,256]{2,1,0:T(8,128)}), f32[32,32,256]{2,1,0:T(8,128)S(1)}, u32[]{:S(2)}, u32[]{:S(2)}) async-start(f32[32,32,256]{2,1,0:T(8,128)} %shard_map.67), calls=%async_computation | async-start | bytes 2097152 | tf_op jit(solution)/shard_map/all_to_all | solution.py:276
  14.2 0.0 copy-done.3
  14.3 13.6 %collective-permute-start = (f32[64,256]{1,0:T(8,128)S(1)}, f32[64,256]{1,0:T(8,128)S(1)}, u32[]{:S(2)}, u32[]{:S(2)}) collective-permute-start(f32[64,256]{1,0:T(8,128)S(1)} %shard_map.68), channel_id=1, source_target_pairs={{0,0},{9,1},{2,2},{11,3},{4,4},{13,5},{6,6},{15,7},{8,8},{1,9},{10... | collective-permute-start | bytes 196616 | tf_op jit(solution)/shard_map/ppermute | solution.py:289
  27.8 1.6 %collective-permute-done.q_part = f32[64,256]{1,0:T(8,128)S(1)} collective-permute-done((f32[64,256]{1,0:T(8,128)S(1)}, f32[64,256]{1,0:T(8,128)S(1)}, u32[]{:S(2)}, u32[]{:S(2)}) %collective-permute-start) | collective-permute-done | bytes 65568 | tf_op jit(solution)/shard_map/ppermute | solution.py:289
  29.5 2.0 %all-to-all-done.merged = f32[32,32,256]{2,1,0:T(8,128)S(1)} async-done(((f32[32,32,256]{2,1,0:T(8,128)}), f32[32,32,256]{2,1,0:T(8,128)S(1)}, u32[]{:S(2)}, u32[]{:S(2)}) %all-to-all-start) | async-done | bytes 1048608 | tf_op jit(solution)/shard_map/all_to_all | solution.py:276
  31.5 0.3 shard_map.70
  31.8 16.3 %all_to_all.15.parts = f32[32,24,128]{2,1,0:T(8,128)S(1)} all-to-all(f32[32,24,128]{2,1,0:T(8,128)S(1)} %shard_map.70), channel_id=1, replica_groups=mesh['dp'=32,'tensor'=16] {'dp'}, dimensions={0} | all-to-all | bytes 786432 | tf_op jit(solution)/shard_map/all_to_all | solution.py:276
  48.1 0.3 shard_map.71
  48.4 0.0 copy-start.2
  48.4 32.3 %all-gather = f32[1280,128]{1,0:T(8,128)S(1)} all-gather(f32[80,128]{1,0:T(8,128)S(1)} %shard_map.71), channel_id=2, replica_groups={{0,17,2,19,4,21,6,23,8,25,10,27,12,29,14,31},{16,1,18,3,20,5,22,7,24,9,..., dimensions={0}, use_global_device_ids=true | all-gather | bytes 696320 | tf_op jit(solution)/shard_map/all_gather | solution.py:296
  80.7 0.0 copy-start
  80.7 3.2 %shard_map.72 = f32[16,72,128]{2,1,0:T(8,128)S(1)} custom-call(s32[1]{0:T(128)} %bitcast.1.t_ref, f32[16,80,128]{2,1,0:T(8,128)S(1)} %bitcast.4), custom_call_target="tpu_custom_call" | custom-call | flops 100000 | bytes 100000 | tf_op jit(solution)/shard_map/pallas_call | solution.py:328
  84.0 0.0 copy-start.1
  84.0 14.8 %all_to_all.16.parts = f32[16,72,128]{2,1,0:T(8,128)S(1)} all-to-all(f32[16,72,128]{2,1,0:T(8,128)S(1)} %shard_map.72), channel_id=1, replica_groups={{0,32,64,96,128,160,192,224,256,288,320,352,384,416,448,480},{16,48,80,..., dimensions={0} | all-to-all | bytes 1179648 | tf_op jit(solution)/shard_map/all_to_all | solution.py:276
  98.7 3.7 %collective-permute-start.1 = (f32[16,72,128]{2,1,0:T(8,128)S(1)}, f32[16,72,128]{2,1,0:T(8,128)S(1)}, u32[]{:S(2)}, u32[]{:S(2)}) collective-permute-start(f32[16,72,128]{2,1,0:T(8,128)S(1)} %all_to_all.16.parts), channel_id=1, source_target_pairs={{0,16},{16,0},{32,48},{48,32},{64,80},{80,64},{96,112},{112,96},{1... | collective-permute-start | bytes 1769480 | tf_op jit(solution)/shard_map/ppermute | solution.py:280
  102.5 0.0 copy-done.2
  102.5 0.0 copy-done
  102.5 0.0 copy-done.1
  102.5 2.1 %shard_map.73 = (f32[1,32,8192]{2,1,0:T(8,128)}, f32[32,8192]{1,0:T(8,128)}, f32[64,512]{1,0:T(8,128)}) custom-call(s32[1]{0:T(128)S(6)} %xor.6.half_ref, bf16[1,32,8192]{2,1,0:T(8,128)(2,1)S(1)} %copy-done.1, f32[1,32,8192]{2,1,0:T(8,128)S(1)} %copy-done, f32[32,8192]{1,0:T(8,128)S(1)} %copy-done.2, f32[16,72,128]{2,1,0:T(8,128)S(1)} %all_to_all.16.parts), custom_call_target="tpu_custom_call" | custom-call | flops 100000 | bytes 100000 | tf_op jit(solution)/shard_map/pallas_call | solution.py:338
  104.6 0.0 collective-permute-done.1.parts
  104.6 2.1 %shard_map.74 = (f32[1,32,8192]{2,1,0:T(8,128)}, f32[32,8192]{1,0:T(8,128)}, f32[64,512]{1,0:T(8,128)}) custom-call(s32[1]{0:T(128)S(6)} %sub.6.half_ref, bf16[1,32,8192]{2,1,0:T(8,128)(2,1)S(1)} %copy-done.1, f32[1,32,8192]{2,1,0:T(8,128)S(1)} %copy-done, f32[32,8192]{1,0:T(8,128)S(1)} %copy-done.2, ...), custom_call_target="tpu_custom_call", output_to_operand_aliasing={{0}: (5, {}), {1}: (6, {}), {2}: (7, {})} | custom-call | flops 100000 | bytes 100000 | tf_op jit(solution)/shard_map/pallas_call | solution.py:341
  (2 shorter events, 0.0 us)
Async XLA Ops:
  3.6 10.6 %copy-start.3 = (f32[64,512]{1,0:T(8,128)S(1)}, f32[64,512]{1,0:T(8,128)}, u32[]{:S(2)}) copy-start(f32[64,512]{1,0:T(8,128)} %q_ref.1) | copy-start | bytes 393220
  3.6 27.9 %all-to-all-start = ((f32[32,32,256]{2,1,0:T(8,128)}), f32[32,32,256]{2,1,0:T(8,128)S(1)}, u32[]{:S(2)}, u32[]{:S(2)}) async-start(f32[32,32,256]{2,1,0:T(8,128)} %shard_map.67), calls=%async_computation | async-start | bytes 2097152 | tf_op jit(solution)/shard_map/all_to_all | solution.py:276
  14.3 15.2 %collective-permute-start = (f32[64,256]{1,0:T(8,128)S(1)}, f32[64,256]{1,0:T(8,128)S(1)}, u32[]{:S(2)}, u32[]{:S(2)}) collective-permute-start(f32[64,256]{1,0:T(8,128)S(1)} %shard_map.68), channel_id=1, source_target_pairs={{0,0},{9,1},{2,2},{11,3},{4,4},{13,5},{6,6},{15,7},{8,8},{1,9},{10... | collective-permute-start | bytes 196616 | tf_op jit(solution)/shard_map/ppermute | solution.py:289
  48.4 54.1 %copy-start.2 = (f32[32,8192]{1,0:T(8,128)S(1)}, f32[32,8192]{1,0:T(8,128)}, u32[]{:S(2)}) copy-start(f32[32,8192]{1,0:T(8,128)} %momentum.3) | copy-start | bytes 3145732
  80.7 21.7 %copy-start = (f32[1,32,8192]{2,1,0:T(8,128)S(1)}, f32[1,32,8192]{2,1,0:T(8,128)}, u32[]{:S(2)}) copy-start(f32[1,32,8192]{2,1,0:T(8,128)} %feedback.5) | copy-start | bytes 3145732
  84.0 18.5 %copy-start.1 = (bf16[1,32,8192]{2,1,0:T(8,128)(2,1)S(1)}, bf16[1,32,8192]{2,1,0:T(8,128)(2,1)}, u32[]{:S(2)}) copy-start(bf16[1,32,8192]{2,1,0:T(8,128)(2,1)} %gradient.5) | copy-start | bytes 1572868
  98.7 5.8 %collective-permute-start.1 = (f32[16,72,128]{2,1,0:T(8,128)S(1)}, f32[16,72,128]{2,1,0:T(8,128)S(1)}, u32[]{:S(2)}, u32[]{:S(2)}) collective-permute-start(f32[16,72,128]{2,1,0:T(8,128)S(1)} %all_to_all.16.parts), channel_id=1, source_target_pairs={{0,16},{16,0},{32,48},{48,32},{64,80},{80,64},{96,112},{112,96},{1... | collective-permute-start | bytes 1769480 | tf_op jit(solution)/shard_map/ppermute | solution.py:280

commit v11 on v10

--- a/solution.py
+++ b/solution.py
@@ -18,7 +18,6 @@
 BLOCK = 16
 GROUP = LANES // BLOCK
 SPAN = BLOCK * TP
-CHUNKS = 4
 SHARD = DP * BLOCK
 CHIPS = DP // 2
 HALF = ROWS // 2
@@ -64,41 +63,16 @@
     return pl.ds(pl.multiple_of(shard * SHARD + half * SPAN, SPAN), SPAN)
 
 
-def merge_kernel(t_ref, gradient, feedback, out, gradient_part, feedback_part, merged, sems):
+def merge_kernel(t_ref, gradient, feedback, out):
     t = t_ref[0]
-    wide = TP // CHUNKS * SHARD
-    copies = []
-    for chunk in range(CHUNKS):
-        lanes = pl.ds(chunk * wide, wide)
-        copies.append(
-            [
-                pltpu.make_async_copy(source.at[0, :, lanes], target.at[:, lanes], sems.at[i, chunk])
-                for i, (source, target) in enumerate(
-                    ((gradient, gradient_part), (feedback, feedback_part))
-                )
-            ]
-        )
-        for copy in copies[chunk]:
-            copy.start()
-    results = []
     for shard in range(TP):
-        if shard % (TP // CHUNKS) == 0:
-            for copy in copies[shard // (TP // CHUNKS)]:
-                copy.wait()
         for half in range(2):
             start = shard * SHARD + half * SPAN
             lanes = slice(start, start + SPAN)
-            place = shard * 2 + half
-            merged[place] = gradient_part[:, lanes].astype(jnp.float32) + feedback_part[:, lanes]
             chip = (shard - t + (4 - half) * (TP // 2)) % TP
-            results.append(
-                pltpu.make_async_copy(
-                    merged.at[place], out.at[chip * 2 + (half ^ (t & 1))], sems.at[2, place]
-                )
+            out[chip * 2 + (half ^ (t & 1))] = (
+                gradient[0, :, lanes].astype(jnp.float32) + feedback[0, :, lanes]
             )
-            results[place].start()
-    for copy in results:
-        copy.wait()
 
 
 def half_kernel(half_ref, q_ref, out):
@@ -305,21 +279,9 @@
     q_part = local(half_kernel, (RANK, SPAN), scalars=1)(core ^ ((t - chip) & 1), q_previous)[0]
     q_part = fetch_shards(q_part)
     q_part = local(twice_kernel, (2 * RANK, SPAN), flops=100_000)(q_part)[0]
-    merged = local(
-        merge_kernel,
-        (DP, ROWS, SPAN),
-        scalars=1,
-        inputs=2,
-        far=(0, 1),
-        far_out=True,
-        room=60,
-        scratch=[
-            pltpu.VMEM(gradient.shape[1:], jnp.bfloat16),
-            pltpu.VMEM(feedback.shape[1:], jnp.float32),
-            pltpu.VMEM((DP, ROWS, SPAN), jnp.float32),
-            pltpu.SemaphoreType.DMA((3, DP)),
-        ],
-    )(t, gradient, feedback)[0]
+    merged = local(merge_kernel, (DP, ROWS, SPAN), scalars=1, inputs=2, room=60)(
+        t, gradient, feedback
+    )[0]
     merged = exchange(merged, "dp")
     factor = local(factor_kernel, (DP, HALF + 8, LANES), inputs=2)(merged, q_part)[0]
     factor = exchange(factor, "dp")

time: 107 us -> 107 us (level)
  no operation moved by 1% of the time
where the time goes in v11:
time: 107 us; the launch traced here: 106 us
  blocking collectives  63.4 us (59%)
  starting transfers between devices  27.9 us (26%)
  Pallas kernels  10.4 us (10%)
  waiting for transfers between devices  3.66 us (3%)
    all_gather x1, blocking collectives, gather_lines(): return lax.all_gather(parts, ('dp', 'tensor'), axis_index_groups=lines)  32.3 us
    all_to_all x2, blocking collectives, exchange(): lax.all_to_all(parts, axis, 0, 0, tiled=True, axis_index_groups=groups)  31.1 us
    ppermute x1, starting transfers between devices, fetch_shards(): return lax.ppermute(parts, ('dp', 'tensor'), pairs)  13.6 us
    all_to_all x1, starting transfers between devices, exchange(): lax.all_to_all(parts, axis, 0, 0, tiled=True, axis_index_groups=groups)  10.6 us
    ppermute x1, starting transfers between devices, swap_cores(): return lax.ppermute(parts, 'dp', [(d, d ^ 1) for d in range(DP)])  3.72 us
    pallas_call x1, Pallas kernels, on_device(): local(solve_kernel, (CHIPS, 2 * ROWS + 8, LANES), scalars=1)(t, parts)[0]  3.21 us
    pallas_call x1, Pallas kernels, on_device(): local(merge_kernel, (DP, ROWS, SPAN), scalars=1, inputs=2, room=60)  2.51 us
  transfers between devices with their start and end apart: 3, of which 2 were waited for; matrix products, arithmetic and copies ran while one was open for 0% of the time, Pallas kernels for 2%

profile of v11, /device:TPU:1, one launch (start us, length us, event | category | flops | bytes accessed | tf_op | source)
XLA Modules:
  0.0 106.2 jit_solution(13569591454204873117)
XLA Ops:
  0.6 2.5 %shard_map.67 = f32[32,32,256]{2,1,0:T(8,128)} custom-call(s32[1]{0:T(128)} %bitcast.1.t_ref, bf16[1,32,8192]{2,1,0:T(8,128)(2,1)} %gradient.5, f32[1,32,8192]{2,1,0:T(8,128)} %feedback.5), custom_call_target="tpu_custom_call" | custom-call | flops 100000 | bytes 100000 | tf_op jit(solution)/shard_map/pallas_call | solution.py:282
  3.1 0.0 copy-start.3
  3.1 10.6 %all-to-all-start = ((f32[32,32,256]{2,1,0:T(8,128)}), f32[32,32,256]{2,1,0:T(8,128)S(1)}, u32[]{:S(2)}, u32[]{:S(2)}) async-start(f32[32,32,256]{2,1,0:T(8,128)} %shard_map.67), calls=%async_computation | async-start | bytes 2097152 | tf_op jit(solution)/shard_map/all_to_all | solution.py:250
  13.8 0.0 copy-done.3
  13.8 13.6 %collective-permute-start = (f32[64,256]{1,0:T(8,128)S(1)}, f32[64,256]{1,0:T(8,128)S(1)}, u32[]{:S(2)}, u32[]{:S(2)}) collective-permute-start(f32[64,256]{1,0:T(8,128)S(1)} %shard_map.68), channel_id=1, source_target_pairs={{0,0},{9,1},{2,2},{11,3},{4,4},{13,5},{6,6},{15,7},{8,8},{1,9},{10... | collective-permute-start | bytes 196616 | tf_op jit(solution)/shard_map/ppermute | solution.py:263
  27.4 1.6 %collective-permute-done.q_part = f32[64,256]{1,0:T(8,128)S(1)} collective-permute-done((f32[64,256]{1,0:T(8,128)S(1)}, f32[64,256]{1,0:T(8,128)S(1)}, u32[]{:S(2)}, u32[]{:S(2)}) %collective-permute-start) | collective-permute-done | bytes 65568 | tf_op jit(solution)/shard_map/ppermute | solution.py:263
  29.0 2.0 %all-to-all-done.merged = f32[32,32,256]{2,1,0:T(8,128)S(1)} async-done(((f32[32,32,256]{2,1,0:T(8,128)}), f32[32,32,256]{2,1,0:T(8,128)S(1)}, u32[]{:S(2)}, u32[]{:S(2)}) %all-to-all-start) | async-done | bytes 1048608 | tf_op jit(solution)/shard_map/all_to_all | solution.py:250
  31.0 0.3 shard_map.70
  31.3 16.3 %all_to_all.15.parts = f32[32,24,128]{2,1,0:T(8,128)S(1)} all-to-all(f32[32,24,128]{2,1,0:T(8,128)S(1)} %shard_map.70), channel_id=1, replica_groups=mesh['dp'=32,'tensor'=16] {'dp'}, dimensions={0} | all-to-all | bytes 786432 | tf_op jit(solution)/shard_map/all_to_all | solution.py:250
  47.6 0.3 shard_map.71
  47.9 0.0 copy-start.2
  47.9 32.3 %all-gather = f32[1280,128]{1,0:T(8,128)S(1)} all-gather(f32[80,128]{1,0:T(8,128)S(1)} %shard_map.71), channel_id=2, replica_groups={{0,17,2,19,4,21,6,23,8,25,10,27,12,29,14,31},{16,1,18,3,20,5,22,7,24,9,..., dimensions={0}, use_global_device_ids=true | all-gather | bytes 696320 | tf_op jit(solution)/shard_map/all_gather | solution.py:270
  80.3 0.0 copy-start
  80.3 3.2 %shard_map.72 = f32[16,72,128]{2,1,0:T(8,128)S(1)} custom-call(s32[1]{0:T(128)} %bitcast.1.t_ref, f32[16,80,128]{2,1,0:T(8,128)S(1)} %bitcast.4), custom_call_target="tpu_custom_call" | custom-call | flops 100000 | bytes 100000 | tf_op jit(solution)/shard_map/pallas_call | solution.py:290
  83.5 0.0 copy-start.1
  83.5 14.8 %all_to_all.16.parts = f32[16,72,128]{2,1,0:T(8,128)S(1)} all-to-all(f32[16,72,128]{2,1,0:T(8,128)S(1)} %shard_map.72), channel_id=1, replica_groups={{0,32,64,96,128,160,192,224,256,288,320,352,384,416,448,480},{16,48,80,..., dimensions={0} | all-to-all | bytes 1179648 | tf_op jit(solution)/shard_map/all_to_all | solution.py:250
  98.3 3.7 %collective-permute-start.1 = (f32[16,72,128]{2,1,0:T(8,128)S(1)}, f32[16,72,128]{2,1,0:T(8,128)S(1)}, u32[]{:S(2)}, u32[]{:S(2)}) collective-permute-start(f32[16,72,128]{2,1,0:T(8,128)S(1)} %all_to_all.16.parts), channel_id=1, source_target_pairs={{0,16},{16,0},{32,48},{48,32},{64,80},{80,64},{96,112},{112,96},{1... | collective-permute-start | bytes 1769480 | tf_op jit(solution)/shard_map/ppermute | solution.py:254
  102.0 0.0 copy-done.2
  102.0 0.0 copy-done
  102.0 0.0 copy-done.1
  102.0 2.1 %shard_map.73 = (f32[1,32,8192]{2,1,0:T(8,128)}, f32[32,8192]{1,0:T(8,128)}, f32[64,512]{1,0:T(8,128)}) custom-call(s32[1]{0:T(128)S(6)} %xor.6.half_ref, bf16[1,32,8192]{2,1,0:T(8,128)(2,1)S(1)} %copy-done.1, f32[1,32,8192]{2,1,0:T(8,128)S(1)} %copy-done, f32[32,8192]{1,0:T(8,128)S(1)} %copy-done.2, f32[16,72,128]{2,1,0:T(8,128)S(1)} %all_to_all.16.parts), custom_call_target="tpu_custom_call" | custom-call | flops 100000 | bytes 100000 | tf_op jit(solution)/shard_map/pallas_call | solution.py:300
  104.1 0.0 collective-permute-done.1.parts
  104.1 2.1 %shard_map.74 = (f32[1,32,8192]{2,1,0:T(8,128)}, f32[32,8192]{1,0:T(8,128)}, f32[64,512]{1,0:T(8,128)}) custom-call(s32[1]{0:T(128)S(6)} %sub.6.half_ref, bf16[1,32,8192]{2,1,0:T(8,128)(2,1)S(1)} %copy-done.1, f32[1,32,8192]{2,1,0:T(8,128)S(1)} %copy-done, f32[32,8192]{1,0:T(8,128)S(1)} %copy-done.2, ...), custom_call_target="tpu_custom_call", output_to_operand_aliasing={{0}: (5, {}), {1}: (6, {}), {2}: (7, {})} | custom-call | flops 100000 | bytes 100000 | tf_op jit(solution)/shard_map/pallas_call | solution.py:303
  (2 shorter events, 0.0 us)
Async XLA Ops:
  3.1 10.6 %copy-start.3 = (f32[64,512]{1,0:T(8,128)S(1)}, f32[64,512]{1,0:T(8,128)}, u32[]{:S(2)}) copy-start(f32[64,512]{1,0:T(8,128)} %q_ref.1) | copy-start | bytes 393220
  3.1 27.9 %all-to-all-start = ((f32[32,32,256]{2,1,0:T(8,128)}), f32[32,32,256]{2,1,0:T(8,128)S(1)}, u32[]{:S(2)}, u32[]{:S(2)}) async-start(f32[32,32,256]{2,1,0:T(8,128)} %shard_map.67), calls=%async_computation | async-start | bytes 2097152 | tf_op jit(solution)/shard_map/all_to_all | solution.py:250
  13.8 15.2 %collective-permute-start = (f32[64,256]{1,0:T(8,128)S(1)}, f32[64,256]{1,0:T(8,128)S(1)}, u32[]{:S(2)}, u32[]{:S(2)}) collective-permute-start(f32[64,256]{1,0:T(8,128)S(1)} %shard_map.68), channel_id=1, source_target_pairs={{0,0},{9,1},{2,2},{11,3},{4,4},{13,5},{6,6},{15,7},{8,8},{1,9},{10... | collective-permute-start | bytes 196616 | tf_op jit(solution)/shard_map/ppermute | solution.py:263
  47.9 54.1 %copy-start.2 = (f32[32,8192]{1,0:T(8,128)S(1)}, f32[32,8192]{1,0:T(8,128)}, u32[]{:S(2)}) copy-start(f32[32,8192]{1,0:T(8,128)} %momentum.3) | copy-start | bytes 3145732
  80.3 21.7 %copy-start = (f32[1,32,8192]{2,1,0:T(8,128)S(1)}, f32[1,32,8192]{2,1,0:T(8,128)}, u32[]{:S(2)}) copy-start(f32[1,32,8192]{2,1,0:T(8,128)} %feedback.5) | copy-start | bytes 3145732
  83.5 18.5 %copy-start.1 = (bf16[1,32,8192]{2,1,0:T(8,128)(2,1)S(1)}, bf16[1,32,8192]{2,1,0:T(8,128)(2,1)}, u32[]{:S(2)}) copy-start(bf16[1,32,8192]{2,1,0:T(8,128)(2,1)} %gradient.5) | copy-start | bytes 1572868
  98.3 5.8 %collective-permute-start.1 = (f32[16,72,128]{2,1,0:T(8,128)S(1)}, f32[16,72,128]{2,1,0:T(8,128)S(1)}, u32[]{:S(2)}, u32[]{:S(2)}) collective-permute-start(f32[16,72,128]{2,1,0:T(8,128)S(1)} %all_to_all.16.parts), channel_id=1, source_target_pairs={{0,16},{16,0},{32,48},{48,32},{64,80},{80,64},{96,112},{112,96},{1... | collective-permute-start | bytes 1769480 | tf_op jit(solution)/shard_map/ppermute | solution.py:254

commit v12 on v11

--- a/solution.py
+++ b/solution.py
@@ -45,6 +45,18 @@
             parts[i] = jnp.where(upper, pltpu.roll(b, step * BLOCK, 1), a)
             parts[i | step] = jnp.where(upper, b, pltpu.roll(a, LANES - step * BLOCK, 1))
     return parts
+
+
+def merge_blocks(parts):
+    block = lax.broadcasted_iota(jnp.int32, parts[0].shape, 1) // BLOCK
+    at = [block == place for place in range(GROUP)]
+    merged = []
+    for tl in range(GROUP):
+        part = parts[(GROUP - tl) % GROUP]
+        for place in range(1, GROUP):
+            part = jnp.where(at[place], parts[(place - tl) % GROUP], part)
+        merged.append(pltpu.roll(part, (GROUP - tl) * BLOCK, 1) if tl else part)
+    return merged
 
 
 def gather_blocks(matrix, lane_block):
@@ -161,26 +173,27 @@
     return jnp.concatenate(work, axis=0)[:, RANK:]
 
 
-def solve_kernel(t_ref, parts, out):
+def solve_kernel(chip_ref, t_ref, parts, out):
     t = t_ref[0]
     whole = unpack_rows(parts[:, :HALF, :].reshape(TP * HALF, LANES))
     whole_t = whole.T
     inverse = inverse_triangle(dot(whole_t, whole, 1, 0))
     basis = dot(unpack_rows(parts[t, :HALF, :]), inverse, 1, 1)
-    approx, q_tiles = [], []
+    tiles = []
     for th in range(TP // GROUP):
         start = HALF + th * ROWS
-        sums = jnp.concatenate(
-            [
-                parts[:, start + h * HALF : start + (h + 1) * HALF, :].reshape(TP * HALF, LANES)
-                for h in range(2)
-            ],
-            axis=0,
+        halves = [parts[:, start + h * HALF : start + (h + 1) * HALF, :] for h in range(2)]
+        tiles.append(
+            jnp.concatenate([half.reshape(TP * HALF, LANES) for half in halves], axis=0)
         )
-        q_tiles.append(dot(inverse, dot(whole_t, sums, 1, 0), 1, 0) * (1.0 / DP))
-        approx.append(dot(basis, q_tiles[th], 1, 0))
-    mine = jnp.where(t // GROUP == 0, q_tiles[0], q_tiles[1])
-    message = jnp.concatenate(approx + [gather_blocks(mine, t % GROUP)], axis=0)
+    sums = jnp.concatenate(tiles, axis=1)
+    q_tile = dot(inverse, dot(whole_t, sums, 1, 0), 1, 0) * (1.0 / DP)
+    approx = dot(basis, q_tile, 1, 0)
+    mine = jnp.where(t // GROUP == 0, q_tile[:, :LANES], q_tile[:, LANES:])
+    message = jnp.concatenate(
+        [approx[:, :LANES], approx[:, LANES:], gather_blocks(mine, t % GROUP)], axis=0
+    )
+    message = pltpu.roll(message, chip_ref[0] % GROUP * BLOCK, 1)
     for chip in range(CHIPS):
         out[chip] = message
 
@@ -191,7 +204,7 @@
     feedback_part, momentum_part, q_part = scratch
     for group in range(CHIPS // GROUP):
         chips = range(group * GROUP, (group + 1) * GROUP)
-        chunks = swap_blocks([parts[chip, 2 * ROWS :, :] for chip in chips])
+        chunks = merge_blocks([parts[chip, 2 * ROWS :, :] for chip in chips])
         q_part[:, group * LANES : (group + 1) * LANES] = jnp.concatenate(chunks, axis=0)
     copies = [pltpu.make_async_copy(q_part, q_out.at[:, columns(0, half)], sems.at[2, 0])]
     copies[0].start()
@@ -200,7 +213,7 @@
         for group in range(CHIPS // GROUP):
             chips = range(group * GROUP, (group + 1) * GROUP)
             place = slice(group * LANES, (group + 1) * LANES)
-            for tl, part in enumerate(swap_blocks([parts[chip, rows, :] for chip in chips])):
+            for tl, part in enumerate(merge_blocks([parts[chip, rows, :] for chip in chips])):
                 shard = th * GROUP + tl
                 start = shard * SHARD + half * SPAN + group * LANES
                 lanes = pl.ds(pl.multiple_of(start, LANES), LANES)
@@ -287,7 +300,7 @@
     factor = exchange(factor, "dp")
     parts = local(project_kernel, (HALF + 2 * ROWS, LANES), scalars=3)(core, chip, t, factor)[0]
     parts = gather_lines(parts)
-    own = local(solve_kernel, (CHIPS, 2 * ROWS + 8, LANES), scalars=1)(t, parts)[0]
+    own = local(solve_kernel, (CHIPS, 2 * ROWS + 8, LANES), scalars=2)(chip, t, parts)[0]
     own = exchange(own, "dp", chips)
     other = swap_cores(own)
     shapes = (feedback.shape, momentum.shape, q_previous.shape)

time: 107 us -> 105 us (0.981)
  Pallas kernels: 10.4 us -> 9.2 us
where the time goes in v12:
time: 105 us
  blocking collectives  63.4 us (60%)
  starting transfers between devices  27.9 us (27%)
  Pallas kernels  9.2 us (9%)
  waiting for transfers between devices  3.66 us (3%)
    all_gather x1, blocking collectives, gather_lines(): return lax.all_gather(parts, ('dp', 'tensor'), axis_index_groups=lines)  32.3 us
    all_to_all x2, blocking collectives, exchange(): lax.all_to_all(parts, axis, 0, 0, tiled=True, axis_index_groups=groups)  31.1 us
    ppermute x1, starting transfers between devices, fetch_shards(): return lax.ppermute(parts, ('dp', 'tensor'), pairs)  13.6 us
    all_to_all x1, starting transfers between devices, exchange(): lax.all_to_all(parts, axis, 0, 0, tiled=True, axis_index_groups=groups)  10.6 us
    ppermute x1, starting transfers between devices, swap_cores(): return lax.ppermute(parts, 'dp', [(d, d ^ 1) for d in range(DP)])  3.72 us
    pallas_call x1, Pallas kernels, on_device(): local(solve_kernel, (CHIPS, 2 * ROWS + 8, LANES), scalars=2)(chip, t, parts)  2.93 us
    pallas_call x1, Pallas kernels, on_device(): local(merge_kernel, (DP, ROWS, SPAN), scalars=1, inputs=2, room=60)  2.51 us
  transfers between devices with their start and end apart: 3, of which 2 were waited for; matrix products, arithmetic and copies ran while one was open for 0% of the time, Pallas kernels for 2%

profile of v12, /device:TPU:1, one launch (start us, length us, event | category | flops | bytes accessed | tf_op | source)
XLA Modules:
  0.0 105.0 jit_solution(16457200925931063621)
XLA Ops:
  0.6 2.5 %shard_map.67 = f32[32,32,256]{2,1,0:T(8,128)} custom-call(s32[1]{0:T(128)} %bitcast.1.t_ref, bf16[1,32,8192]{2,1,0:T(8,128)(2,1)} %gradient.5, f32[1,32,8192]{2,1,0:T(8,128)} %feedback.5), custom_call_target="tpu_custom_call" | custom-call | flops 100000 | bytes 100000 | tf_op jit(solution)/shard_map/pallas_call | solution.py:295
  3.1 0.0 copy-start.3
  3.1 10.6 %all-to-all-start = ((f32[32,32,256]{2,1,0:T(8,128)}), f32[32,32,256]{2,1,0:T(8,128)S(1)}, u32[]{:S(2)}, u32[]{:S(2)}) async-start(f32[32,32,256]{2,1,0:T(8,128)} %shard_map.67), calls=%async_computation | async-start | bytes 2097152 | tf_op jit(solution)/shard_map/all_to_all | solution.py:263
  13.8 0.0 copy-done.3
  13.8 13.6 %collective-permute-start = (f32[64,256]{1,0:T(8,128)S(1)}, f32[64,256]{1,0:T(8,128)S(1)}, u32[]{:S(2)}, u32[]{:S(2)}) collective-permute-start(f32[64,256]{1,0:T(8,128)S(1)} %shard_map.68), channel_id=1, source_target_pairs={{0,0},{9,1},{2,2},{11,3},{4,4},{13,5},{6,6},{15,7},{8,8},{1,9},{10... | collective-permute-start | bytes 196616 | tf_op jit(solution)/shard_map/ppermute | solution.py:276
  27.4 1.6 %collective-permute-done.q_part = f32[64,256]{1,0:T(8,128)S(1)} collective-permute-done((f32[64,256]{1,0:T(8,128)S(1)}, f32[64,256]{1,0:T(8,128)S(1)}, u32[]{:S(2)}, u32[]{:S(2)}) %collective-permute-start) | collective-permute-done | bytes 65568 | tf_op jit(solution)/shard_map/ppermute | solution.py:276
  29.0 2.0 %all-to-all-done.merged = f32[32,32,256]{2,1,0:T(8,128)S(1)} async-done(((f32[32,32,256]{2,1,0:T(8,128)}), f32[32,32,256]{2,1,0:T(8,128)S(1)}, u32[]{:S(2)}, u32[]{:S(2)}) %all-to-all-start) | async-done | bytes 1048608 | tf_op jit(solution)/shard_map/all_to_all | solution.py:263
  31.0 0.3 shard_map.70
  31.3 16.3 %all_to_all.15.parts = f32[32,24,128]{2,1,0:T(8,128)S(1)} all-to-all(f32[32,24,128]{2,1,0:T(8,128)S(1)} %shard_map.70), channel_id=1, replica_groups=mesh['dp'=32,'tensor'=16] {'dp'}, dimensions={0} | all-to-all | bytes 786432 | tf_op jit(solution)/shard_map/all_to_all | solution.py:263
  47.6 0.3 shard_map.71
  47.9 0.0 copy-start.2
  47.9 32.3 %all-gather = f32[1280,128]{1,0:T(8,128)S(1)} all-gather(f32[80,128]{1,0:T(8,128)S(1)} %shard_map.71), channel_id=2, replica_groups={{0,17,2,19,4,21,6,23,8,25,10,27,12,29,14,31},{16,1,18,3,20,5,22,7,24,9,..., dimensions={0}, use_global_device_ids=true | all-gather | bytes 696320 | tf_op jit(solution)/shard_map/all_gather | solution.py:283
  80.3 0.0 copy-start
  80.3 2.9 %shard_map.72 = f32[16,72,128]{2,1,0:T(8,128)S(1)} custom-call(s32[1]{0:T(128)} %bitcast.2.chip_ref, s32[1]{0:T(128)} %bitcast.1.t_ref, f32[16,80,128]{2,1,0:T(8,128)S(1)} %bitcast.4), custom_call_target="tpu_custom_call" | custom-call | flops 100000 | bytes 100000 | tf_op jit(solution)/shard_map/pallas_call | solution.py:303
  83.2 0.0 copy-start.1
  83.2 14.8 %all_to_all.16.parts = f32[16,72,128]{2,1,0:T(8,128)S(1)} all-to-all(f32[16,72,128]{2,1,0:T(8,128)S(1)} %shard_map.72), channel_id=1, replica_groups={{0,32,64,96,128,160,192,224,256,288,320,352,384,416,448,480},{16,48,80,..., dimensions={0} | all-to-all | bytes 1179648 | tf_op jit(solution)/shard_map/all_to_all | solution.py:263
  98.0 3.7 %collective-permute-start.1 = (f32[16,72,128]{2,1,0:T(8,128)S(1)}, f32[16,72,128]{2,1,0:T(8,128)S(1)}, u32[]{:S(2)}, u32[]{:S(2)}) collective-permute-start(f32[16,72,128]{2,1,0:T(8,128)S(1)} %all_to_all.16.parts), channel_id=1, source_target_pairs={{0,16},{16,0},{32,48},{48,32},{64,80},{80,64},{96,112},{112,96},{1... | collective-permute-start | bytes 1769480 | tf_op jit(solution)/shard_map/ppermute | solution.py:267
  101.7 0.0 copy-done.2
  101.7 0.0 copy-done
  101.7 0.0 copy-done.1
  101.7 1.6 %shard_map.73 = (f32[1,32,8192]{2,1,0:T(8,128)}, f32[32,8192]{1,0:T(8,128)}, f32[64,512]{1,0:T(8,128)}) custom-call(s32[1]{0:T(128)S(6)} %xor.6.half_ref, bf16[1,32,8192]{2,1,0:T(8,128)(2,1)S(1)} %copy-done.1, f32[1,32,8192]{2,1,0:T(8,128)S(1)} %copy-done, f32[32,8192]{1,0:T(8,128)S(1)} %copy-done.2, f32[16,72,128]{2,1,0:T(8,128)S(1)} %all_to_all.16.parts), custom_call_target="tpu_custom_call" | custom-call | flops 100000 | bytes 100000 | tf_op jit(solution)/shard_map/pallas_call | solution.py:313
  103.4 0.0 collective-permute-done.1.parts
  103.4 1.6 %shard_map.74 = (f32[1,32,8192]{2,1,0:T(8,128)}, f32[32,8192]{1,0:T(8,128)}, f32[64,512]{1,0:T(8,128)}) custom-call(s32[1]{0:T(128)S(6)} %sub.6.half_ref, bf16[1,32,8192]{2,1,0:T(8,128)(2,1)S(1)} %copy-done.1, f32[1,32,8192]{2,1,0:T(8,128)S(1)} %copy-done, f32[32,8192]{1,0:T(8,128)S(1)} %copy-done.2, ...), custom_call_target="tpu_custom_call", output_to_operand_aliasing={{0}: (5, {}), {1}: (6, {}), {2}: (7, {})} | custom-call | flops 100000 | bytes 100000 | tf_op jit(solution)/shard_map/pallas_call | solution.py:316
  (2 shorter events, 0.0 us)
Async XLA Ops:
  3.1 10.6 %copy-start.3 = (f32[64,512]{1,0:T(8,128)S(1)}, f32[64,512]{1,0:T(8,128)}, u32[]{:S(2)}) copy-start(f32[64,512]{1,0:T(8,128)} %q_ref.1) | copy-start | bytes 393220
  3.1 27.9 %all-to-all-start = ((f32[32,32,256]{2,1,0:T(8,128)}), f32[32,32,256]{2,1,0:T(8,128)S(1)}, u32[]{:S(2)}, u32[]{:S(2)}) async-start(f32[32,32,256]{2,1,0:T(8,128)} %shard_map.67), calls=%async_computation | async-start | bytes 2097152 | tf_op jit(solution)/shard_map/all_to_all | solution.py:263
  13.8 15.2 %collective-permute-start = (f32[64,256]{1,0:T(8,128)S(1)}, f32[64,256]{1,0:T(8,128)S(1)}, u32[]{:S(2)}, u32[]{:S(2)}) collective-permute-start(f32[64,256]{1,0:T(8,128)S(1)} %shard_map.68), channel_id=1, source_target_pairs={{0,0},{9,1},{2,2},{11,3},{4,4},{13,5},{6,6},{15,7},{8,8},{1,9},{10... | collective-permute-start | bytes 196616 | tf_op jit(solution)/shard_map/ppermute | solution.py:276
  47.9 53.8 %copy-start.2 = (f32[32,8192]{1,0:T(8,128)S(1)}, f32[32,8192]{1,0:T(8,128)}, u32[]{:S(2)}) copy-start(f32[32,8192]{1,0:T(8,128)} %momentum.3) | copy-start | bytes 3145732
  80.3 21.5 %copy-start = (f32[1,32,8192]{2,1,0:T(8,128)S(1)}, f32[1,32,8192]{2,1,0:T(8,128)}, u32[]{:S(2)}) copy-start(f32[1,32,8192]{2,1,0:T(8,128)} %feedback.5) | copy-start | bytes 3145732
  83.2 18.5 %copy-start.1 = (bf16[1,32,8192]{2,1,0:T(8,128)(2,1)S(1)}, bf16[1,32,8192]{2,1,0:T(8,128)(2,1)}, u32[]{:S(2)}) copy-start(bf16[1,32,8192]{2,1,0:T(8,128)(2,1)} %gradient.5) | copy-start | bytes 1572868
  98.0 5.4 %collective-permute-start.1 = (f32[16,72,128]{2,1,0:T(8,128)S(1)}, f32[16,72,128]{2,1,0:T(8,128)S(1)}, u32[]{:S(2)}, u32[]{:S(2)}) collective-permute-start(f32[16,72,128]{2,1,0:T(8,128)S(1)} %all_to_all.16.parts), channel_id=1, source_target_pairs={{0,16},{16,0},{32,48},{48,32},{64,80},{80,64},{96,112},{112,96},{1... | collective-permute-start | bytes 1769480 | tf_op jit(solution)/shard_map/ppermute | solution.py:267

commit v13 on v12

--- a/solution.py
+++ b/solution.py
@@ -272,7 +272,7 @@
     for d in range(DP):
         for t in range(TP):
             plane = (t + d // 2 + (d & 1 ^ t & 1) * (TP // 2)) % TP
-            pairs.append((d * TP + plane, d * TP + t))
+            pairs.append(((d ^ 1) * TP + plane, d * TP + t))
     return lax.ppermute(parts, ("dp", "tensor"), pairs)
 
 
@@ -289,7 +289,7 @@
     t = lax.axis_index("tensor").reshape(1)
     chips = [list(range(c, DP, 2)) for c in range(2)]
     half = core ^ (t & 1)
-    q_part = local(half_kernel, (RANK, SPAN), scalars=1)(core ^ ((t - chip) & 1), q_previous)[0]
+    q_part = local(half_kernel, (RANK, SPAN), scalars=1)(core ^ ((t - chip + 1) & 1), q_previous)[0]
     q_part = fetch_shards(q_part)
     q_part = local(twice_kernel, (2 * RANK, SPAN), flops=100_000)(q_part)[0]
     merged = local(merge_kernel, (DP, ROWS, SPAN), scalars=1, inputs=2, room=60)(

time: 105 us -> 104 us (level)
  waiting for transfers between devices: 3.66 us -> 15 us
  starting transfers between devices: 27.9 us -> 16.6 us
    ppermute x1, waiting for transfers between devices: 1.64 us -> 13.5 us  [fetch_shards(): return lax.ppermute(parts, ('dp', 'tensor'), pairs)]
    ppermute x1, starting transfers between devices: 13.6 us -> 2.26 us  [fetch_shards(): return lax.ppermute(parts, ('dp', 'tensor'), pairs)]
    all_gather x1, blocking collectives: 32.3 us -> 30.1 us  [gather_lines(): return lax.all_gather(parts, ('dp', 'tensor'), axis_index_groups=lines)]
    all_to_all x2, blocking collectives: 31.1 us -> 32.4 us  [exchange(): lax.all_to_all(parts, axis, 0, 0, tiled=True, axis_index_groups=groups)]
where the time goes in v13:
time: 104 us
  blocking collectives  62.4 us (60%)
  starting transfers between devices  16.6 us (16%)
  waiting for transfers between devices  15 us (14%)
  Pallas kernels  9.2 us (9%)
    all_to_all x2, blocking collectives, exchange(): lax.all_to_all(parts, axis, 0, 0, tiled=True, axis_index_groups=groups)  32.4 us
    all_gather x1, blocking collectives, gather_lines(): return lax.all_gather(parts, ('dp', 'tensor'), axis_index_groups=lines)  30.1 us
    ppermute x1, waiting for transfers between devices, fetch_shards(): return lax.ppermute(parts, ('dp', 'tensor'), pairs)  13.5 us
    all_to_all x1, starting transfers between devices, exchange(): lax.all_to_all(parts, axis, 0, 0, tiled=True, axis_index_groups=groups)  10.6 us
    ppermute x1, starting transfers between devices, swap_cores(): return lax.ppermute(parts, 'dp', [(d, d ^ 1) for d in range(DP)])  3.73 us
    pallas_call x1, Pallas kernels, on_device(): local(solve_kernel, (CHIPS, 2 * ROWS + 8, LANES), scalars=2)(chip, t, parts)  2.93 us
    pallas_call x1, Pallas kernels, on_device(): local(merge_kernel, (DP, ROWS, SPAN), scalars=1, inputs=2, room=60)  2.51 us
    ppermute x1, starting transfers between devices, fetch_shards(): return lax.ppermute(parts, ('dp', 'tensor'), pairs)  2.26 us
  transfers between devices with their start and end apart: 3, of which 2 were waited for; matrix products, arithmetic and copies ran while one was open for 0% of the time, Pallas kernels for 2%

profile of v13, /device:TPU:1, one launch (start us, length us, event | category | flops | bytes accessed | tf_op | source)
XLA Modules:
  0.0 104.0 jit_solution(1350270600461960384)
XLA Ops:
  0.6 2.5 %shard_map.67 = f32[32,32,256]{2,1,0:T(8,128)} custom-call(s32[1]{0:T(128)} %bitcast.1.t_ref, bf16[1,32,8192]{2,1,0:T(8,128)(2,1)} %gradient.5, f32[1,32,8192]{2,1,0:T(8,128)} %feedback.5), custom_call_target="tpu_custom_call" | custom-call | flops 100000 | bytes 100000 | tf_op jit(solution)/shard_map/pallas_call | solution.py:295
  3.1 0.0 copy-start.3
  3.1 10.6 %all-to-all-start = ((f32[32,32,256]{2,1,0:T(8,128)}), f32[32,32,256]{2,1,0:T(8,128)S(1)}, u32[]{:S(2)}, u32[]{:S(2)}) async-start(f32[32,32,256]{2,1,0:T(8,128)} %shard_map.67), calls=%async_computation | async-start | bytes 2097152 | tf_op jit(solution)/shard_map/all_to_all | solution.py:263
  13.8 0.0 copy-done.3
  13.8 2.3 %collective-permute-start = (f32[64,256]{1,0:T(8,128)S(1)}, f32[64,256]{1,0:T(8,128)S(1)}, u32[]{:S(2)}, u32[]{:S(2)}) collective-permute-start(f32[64,256]{1,0:T(8,128)S(1)} %shard_map.68), channel_id=1, source_target_pairs={{16,0},{25,1},{18,2},{27,3},{20,4},{29,5},{22,6},{31,7},{24,8},{17... | collective-permute-start | bytes 196616 | tf_op jit(solution)/shard_map/ppermute | solution.py:276
  16.1 13.5 %collective-permute-done.q_part = f32[64,256]{1,0:T(8,128)S(1)} collective-permute-done((f32[64,256]{1,0:T(8,128)S(1)}, f32[64,256]{1,0:T(8,128)S(1)}, u32[]{:S(2)}, u32[]{:S(2)}) %collective-permute-start) | collective-permute-done | bytes 65568 | tf_op jit(solution)/shard_map/ppermute | solution.py:276
  29.5 1.5 %all-to-all-done.merged = f32[32,32,256]{2,1,0:T(8,128)S(1)} async-done(((f32[32,32,256]{2,1,0:T(8,128)}), f32[32,32,256]{2,1,0:T(8,128)S(1)}, u32[]{:S(2)}, u32[]{:S(2)}) %all-to-all-start) | async-done | bytes 1048608 | tf_op jit(solution)/shard_map/all_to_all | solution.py:263
  31.0 0.3 shard_map.70
  31.3 17.6 %all_to_all.15.parts = f32[32,24,128]{2,1,0:T(8,128)S(1)} all-to-all(f32[32,24,128]{2,1,0:T(8,128)S(1)} %shard_map.70), channel_id=1, replica_groups=mesh['dp'=32,'tensor'=16] {'dp'}, dimensions={0} | all-to-all | bytes 786432 | tf_op jit(solution)/shard_map/all_to_all | solution.py:263
  48.9 0.3 shard_map.71
  49.2 0.0 copy-start.2
  49.2 30.1 %all-gather = f32[1280,128]{1,0:T(8,128)S(1)} all-gather(f32[80,128]{1,0:T(8,128)S(1)} %shard_map.71), channel_id=2, replica_groups={{0,17,2,19,4,21,6,23,8,25,10,27,12,29,14,31},{16,1,18,3,20,5,22,7,24,9,..., dimensions={0}, use_global_device_ids=true | all-gather | bytes 696320 | tf_op jit(solution)/shard_map/all_gather | solution.py:283
  79.3 0.0 copy-start
  79.3 2.9 %shard_map.72 = f32[16,72,128]{2,1,0:T(8,128)S(1)} custom-call(s32[1]{0:T(128)} %bitcast.2.chip_ref, s32[1]{0:T(128)} %bitcast.1.t_ref, f32[16,80,128]{2,1,0:T(8,128)S(1)} %bitcast.4), custom_call_target="tpu_custom_call" | custom-call | flops 100000 | bytes 100000 | tf_op jit(solution)/shard_map/pallas_call | solution.py:303
  82.2 0.0 copy-start.1
  82.2 14.8 %all_to_all.16.parts = f32[16,72,128]{2,1,0:T(8,128)S(1)} all-to-all(f32[16,72,128]{2,1,0:T(8,128)S(1)} %shard_map.72), channel_id=1, replica_groups={{0,32,64,96,128,160,192,224,256,288,320,352,384,416,448,480},{16,48,80,..., dimensions={0} | all-to-all | bytes 1179648 | tf_op jit(solution)/shard_map/all_to_all | solution.py:263
  97.0 3.7 %collective-permute-start.1 = (f32[16,72,128]{2,1,0:T(8,128)S(1)}, f32[16,72,128]{2,1,0:T(8,128)S(1)}, u32[]{:S(2)}, u32[]{:S(2)}) collective-permute-start(f32[16,72,128]{2,1,0:T(8,128)S(1)} %all_to_all.16.parts), channel_id=1, source_target_pairs={{0,16},{16,0},{32,48},{48,32},{64,80},{80,64},{96,112},{112,96},{1... | collective-permute-start | bytes 1769480 | tf_op jit(solution)/shard_map/ppermute | solution.py:267
  100.7 0.0 copy-done.2
  100.7 0.0 copy-done
  100.7 0.0 copy-done.1
  100.8 1.6 %shard_map.73 = (f32[1,32,8192]{2,1,0:T(8,128)}, f32[32,8192]{1,0:T(8,128)}, f32[64,512]{1,0:T(8,128)}) custom-call(s32[1]{0:T(128)S(6)} %xor.6.half_ref, bf16[1,32,8192]{2,1,0:T(8,128)(2,1)S(1)} %copy-done.1, f32[1,32,8192]{2,1,0:T(8,128)S(1)} %copy-done, f32[32,8192]{1,0:T(8,128)S(1)} %copy-done.2, f32[16,72,128]{2,1,0:T(8,128)S(1)} %all_to_all.16.parts), custom_call_target="tpu_custom_call" | custom-call | flops 100000 | bytes 100000 | tf_op jit(solution)/shard_map/pallas_call | solution.py:313
  102.4 0.0 collective-permute-done.1.parts
  102.4 1.6 %shard_map.74 = (f32[1,32,8192]{2,1,0:T(8,128)}, f32[32,8192]{1,0:T(8,128)}, f32[64,512]{1,0:T(8,128)}) custom-call(s32[1]{0:T(128)S(6)} %sub.6.half_ref, bf16[1,32,8192]{2,1,0:T(8,128)(2,1)S(1)} %copy-done.1, f32[1,32,8192]{2,1,0:T(8,128)S(1)} %copy-done, f32[32,8192]{1,0:T(8,128)S(1)} %copy-done.2, ...), custom_call_target="tpu_custom_call", output_to_operand_aliasing={{0}: (5, {}), {1}: (6, {}), {2}: (7, {})} | custom-call | flops 100000 | bytes 100000 | tf_op jit(solution)/shard_map/pallas_call | solution.py:316
  (2 shorter events, 0.0 us)
Async XLA Ops:
  3.1 10.6 %copy-start.3 = (f32[64,512]{1,0:T(8,128)S(1)}, f32[64,512]{1,0:T(8,128)}, u32[]{:S(2)}) copy-start(f32[64,512]{1,0:T(8,128)} %q_ref.1) | copy-start | bytes 393220
  3.1 27.9 %all-to-all-start = ((f32[32,32,256]{2,1,0:T(8,128)}), f32[32,32,256]{2,1,0:T(8,128)S(1)}, u32[]{:S(2)}, u32[]{:S(2)}) async-start(f32[32,32,256]{2,1,0:T(8,128)} %shard_map.67), calls=%async_computation | async-start | bytes 2097152 | tf_op jit(solution)/shard_map/all_to_all | solution.py:263
  13.8 15.7 %collective-permute-start = (f32[64,256]{1,0:T(8,128)S(1)}, f32[64,256]{1,0:T(8,128)S(1)}, u32[]{:S(2)}, u32[]{:S(2)}) collective-permute-start(f32[64,256]{1,0:T(8,128)S(1)} %shard_map.68), channel_id=1, source_target_pairs={{16,0},{25,1},{18,2},{27,3},{20,4},{29,5},{22,6},{31,7},{24,8},{17... | collective-permute-start | bytes 196616 | tf_op jit(solution)/shard_map/ppermute | solution.py:276
  49.2 51.5 %copy-start.2 = (f32[32,8192]{1,0:T(8,128)S(1)}, f32[32,8192]{1,0:T(8,128)}, u32[]{:S(2)}) copy-start(f32[32,8192]{1,0:T(8,128)} %momentum.3) | copy-start | bytes 3145732
  79.3 21.5 %copy-start = (f32[1,32,8192]{2,1,0:T(8,128)S(1)}, f32[1,32,8192]{2,1,0:T(8,128)}, u32[]{:S(2)}) copy-start(f32[1,32,8192]{2,1,0:T(8,128)} %feedback.5) | copy-start | bytes 3145732
  82.2 18.5 %copy-start.1 = (bf16[1,32,8192]{2,1,0:T(8,128)(2,1)S(1)}, bf16[1,32,8192]{2,1,0:T(8,128)(2,1)}, u32[]{:S(2)}) copy-start(bf16[1,32,8192]{2,1,0:T(8,128)(2,1)} %gradient.5) | copy-start | bytes 1572868
  97.0 5.4 %collective-permute-start.1 = (f32[16,72,128]{2,1,0:T(8,128)S(1)}, f32[16,72,128]{2,1,0:T(8,128)S(1)}, u32[]{:S(2)}, u32[]{:S(2)}) collective-permute-start(f32[16,72,128]{2,1,0:T(8,128)S(1)} %all_to_all.16.parts), channel_id=1, source_target_pairs={{0,16},{16,0},{32,48},{48,32},{64,80},{80,64},{96,112},{112,96},{1... | collective-permute-start | bytes 1769480 | tf_op jit(solution)/shard_map/ppermute | solution.py:267

commit v14 on v13

--- a/solution.py
+++ b/solution.py
@@ -21,6 +21,7 @@
 SHARD = DP * BLOCK
 CHIPS = DP // 2
 HALF = ROWS // 2
+PART = ROWS // GROUP
 
 
 def dot(left, right, left_dim, right_dim):
@@ -103,40 +104,35 @@
     factor = dot(total, q_twice[...], 1, 1)
     lane = lax.broadcasted_iota(jnp.int32, (HALF, LANES), 1)
     packed = jnp.where(lane < RANK, factor[:HALF], factor[HALF:])
-    pieces = swap_blocks(
-        [
-            total[g * 8 : (g + 1) * 8, h * LANES : (h + 1) * LANES]
-            for h in range(2)
-            for g in range(ROWS // 8)
-        ]
-    )
+    pieces = []
+    for h in range(2):
+        lanes = slice(h * LANES, (h + 1) * LANES)
+        pieces += swap_blocks([total[g * PART : (g + 1) * PART, lanes] for g in range(GROUP)])
     for d in range(DP):
-        out[d, :HALF, :] = packed
-        out[d, HALF:, :] = pieces[d // 2 % GROUP]
+        for i in range(HALF // PART):
+            out[d, i] = packed[i * PART : (i + 1) * PART]
+        out[d, HALF // PART] = pieces[d // 2]
 
 
 def unpack_rows(packed):
     return jnp.concatenate([packed[:, :RANK], packed[:, RANK:]], axis=0)
 
 
-def project_kernel(core_ref, chip_ref, t_ref, parts, out):
+def project_kernel(core_ref, t_ref, parts, out):
     half = core_ref[0] ^ (t_ref[0] & 1)
-    packed = parts[0, :HALF, :]
-    for d in range(1, DP):
-        packed = packed + parts[d, :HALF, :]
-    out[:HALF, :] = packed
-    low = chip_ref[0] < GROUP
+    for i in range(HALF // PART):
+        packed = parts[0, i]
+        for d in range(1, DP):
+            packed = packed + parts[d, i]
+        out[i * PART : (i + 1) * PART, :] = packed
     for th in range(TP // GROUP):
         pieces = []
         for tl in range(GROUP):
             source = (th * GROUP + tl - t_ref[0] + (4 - half) * (TP // 2)) % TP
-            pieces.append(parts[source * 2 + core_ref[0], HALF:, :])
-        pieces = swap_blocks(pieces)
-        start = HALF + th * ROWS
-        for g in range(ROWS // 8):
-            out[start + g * 8 : start + (g + 1) * 8, :] = jnp.where(
-                low, pieces[g], pieces[g + ROWS // 8]
-            )
+            pieces.append(parts[source * 2 + core_ref[0], HALF // PART])
+        for g, piece in enumerate(swap_blocks(pieces)):
+            start = HALF + th * ROWS + g * PART
+            out[start : start + PART, :] = piece
 
 
 def inverse_triangle(gram):
@@ -296,9 +292,9 @@
         t, gradient, feedback
     )[0]
     merged = exchange(merged, "dp")
-    factor = local(factor_kernel, (DP, HALF + 8, LANES), inputs=2)(merged, q_part)[0]
+    factor = local(factor_kernel, (DP, HALF // PART + 1, PART, LANES), inputs=2)(merged, q_part)[0]
     factor = exchange(factor, "dp")
-    parts = local(project_kernel, (HALF + 2 * ROWS, LANES), scalars=3)(core, chip, t, factor)[0]
+    parts = local(project_kernel, (HALF + 2 * ROWS, LANES), scalars=2)(core, t, factor)[0]
     parts = gather_lines(parts)
     own = local(solve_kernel, (CHIPS, 2 * ROWS + 8, LANES), scalars=2)(chip, t, parts)[0]
     own = exchange(own, "dp", chips)

time: 104 us -> 104 us (level)
  no operation moved by 1% of the time
where the time goes in v14:
time: 104 us; the launch traced here: 103 us
  blocking collectives  61.7 us (59%)
  starting transfers between devices  16.6 us (16%)
  waiting for transfers between devices  15 us (14%)
  Pallas kernels  9.24 us (9%)
    all_to_all x2, blocking collectives, exchange(): lax.all_to_all(parts, axis, 0, 0, tiled=True, axis_index_groups=groups)  31.6 us
    all_gather x1, blocking collectives, gather_lines(): return lax.all_gather(parts, ('dp', 'tensor'), axis_index_groups=lines)  30.1 us
    ppermute x1, waiting for transfers between devices, fetch_shards(): return lax.ppermute(parts, ('dp', 'tensor'), pairs)  13.5 us
    all_to_all x1, starting transfers between devices, exchange(): lax.all_to_all(parts, axis, 0, 0, tiled=True, axis_index_groups=groups)  10.6 us
    ppermute x1, starting transfers between devices, swap_cores(): return lax.ppermute(parts, 'dp', [(d, d ^ 1) for d in range(DP)])  3.72 us
    pallas_call x1, Pallas kernels, on_device(): local(solve_kernel, (CHIPS, 2 * ROWS + 8, LANES), scalars=2)(chip, t, parts)  2.93 us
    pallas_call x1, Pallas kernels, on_device(): local(merge_kernel, (DP, ROWS, SPAN), scalars=1, inputs=2, room=60)  2.51 us
    ppermute x1, starting transfers between devices, fetch_shards(): return lax.ppermute(parts, ('dp', 'tensor'), pairs)  2.26 us
  transfers between devices with their start and end apart: 3, of which 2 were waited for; matrix products, arithmetic and copies ran while one was open for 0% of the time, Pallas kernels for 2%

profile of v14, /device:TPU:1, one launch (start us, length us, event | category | flops | bytes accessed | tf_op | source)
XLA Modules:
  0.0 103.3 jit_solution(14293789251667099699)
XLA Ops:
  0.6 2.5 %shard_map.67 = f32[32,32,256]{2,1,0:T(8,128)} custom-call(s32[1]{0:T(128)} %bitcast.1.t_ref, bf16[1,32,8192]{2,1,0:T(8,128)(2,1)} %gradient.5, f32[1,32,8192]{2,1,0:T(8,128)} %feedback.5), custom_call_target="tpu_custom_call" | custom-call | flops 100000 | bytes 100000 | tf_op jit(solution)/shard_map/pallas_call | solution.py:291
  3.1 0.0 copy-start.3
  3.1 10.6 %all-to-all-start = ((f32[32,32,256]{2,1,0:T(8,128)}), f32[32,32,256]{2,1,0:T(8,128)S(1)}, u32[]{:S(2)}, u32[]{:S(2)}) async-start(f32[32,32,256]{2,1,0:T(8,128)} %shard_map.67), calls=%async_computation | async-start | bytes 2097152 | tf_op jit(solution)/shard_map/all_to_all | solution.py:259
  13.8 0.0 copy-done.3
  13.8 2.3 %collective-permute-start = (f32[64,256]{1,0:T(8,128)S(1)}, f32[64,256]{1,0:T(8,128)S(1)}, u32[]{:S(2)}, u32[]{:S(2)}) collective-permute-start(f32[64,256]{1,0:T(8,128)S(1)} %shard_map.68), channel_id=1, source_target_pairs={{16,0},{25,1},{18,2},{27,3},{20,4},{29,5},{22,6},{31,7},{24,8},{17... | collective-permute-start | bytes 196616 | tf_op jit(solution)/shard_map/ppermute | solution.py:272
  16.1 13.5 %collective-permute-done.q_part = f32[64,256]{1,0:T(8,128)S(1)} collective-permute-done((f32[64,256]{1,0:T(8,128)S(1)}, f32[64,256]{1,0:T(8,128)S(1)}, u32[]{:S(2)}, u32[]{:S(2)}) %collective-permute-start) | collective-permute-done | bytes 65568 | tf_op jit(solution)/shard_map/ppermute | solution.py:272
  29.5 1.5 %all-to-all-done.merged = f32[32,32,256]{2,1,0:T(8,128)S(1)} async-done(((f32[32,32,256]{2,1,0:T(8,128)}), f32[32,32,256]{2,1,0:T(8,128)S(1)}, u32[]{:S(2)}, u32[]{:S(2)}) %all-to-all-start) | async-done | bytes 1048608 | tf_op jit(solution)/shard_map/all_to_all | solution.py:259
  31.0 0.3 shard_map.70
  31.4 17.0 %all_to_all.15.parts = f32[32,5,4,128]{3,2,1,0:T(4,128)S(1)} all-to-all(f32[32,5,4,128]{3,2,1,0:T(4,128)S(1)} %shard_map.70), channel_id=1, replica_groups=mesh['dp'=32,'tensor'=16] {'dp'}, dimensions={0} | all-to-all | bytes 655360 | tf_op jit(solution)/shard_map/all_to_all | solution.py:259
  48.3 0.3 shard_map.71
  48.6 0.0 copy-start.2
  48.6 30.1 %all-gather = f32[1280,128]{1,0:T(8,128)S(1)} all-gather(f32[80,128]{1,0:T(8,128)S(1)} %shard_map.71), channel_id=2, replica_groups={{0,17,2,19,4,21,6,23,8,25,10,27,12,29,14,31},{16,1,18,3,20,5,22,7,24,9,..., dimensions={0}, use_global_device_ids=true | all-gather | bytes 696320 | tf_op jit(solution)/shard_map/all_gather | solution.py:279
  78.7 0.0 copy-start
  78.7 2.9 %shard_map.72 = f32[16,72,128]{2,1,0:T(8,128)S(1)} custom-call(s32[1]{0:T(128)} %bitcast.2.chip_ref, s32[1]{0:T(128)} %bitcast.1.t_ref, f32[16,80,128]{2,1,0:T(8,128)S(1)} %bitcast.4), custom_call_target="tpu_custom_call" | custom-call | flops 100000 | bytes 100000 | tf_op jit(solution)/shard_map/pallas_call | solution.py:299
  81.7 0.0 copy-start.1
  81.7 14.7 %all_to_all.16.parts = f32[16,72,128]{2,1,0:T(8,128)S(1)} all-to-all(f32[16,72,128]{2,1,0:T(8,128)S(1)} %shard_map.72), channel_id=1, replica_groups={{0,32,64,96,128,160,192,224,256,288,320,352,384,416,448,480},{16,48,80,..., dimensions={0} | all-to-all | bytes 1179648 | tf_op jit(solution)/shard_map/all_to_all | solution.py:259
  96.3 3.7 %collective-permute-start.1 = (f32[16,72,128]{2,1,0:T(8,128)S(1)}, f32[16,72,128]{2,1,0:T(8,128)S(1)}, u32[]{:S(2)}, u32[]{:S(2)}) collective-permute-start(f32[16,72,128]{2,1,0:T(8,128)S(1)} %all_to_all.16.parts), channel_id=1, source_target_pairs={{0,16},{16,0},{32,48},{48,32},{64,80},{80,64},{96,112},{112,96},{1... | collective-permute-start | bytes 1769480 | tf_op jit(solution)/shard_map/ppermute | solution.py:263
  100.1 0.0 copy-done.2
  100.1 0.0 copy-done
  100.1 0.0 copy-done.1
  100.1 1.6 %shard_map.73 = (f32[1,32,8192]{2,1,0:T(8,128)}, f32[32,8192]{1,0:T(8,128)}, f32[64,512]{1,0:T(8,128)}) custom-call(s32[1]{0:T(128)S(6)} %xor.6.half_ref, bf16[1,32,8192]{2,1,0:T(8,128)(2,1)S(1)} %copy-done.1, f32[1,32,8192]{2,1,0:T(8,128)S(1)} %copy-done, f32[32,8192]{1,0:T(8,128)S(1)} %copy-done.2, f32[16,72,128]{2,1,0:T(8,128)S(1)} %all_to_all.16.parts), custom_call_target="tpu_custom_call" | custom-call | flops 100000 | bytes 100000 | tf_op jit(solution)/shard_map/pallas_call | solution.py:309
  101.7 0.0 collective-permute-done.1.parts
  101.7 1.6 %shard_map.74 = (f32[1,32,8192]{2,1,0:T(8,128)}, f32[32,8192]{1,0:T(8,128)}, f32[64,512]{1,0:T(8,128)}) custom-call(s32[1]{0:T(128)S(6)} %sub.6.half_ref, bf16[1,32,8192]{2,1,0:T(8,128)(2,1)S(1)} %copy-done.1, f32[1,32,8192]{2,1,0:T(8,128)S(1)} %copy-done, f32[32,8192]{1,0:T(8,128)S(1)} %copy-done.2, ...), custom_call_target="tpu_custom_call", output_to_operand_aliasing={{0}: (5, {}), {1}: (6, {}), {2}: (7, {})} | custom-call | flops 100000 | bytes 100000 | tf_op jit(solution)/shard_map/pallas_call | solution.py:312
  (2 shorter events, 0.0 us)
Async XLA Ops:
  3.1 10.6 %copy-start.3 = (f32[64,512]{1,0:T(8,128)S(1)}, f32[64,512]{1,0:T(8,128)}, u32[]{:S(2)}) copy-start(f32[64,512]{1,0:T(8,128)} %q_ref.1) | copy-start | bytes 393220
  3.1 27.9 %all-to-all-start = ((f32[32,32,256]{2,1,0:T(8,128)}), f32[32,32,256]{2,1,0:T(8,128)S(1)}, u32[]{:S(2)}, u32[]{:S(2)}) async-start(f32[32,32,256]{2,1,0:T(8,128)} %shard_map.67), calls=%async_computation | async-start | bytes 2097152 | tf_op jit(solution)/shard_map/all_to_all | solution.py:259
  13.8 15.7 %collective-permute-start = (f32[64,256]{1,0:T(8,128)S(1)}, f32[64,256]{1,0:T(8,128)S(1)}, u32[]{:S(2)}, u32[]{:S(2)}) collective-permute-start(f32[64,256]{1,0:T(8,128)S(1)} %shard_map.68), channel_id=1, source_target_pairs={{16,0},{25,1},{18,2},{27,3},{20,4},{29,5},{22,6},{31,7},{24,8},{17... | collective-permute-start | bytes 196616 | tf_op jit(solution)/shard_map/ppermute | solution.py:272
  48.6 51.4 %copy-start.2 = (f32[32,8192]{1,0:T(8,128)S(1)}, f32[32,8192]{1,0:T(8,128)}, u32[]{:S(2)}) copy-start(f32[32,8192]{1,0:T(8,128)} %momentum.3) | copy-start | bytes 3145732
  78.7 21.4 %copy-start = (f32[1,32,8192]{2,1,0:T(8,128)S(1)}, f32[1,32,8192]{2,1,0:T(8,128)}, u32[]{:S(2)}) copy-start(f32[1,32,8192]{2,1,0:T(8,128)} %feedback.5) | copy-start | bytes 3145732
  81.7 18.4 %copy-start.1 = (bf16[1,32,8192]{2,1,0:T(8,128)(2,1)S(1)}, bf16[1,32,8192]{2,1,0:T(8,128)(2,1)}, u32[]{:S(2)}) copy-start(bf16[1,32,8192]{2,1,0:T(8,128)(2,1)} %gradient.5) | copy-start | bytes 1572868
  96.3 5.4 %collective-permute-start.1 = (f32[16,72,128]{2,1,0:T(8,128)S(1)}, f32[16,72,128]{2,1,0:T(8,128)S(1)}, u32[]{:S(2)}, u32[]{:S(2)}) collective-permute-start(f32[16,72,128]{2,1,0:T(8,128)S(1)} %all_to_all.16.parts), channel_id=1, source_target_pairs={{0,16},{16,0},{32,48},{48,32},{64,80},{80,64},{96,112},{112,96},{1... | collective-permute-start | bytes 1769480 | tf_op jit(solution)/shard_map/ppermute | solution.py:263

commit v15 on v14

--- a/solution.py
+++ b/solution.py
@@ -92,16 +92,12 @@
     out[...] = jnp.where(half_ref[0] == 0, q_ref[:, :SPAN], q_ref[:, SPAN:])
 
 
-def twice_kernel(q_part, out):
-    out[:RANK, :] = q_part[...]
-    out[RANK:, :] = q_part[...]
-
-
-def factor_kernel(merged, q_twice, out):
+def factor_kernel(merged, q_part, out):
     total = merged[0]
     for d in range(1, DP):
         total = total + merged[d]
-    factor = dot(total, q_twice[...], 1, 1)
+    q_twice = jnp.concatenate([q_part[...], q_part[...]], axis=0)
+    factor = dot(total, q_twice, 1, 1)
     lane = lax.broadcasted_iota(jnp.int32, (HALF, LANES), 1)
     packed = jnp.where(lane < RANK, factor[:HALF], factor[HALF:])
     pieces = []
@@ -287,7 +283,6 @@
     half = core ^ (t & 1)
     q_part = local(half_kernel, (RANK, SPAN), scalars=1)(core ^ ((t - chip + 1) & 1), q_previous)[0]
     q_part = fetch_shards(q_part)
-    q_part = local(twice_kernel, (2 * RANK, SPAN), flops=100_000)(q_part)[0]
     merged = local(merge_kernel, (DP, ROWS, SPAN), scalars=1, inputs=2, room=60)(
         t, gradient, feedback
     )[0]

time: 104 us -> 104 us (level)
  no operation moved by 1% of the time
where the time goes in v15:
time: 104 us; the launch traced here: 103 us
  blocking collectives  61.7 us (59%)
  starting transfers between devices  16.6 us (16%)
  waiting for transfers between devices  15 us (14%)
  Pallas kernels  9.23 us (9%)
    all_to_all x2, blocking collectives, exchange(): lax.all_to_all(parts, axis, 0, 0, tiled=True, axis_index_groups=groups)  31.6 us
    all_gather x1, blocking collectives, gather_lines(): return lax.all_gather(parts, ('dp', 'tensor'), axis_index_groups=lines)  30.1 us
    ppermute x1, waiting for transfers between devices, fetch_shards(): return lax.ppermute(parts, ('dp', 'tensor'), pairs)  13.5 us
    all_to_all x1, starting transfers between devices, exchange(): lax.all_to_all(parts, axis, 0, 0, tiled=True, axis_index_groups=groups)  10.6 us
    ppermute x1, starting transfers between devices, swap_cores(): return lax.ppermute(parts, 'dp', [(d, d ^ 1) for d in range(DP)])  3.72 us
    pallas_call x1, Pallas kernels, on_device(): local(solve_kernel, (CHIPS, 2 * ROWS + 8, LANES), scalars=2)(chip, t, parts)  2.93 us
    pallas_call x1, Pallas kernels, on_device(): local(merge_kernel, (DP, ROWS, SPAN), scalars=1, inputs=2, room=60)  2.51 us
    ppermute x1, starting transfers between devices, fetch_shards(): return lax.ppermute(parts, ('dp', 'tensor'), pairs)  2.26 us
  transfers between devices with their start and end apart: 3, of which 2 were waited for; matrix products, arithmetic and copies ran while one was open for 0% of the time, Pallas kernels for 2%

profile of v15, /device:TPU:1, one launch (start us, length us, event | category | flops | bytes accessed | tf_op | source)
XLA Modules:
  0.0 103.3 jit_solution(16655984599190313872)
XLA Ops:
  0.6 2.5 %shard_map.67 = f32[32,32,256]{2,1,0:T(8,128)} custom-call(s32[1]{0:T(128)} %bitcast.1.t_ref, bf16[1,32,8192]{2,1,0:T(8,128)(2,1)} %gradient.5, f32[1,32,8192]{2,1,0:T(8,128)} %feedback.5), custom_call_target="tpu_custom_call" | custom-call | flops 100000 | bytes 100000 | tf_op jit(solution)/shard_map/pallas_call | solution.py:286
  3.1 0.0 copy-start.3
  3.1 10.6 %all-to-all-start = ((f32[32,32,256]{2,1,0:T(8,128)}), f32[32,32,256]{2,1,0:T(8,128)S(1)}, u32[]{:S(2)}, u32[]{:S(2)}) async-start(f32[32,32,256]{2,1,0:T(8,128)} %shard_map.67), calls=%async_computation | async-start | bytes 2097152 | tf_op jit(solution)/shard_map/all_to_all | solution.py:255
  13.8 0.0 copy-done.3
  13.8 2.3 %collective-permute-start = (f32[64,256]{1,0:T(8,128)S(1)}, f32[64,256]{1,0:T(8,128)S(1)}, u32[]{:S(2)}, u32[]{:S(2)}) collective-permute-start(f32[64,256]{1,0:T(8,128)S(1)} %shard_map.68), channel_id=1, source_target_pairs={{16,0},{25,1},{18,2},{27,3},{20,4},{29,5},{22,6},{31,7},{24,8},{17... | collective-permute-start | bytes 196616 | tf_op jit(solution)/shard_map/ppermute | solution.py:268
  16.1 13.5 %collective-permute-done.q_part = f32[64,256]{1,0:T(8,128)S(1)} collective-permute-done((f32[64,256]{1,0:T(8,128)S(1)}, f32[64,256]{1,0:T(8,128)S(1)}, u32[]{:S(2)}, u32[]{:S(2)}) %collective-permute-start) | collective-permute-done | bytes 65568 | tf_op jit(solution)/shard_map/ppermute | solution.py:268
  29.5 1.5 %all-to-all-done.merged = f32[32,32,256]{2,1,0:T(8,128)S(1)} async-done(((f32[32,32,256]{2,1,0:T(8,128)}), f32[32,32,256]{2,1,0:T(8,128)S(1)}, u32[]{:S(2)}, u32[]{:S(2)}) %all-to-all-start) | async-done | bytes 1048608 | tf_op jit(solution)/shard_map/all_to_all | solution.py:255
  31.0 0.3 shard_map.69
  31.4 17.0 %all_to_all.15.parts = f32[32,5,4,128]{3,2,1,0:T(4,128)S(1)} all-to-all(f32[32,5,4,128]{3,2,1,0:T(4,128)S(1)} %shard_map.69), channel_id=1, replica_groups=mesh['dp'=32,'tensor'=16] {'dp'}, dimensions={0} | all-to-all | bytes 655360 | tf_op jit(solution)/shard_map/all_to_all | solution.py:255
  48.3 0.3 shard_map.70
  48.6 0.0 copy-start.2
  48.6 30.1 %all-gather = f32[1280,128]{1,0:T(8,128)S(1)} all-gather(f32[80,128]{1,0:T(8,128)S(1)} %shard_map.70), channel_id=2, replica_groups={{0,17,2,19,4,21,6,23,8,25,10,27,12,29,14,31},{16,1,18,3,20,5,22,7,24,9,..., dimensions={0}, use_global_device_ids=true | all-gather | bytes 696320 | tf_op jit(solution)/shard_map/all_gather | solution.py:275
  78.7 0.0 copy-start
  78.7 2.9 %shard_map.71 = f32[16,72,128]{2,1,0:T(8,128)S(1)} custom-call(s32[1]{0:T(128)} %bitcast.2.chip_ref, s32[1]{0:T(128)} %bitcast.1.t_ref, f32[16,80,128]{2,1,0:T(8,128)S(1)} %bitcast.4), custom_call_target="tpu_custom_call" | custom-call | flops 100000 | bytes 100000 | tf_op jit(solution)/shard_map/pallas_call | solution.py:294
  81.7 0.0 copy-start.1
  81.7 14.7 %all_to_all.16.parts = f32[16,72,128]{2,1,0:T(8,128)S(1)} all-to-all(f32[16,72,128]{2,1,0:T(8,128)S(1)} %shard_map.71), channel_id=1, replica_groups={{0,32,64,96,128,160,192,224,256,288,320,352,384,416,448,480},{16,48,80,..., dimensions={0} | all-to-all | bytes 1179648 | tf_op jit(solution)/shard_map/all_to_all | solution.py:255
  96.3 3.7 %collective-permute-start.1 = (f32[16,72,128]{2,1,0:T(8,128)S(1)}, f32[16,72,128]{2,1,0:T(8,128)S(1)}, u32[]{:S(2)}, u32[]{:S(2)}) collective-permute-start(f32[16,72,128]{2,1,0:T(8,128)S(1)} %all_to_all.16.parts), channel_id=1, source_target_pairs={{0,16},{16,0},{32,48},{48,32},{64,80},{80,64},{96,112},{112,96},{1... | collective-permute-start | bytes 1769480 | tf_op jit(solution)/shard_map/ppermute | solution.py:259
  100.1 0.0 copy-done.2
  100.1 0.0 copy-done
  100.1 0.0 copy-done.1
  100.1 1.6 %shard_map.72 = (f32[1,32,8192]{2,1,0:T(8,128)}, f32[32,8192]{1,0:T(8,128)}, f32[64,512]{1,0:T(8,128)}) custom-call(s32[1]{0:T(128)S(6)} %xor.6.half_ref, bf16[1,32,8192]{2,1,0:T(8,128)(2,1)S(1)} %copy-done.1, f32[1,32,8192]{2,1,0:T(8,128)S(1)} %copy-done, f32[32,8192]{1,0:T(8,128)S(1)} %copy-done.2, f32[16,72,128]{2,1,0:T(8,128)S(1)} %all_to_all.16.parts), custom_call_target="tpu_custom_call" | custom-call | flops 100000 | bytes 100000 | tf_op jit(solution)/shard_map/pallas_call | solution.py:304
  101.7 0.0 collective-permute-done.1.parts
  101.7 1.6 %shard_map.73 = (f32[1,32,8192]{2,1,0:T(8,128)}, f32[32,8192]{1,0:T(8,128)}, f32[64,512]{1,0:T(8,128)}) custom-call(s32[1]{0:T(128)S(6)} %sub.6.half_ref, bf16[1,32,8192]{2,1,0:T(8,128)(2,1)S(1)} %copy-done.1, f32[1,32,8192]{2,1,0:T(8,128)S(1)} %copy-done, f32[32,8192]{1,0:T(8,128)S(1)} %copy-done.2, ...), custom_call_target="tpu_custom_call", output_to_operand_aliasing={{0}: (5, {}), {1}: (6, {}), {2}: (7, {})} | custom-call | flops 100000 | bytes 100000 | tf_op jit(solution)/shard_map/pallas_call | solution.py:307
  (1 shorter events, 0.0 us)
Async XLA Ops:
  3.1 10.6 %copy-start.3 = (f32[64,512]{1,0:T(8,128)S(1)}, f32[64,512]{1,0:T(8,128)}, u32[]{:S(2)}) copy-start(f32[64,512]{1,0:T(8,128)} %q_ref.1) | copy-start | bytes 393220
  3.1 27.9 %all-to-all-start = ((f32[32,32,256]{2,1,0:T(8,128)}), f32[32,32,256]{2,1,0:T(8,128)S(1)}, u32[]{:S(2)}, u32[]{:S(2)}) async-start(f32[32,32,256]{2,1,0:T(8,128)} %shard_map.67), calls=%async_computation | async-start | bytes 2097152 | tf_op jit(solution)/shard_map/all_to_all | solution.py:255
  13.8 15.7 %collective-permute-start = (f32[64,256]{1,0:T(8,128)S(1)}, f32[64,256]{1,0:T(8,128)S(1)}, u32[]{:S(2)}, u32[]{:S(2)}) collective-permute-start(f32[64,256]{1,0:T(8,128)S(1)} %shard_map.68), channel_id=1, source_target_pairs={{16,0},{25,1},{18,2},{27,3},{20,4},{29,5},{22,6},{31,7},{24,8},{17... | collective-permute-start | bytes 196616 | tf_op jit(solution)/shard_map/ppermute | solution.py:268
  48.6 51.5 %copy-start.2 = (f32[32,8192]{1,0:T(8,128)S(1)}, f32[32,8192]{1,0:T(8,128)}, u32[]{:S(2)}) copy-start(f32[32,8192]{1,0:T(8,128)} %momentum.3) | copy-start | bytes 3145732
  78.7 21.4 %copy-start = (f32[1,32,8192]{2,1,0:T(8,128)S(1)}, f32[1,32,8192]{2,1,0:T(8,128)}, u32[]{:S(2)}) copy-start(f32[1,32,8192]{2,1,0:T(8,128)} %feedback.5) | copy-start | bytes 3145732
  81.7 18.4 %copy-start.1 = (bf16[1,32,8192]{2,1,0:T(8,128)(2,1)S(1)}, bf16[1,32,8192]{2,1,0:T(8,128)(2,1)}, u32[]{:S(2)}) copy-start(bf16[1,32,8192]{2,1,0:T(8,128)(2,1)} %gradient.5) | copy-start | bytes 1572868
  96.3 5.4 %collective-permute-start.1 = (f32[16,72,128]{2,1,0:T(8,128)S(1)}, f32[16,72,128]{2,1,0:T(8,128)S(1)}, u32[]{:S(2)}, u32[]{:S(2)}) collective-permute-start(f32[16,72,128]{2,1,0:T(8,128)S(1)} %all_to_all.16.parts), channel_id=1, source_target_pairs={{0,16},{16,0},{32,48},{48,32},{64,80},{80,64},{96,112},{112,96},{1... | collective-permute-start | bytes 1769480 | tf_op jit(solution)/shard_map/ppermute | solution.py:259

commit v16 on v15

--- a/solution.py
+++ b/solution.py
@@ -212,18 +212,18 @@
                 merged = gradient[0, :, lanes].astype(jnp.float32) + feedback[0, :, lanes]
                 feedback_part[shard, :, place] = merged - part
                 momentum_part[shard, :, place] = BETA * momentum[:, lanes] + part
-        for shard in range(th * GROUP, (th + 1) * GROUP):
-            lanes = columns(shard, half)
-            copies += [
-                pltpu.make_async_copy(
-                    feedback_part.at[shard], new_feedback.at[0, :, lanes], sems.at[0, shard]
-                ),
-                pltpu.make_async_copy(
-                    momentum_part.at[shard], new_momentum.at[:, lanes], sems.at[1, shard]
-                ),
-            ]
-            copies[-2].start()
-            copies[-1].start()
+                if group == CHIPS // GROUP - 1:
+                    lanes = columns(shard, half)
+                    copies += [
+                        pltpu.make_async_copy(
+                            feedback_part.at[shard], new_feedback.at[0, :, lanes], sems.at[0, shard]
+                        ),
+                        pltpu.make_async_copy(
+                            momentum_part.at[shard], new_momentum.at[:, lanes], sems.at[1, shard]
+                        ),
+                    ]
+                    copies[-2].start()
+                    copies[-1].start()
     for copy in copies:
         copy.wait()
 

time: 104 us -> 104 us (level)
  no operation moved by 1% of the time
where the time goes in v16:
time: 104 us; the launch traced here: 103 us
  blocking collectives  61.7 us (59%)
  starting transfers between devices  16.6 us (16%)
  waiting for transfers between devices  15 us (14%)
  Pallas kernels  9.1 us (9%)
    all_to_all x2, blocking collectives, exchange(): lax.all_to_all(parts, axis, 0, 0, tiled=True, axis_index_groups=groups)  31.6 us
    all_gather x1, blocking collectives, gather_lines(): return lax.all_gather(parts, ('dp', 'tensor'), axis_index_groups=lines)  30.1 us
    ppermute x1, waiting for transfers between devices, fetch_shards(): return lax.ppermute(parts, ('dp', 'tensor'), pairs)  13.5 us
    all_to_all x1, starting transfers between devices, exchange(): lax.all_to_all(parts, axis, 0, 0, tiled=True, axis_index_groups=groups)  10.6 us
    ppermute x1, starting transfers between devices, swap_cores(): return lax.ppermute(parts, 'dp', [(d, d ^ 1) for d in range(DP)])  3.72 us
    pallas_call x1, Pallas kernels, on_device(): local(solve_kernel, (CHIPS, 2 * ROWS + 8, LANES), scalars=2)(chip, t, parts)  2.93 us
    pallas_call x1, Pallas kernels, on_device(): local(merge_kernel, (DP, ROWS, SPAN), scalars=1, inputs=2, room=60)  2.51 us
    ppermute x1, starting transfers between devices, fetch_shards(): return lax.ppermute(parts, ('dp', 'tensor'), pairs)  2.26 us
  transfers between devices with their start and end apart: 3, of which 2 were waited for; matrix products, arithmetic and copies ran while one was open for 0% of the time, Pallas kernels for 2%

profile of v16, /device:TPU:1, one launch (start us, length us, event | category | flops | bytes accessed | tf_op | source)
XLA Modules:
  0.0 103.2 jit_solution(110955576780954740)
XLA Ops:
  0.6 2.5 %shard_map.67 = f32[32,32,256]{2,1,0:T(8,128)} custom-call(s32[1]{0:T(128)} %bitcast.1.t_ref, bf16[1,32,8192]{2,1,0:T(8,128)(2,1)} %gradient.5, f32[1,32,8192]{2,1,0:T(8,128)} %feedback.5), custom_call_target="tpu_custom_call" | custom-call | flops 100000 | bytes 100000 | tf_op jit(solution)/shard_map/pallas_call | solution.py:286
  3.1 0.0 copy-start.3
  3.1 10.6 %all-to-all-start = ((f32[32,32,256]{2,1,0:T(8,128)}), f32[32,32,256]{2,1,0:T(8,128)S(1)}, u32[]{:S(2)}, u32[]{:S(2)}) async-start(f32[32,32,256]{2,1,0:T(8,128)} %shard_map.67), calls=%async_computation | async-start | bytes 2097152 | tf_op jit(solution)/shard_map/all_to_all | solution.py:255
  13.8 0.0 copy-done.3
  13.8 2.3 %collective-permute-start = (f32[64,256]{1,0:T(8,128)S(1)}, f32[64,256]{1,0:T(8,128)S(1)}, u32[]{:S(2)}, u32[]{:S(2)}) collective-permute-start(f32[64,256]{1,0:T(8,128)S(1)} %shard_map.68), channel_id=1, source_target_pairs={{16,0},{25,1},{18,2},{27,3},{20,4},{29,5},{22,6},{31,7},{24,8},{17... | collective-permute-start | bytes 196616 | tf_op jit(solution)/shard_map/ppermute | solution.py:268
  16.1 13.5 %collective-permute-done.q_part = f32[64,256]{1,0:T(8,128)S(1)} collective-permute-done((f32[64,256]{1,0:T(8,128)S(1)}, f32[64,256]{1,0:T(8,128)S(1)}, u32[]{:S(2)}, u32[]{:S(2)}) %collective-permute-start) | collective-permute-done | bytes 65568 | tf_op jit(solution)/shard_map/ppermute | solution.py:268
  29.5 1.5 %all-to-all-done.merged = f32[32,32,256]{2,1,0:T(8,128)S(1)} async-done(((f32[32,32,256]{2,1,0:T(8,128)}), f32[32,32,256]{2,1,0:T(8,128)S(1)}, u32[]{:S(2)}, u32[]{:S(2)}) %all-to-all-start) | async-done | bytes 1048608 | tf_op jit(solution)/shard_map/all_to_all | solution.py:255
  31.0 0.3 shard_map.69
  31.4 17.0 %all_to_all.15.parts = f32[32,5,4,128]{3,2,1,0:T(4,128)S(1)} all-to-all(f32[32,5,4,128]{3,2,1,0:T(4,128)S(1)} %shard_map.69), channel_id=1, replica_groups=mesh['dp'=32,'tensor'=16] {'dp'}, dimensions={0} | all-to-all | bytes 655360 | tf_op jit(solution)/shard_map/all_to_all | solution.py:255
  48.3 0.3 shard_map.70
  48.6 0.0 copy-start.2
  48.6 30.1 %all-gather = f32[1280,128]{1,0:T(8,128)S(1)} all-gather(f32[80,128]{1,0:T(8,128)S(1)} %shard_map.70), channel_id=2, replica_groups={{0,17,2,19,4,21,6,23,8,25,10,27,12,29,14,31},{16,1,18,3,20,5,22,7,24,9,..., dimensions={0}, use_global_device_ids=true | all-gather | bytes 696320 | tf_op jit(solution)/shard_map/all_gather | solution.py:275
  78.7 0.0 copy-start
  78.7 2.9 %shard_map.71 = f32[16,72,128]{2,1,0:T(8,128)S(1)} custom-call(s32[1]{0:T(128)} %bitcast.2.chip_ref, s32[1]{0:T(128)} %bitcast.1.t_ref, f32[16,80,128]{2,1,0:T(8,128)S(1)} %bitcast.4), custom_call_target="tpu_custom_call" | custom-call | flops 100000 | bytes 100000 | tf_op jit(solution)/shard_map/pallas_call | solution.py:294
  81.7 0.0 copy-start.1
  81.7 14.7 %all_to_all.16.parts = f32[16,72,128]{2,1,0:T(8,128)S(1)} all-to-all(f32[16,72,128]{2,1,0:T(8,128)S(1)} %shard_map.71), channel_id=1, replica_groups={{0,32,64,96,128,160,192,224,256,288,320,352,384,416,448,480},{16,48,80,..., dimensions={0} | all-to-all | bytes 1179648 | tf_op jit(solution)/shard_map/all_to_all | solution.py:255
  96.3 3.7 %collective-permute-start.1 = (f32[16,72,128]{2,1,0:T(8,128)S(1)}, f32[16,72,128]{2,1,0:T(8,128)S(1)}, u32[]{:S(2)}, u32[]{:S(2)}) collective-permute-start(f32[16,72,128]{2,1,0:T(8,128)S(1)} %all_to_all.16.parts), channel_id=1, source_target_pairs={{0,16},{16,0},{32,48},{48,32},{64,80},{80,64},{96,112},{112,96},{1... | collective-permute-start | bytes 1769480 | tf_op jit(solution)/shard_map/ppermute | solution.py:259
  100.1 0.0 copy-done.2
  100.1 0.0 copy-done
  100.1 0.0 copy-done.1
  100.1 1.5 %shard_map.72 = (f32[1,32,8192]{2,1,0:T(8,128)}, f32[32,8192]{1,0:T(8,128)}, f32[64,512]{1,0:T(8,128)}) custom-call(s32[1]{0:T(128)S(6)} %xor.6.half_ref, bf16[1,32,8192]{2,1,0:T(8,128)(2,1)S(1)} %copy-done.1, f32[1,32,8192]{2,1,0:T(8,128)S(1)} %copy-done, f32[32,8192]{1,0:T(8,128)S(1)} %copy-done.2, f32[16,72,128]{2,1,0:T(8,128)S(1)} %all_to_all.16.parts), custom_call_target="tpu_custom_call" | custom-call | flops 100000 | bytes 100000 | tf_op jit(solution)/shard_map/pallas_call | solution.py:304
  101.6 0.0 collective-permute-done.1.parts
  101.7 1.5 %shard_map.73 = (f32[1,32,8192]{2,1,0:T(8,128)}, f32[32,8192]{1,0:T(8,128)}, f32[64,512]{1,0:T(8,128)}) custom-call(s32[1]{0:T(128)S(6)} %sub.6.half_ref, bf16[1,32,8192]{2,1,0:T(8,128)(2,1)S(1)} %copy-done.1, f32[1,32,8192]{2,1,0:T(8,128)S(1)} %copy-done, f32[32,8192]{1,0:T(8,128)S(1)} %copy-done.2, ...), custom_call_target="tpu_custom_call", output_to_operand_aliasing={{0}: (5, {}), {1}: (6, {}), {2}: (7, {})} | custom-call | flops 100000 | bytes 100000 | tf_op jit(solution)/shard_map/pallas_call | solution.py:307
  (1 shorter events, 0.0 us)
Async XLA Ops:
  3.1 10.6 %copy-start.3 = (f32[64,512]{1,0:T(8,128)S(1)}, f32[64,512]{1,0:T(8,128)}, u32[]{:S(2)}) copy-start(f32[64,512]{1,0:T(8,128)} %q_ref.1) | copy-start | bytes 393220
  3.1 27.9 %all-to-all-start = ((f32[32,32,256]{2,1,0:T(8,128)}), f32[32,32,256]{2,1,0:T(8,128)S(1)}, u32[]{:S(2)}, u32[]{:S(2)}) async-start(f32[32,32,256]{2,1,0:T(8,128)} %shard_map.67), calls=%async_computation | async-start | bytes 2097152 | tf_op jit(solution)/shard_map/all_to_all | solution.py:255
  13.8 15.7 %collective-permute-start = (f32[64,256]{1,0:T(8,128)S(1)}, f32[64,256]{1,0:T(8,128)S(1)}, u32[]{:S(2)}, u32[]{:S(2)}) collective-permute-start(f32[64,256]{1,0:T(8,128)S(1)} %shard_map.68), channel_id=1, source_target_pairs={{16,0},{25,1},{18,2},{27,3},{20,4},{29,5},{22,6},{31,7},{24,8},{17... | collective-permute-start | bytes 196616 | tf_op jit(solution)/shard_map/ppermute | solution.py:268
  48.6 51.5 %copy-start.2 = (f32[32,8192]{1,0:T(8,128)S(1)}, f32[32,8192]{1,0:T(8,128)}, u32[]{:S(2)}) copy-start(f32[32,8192]{1,0:T(8,128)} %momentum.3) | copy-start | bytes 3145732
  78.7 21.4 %copy-start = (f32[1,32,8192]{2,1,0:T(8,128)S(1)}, f32[1,32,8192]{2,1,0:T(8,128)}, u32[]{:S(2)}) copy-start(f32[1,32,8192]{2,1,0:T(8,128)} %feedback.5) | copy-start | bytes 3145732
  81.7 18.4 %copy-start.1 = (bf16[1,32,8192]{2,1,0:T(8,128)(2,1)S(1)}, bf16[1,32,8192]{2,1,0:T(8,128)(2,1)}, u32[]{:S(2)}) copy-start(bf16[1,32,8192]{2,1,0:T(8,128)(2,1)} %gradient.5) | copy-start | bytes 1572868
  96.3 5.3 %collective-permute-start.1 = (f32[16,72,128]{2,1,0:T(8,128)S(1)}, f32[16,72,128]{2,1,0:T(8,128)S(1)}, u32[]{:S(2)}, u32[]{:S(2)}) collective-permute-start(f32[16,72,128]{2,1,0:T(8,128)S(1)} %all_to_all.16.parts), channel_id=1, source_target_pairs={{0,16},{16,0},{32,48},{48,32},{64,80},{80,64},{96,112},{112,96},{1... | collective-permute-start | bytes 1769480 | tf_op jit(solution)/shard_map/ppermute | solution.py:259
